TPU v7x, 256 devices: a whole 4x4x8 slice. The times are simulated.
256 devices in a mesh: section: 2 (over core), slab: 32 (over z_hi, y, x), dp: 4 (over z_lo).
Axes of the slice: x: 4, y: 4, z: 8 (z_hi: 2, z_lo: 4; z = z_hi * 4 + z_lo), core: 2. Of those that a mesh axis runs over, the one named last changes fastest.
Arguments:
- fields: bfloat16 [2, 64, 16, 2, 64, 256], P('section', 'slab', 'dp'), may hold values from -6 to 6
- kernels: bfloat16 [2, 2, 3, 3, 256, 256], P('section'), may hold values from -0.09375 to 0.09375
- codebook: bfloat16 [32768, 256], P('slab'), may hold values from -6 to 6
- codes: int32 [64, 16, 2, 64], P(None, 'dp'), may hold values from 0 to 32767
Outputs:
- weight_grads: float32 [2, 2, 3, 3, 256, 256], P('section')
All inputs are finite; a program needn't handle non-finite values.
Results may differ from a plain program's by a relative error of at most 0.0014.
Values may be sent and summed in bfloat16 or wider, within the bound.
No kernel may reach another device: no remote copies, remote signals or barrier semaphores. Data moves between devices by JAX's collectives and lax.ppermute only.
A program may use at most 128 MiB of HBM per device.

v0:
```python
import math

import jax
import jax.numpy as jnp
from jax import lax
from jax.sharding import PartitionSpec as P

COMMIT = 0.5


def extended(cells, sides, width):
    for axis, dim in sides:
        count = lax.axis_size(axis)
        ends = count - 1
        head = lax.slice_in_dim(cells, 0, width, axis=dim)
        tail = lax.slice_in_dim(cells, cells.shape[dim] - width, cells.shape[dim], axis=dim)
        cells = jnp.concatenate(
            [
                lax.ppermute(tail, axis, [(i, (i + 1) % count) for i in range(ends)]),
                cells,
                lax.ppermute(head, axis, [((i + 1) % count, i) for i in range(ends)]),
            ],
            axis=dim,
        )
    return cells


def silu_slope(pre_act):
    sig = jax.nn.sigmoid(pre_act)
    return sig * (1.0 + pre_act * (1.0 - sig))


def columns(padded, offset_sign, row_count, frame_count, across):
    pieces = []
    for tap_t in range(2):
        for tap_r in range(3):
            for tap_q in range(3):
                shift_t = 1 + offset_sign * (tap_t - 1)
                shift_r = 1 + offset_sign * (tap_r - 1)
                shift_q = 1 + offset_sign * (tap_q - 1)
                pieces.append(
                    padded[
                        shift_r : shift_r + row_count,
                        :,
                        shift_t : shift_t + frame_count,
                        shift_q : shift_q + across,
                        :,
                    ]
                )
    return jnp.concatenate(pieces, axis=-1)


def pick_rows(book_piece, wanted):
    book_count = book_piece.shape[0]
    inside = (wanted >= 0) & (wanted < book_count)
    taken = jnp.take(book_piece, jnp.clip(wanted, 0, book_count - 1), axis=0)
    return jnp.where(inside[..., None], taken.astype(jnp.float32), 0.0)


def on_device(fields, kernels, codebook, codes):
    section_id = lax.axis_index("section")
    own_field = fields[0]
    kernel = kernels[0]
    row_count, batch_count, frame_count, across, channels = own_field.shape
    own_codes = lax.dynamic_slice_in_dim(
        codes, lax.axis_index("slab") * row_count, row_count, 0
    ).reshape(-1)
    looked = pick_rows(lax.all_gather(codebook, "slab", axis=0, tiled=True), own_codes)
    looked_up = looked.astype(jnp.bfloat16).reshape(own_field.shape)
    turned = jnp.transpose(looked_up, (3, 1, 2, 0, 4))
    relayed = lax.all_to_all(turned, "slab", split_axis=0, concat_axis=3, tiled=True)
    quantized = jnp.where(section_id == 1, relayed, looked_up)
    source = jnp.where(section_id == 0, own_field, quantized)
    rimmed = extended(source, (("slab", 0),), 1)
    padded = jnp.pad(rimmed, ((0, 0), (0, 0), (1, 1), (1, 1), (0, 0)))
    tap_cols = columns(padded, 1, row_count, frame_count, across).reshape(-1, 18 * channels)
    pre_act = jnp.dot(tap_cols, kernel.reshape(-1, channels), preferred_element_type=jnp.float32)
    field_rows = own_field.reshape(-1, channels)
    dec_grad = jnp.where(
        section_id == 1,
        (field_rows.astype(jnp.float32) * silu_slope(pre_act)).astype(jnp.bfloat16),
        jnp.zeros_like(field_rows),
    )
    grad_rim = extended(dec_grad.reshape(own_field.shape), (("slab", 0),), 1)

    def adjoint_part(rimmed_grad):
        grad_pad = jnp.pad(rimmed_grad, ((0, 0), (0, 0), (1, 1), (1, 1), (0, 0)))
        grad_cols = columns(grad_pad, -1, row_count, frame_count, across).reshape(-1, 18 * channels)
        kernel_t = jnp.swapaxes(kernel, -1, -2).reshape(-1, channels)
        back_rows = jnp.dot(grad_cols, kernel_t, preferred_element_type=jnp.float32)
        return back_rows.astype(jnp.bfloat16).reshape(own_field.shape)

    def skipped(rimmed_grad):
        return jnp.zeros(own_field.shape, jnp.bfloat16)

    back_dec = lax.cond(section_id == 1, adjoint_part, skipped, grad_rim)
    flipped = jnp.transpose(back_dec, (3, 1, 2, 0, 4))
    returned = lax.all_to_all(
        lax.all_to_all(
            jnp.stack([flipped, flipped]), "section", split_axis=0, concat_axis=0, tiled=True
        ),
        "slab",
        split_axis=1,
        concat_axis=4,
        tiled=True,
    )[1]
    enc_grad = (
        returned.reshape(-1, channels).astype(jnp.float32)
        + COMMIT * (pre_act - quantized.reshape(-1, channels).astype(jnp.float32))
    ).astype(jnp.bfloat16)
    weight_side = jnp.where(section_id == 0, enc_grad, dec_grad)
    partial_grad = lax.dot_general(
        tap_cols, weight_side, (((0,), (0,)), ((), ())), preferred_element_type=jnp.float32
    )
    summed = lax.psum(partial_grad, ("slab", "dp"))
    positions = (
        row_count * lax.axis_size("slab") * across * batch_count * lax.axis_size("dp") * frame_count
    )
    return (summed / math.sqrt(positions)).reshape(1, 2, 3, 3, channels, channels)


def solution(mesh):
    placed = (
        P("section", "slab", "dp", None, None, None),
        P("section", None, None, None, None, None),
        P("slab", None),
        P(None, "dp", None, None),
    )
    return jax.shard_map(
        on_device,
        mesh=mesh,
        in_specs=placed,
        out_specs=P("section", None, None, None, None, None),
        check_vma=False,
    )
```

profile of v0, /device:TPU:2, one launch (start us, length us, event | category | flops | bytes accessed | tf_op | source)
XLA Modules:
  0.0 651.6 jit_solution(760856895260644482)
XLA Ops:
  6.5 0.7 all-gather.2.cloned.1.call-update
  7.3 0.7 compare_and_fusion
  8.1 251.7 %all-gather.2.cloned.1.call-done = bf16[32768,256]{1,0:T(8,128)(2,1)} async-done(((bf16[1024,256]{1,0:T(8,128)(2,1)}), bf16[32768,256]{1,0:T(8,128)(2,1)}) %all-gather.2.cloned.1.call-update) | async-done | bytes 16777232 | tf_op jit(solution)/shard_map/all_gather | solution.py:68
  259.8 11.4 %gather_fusion = bf16[1024,256]{1,0:T(8,128)(2,1)S(1)} fusion(bf16[32768,256]{1,0:T(8,128)(2,1)} %all-gather.2.cloned.1.call-done, s32[1024]{0:T(1024)S(1)} %broadcast_clamp_fusion), kind=kCustom, calls=%fused_computation | custom fusion | bytes 1052672 | tf_op jit(solution)/shard_map/jit(_take)/gather | solution.py:56
  271.2 0.3 fusion.35
  271.5 1.3 copy.24
  272.9 5.9 all-to-all-start
  278.8 14.9 %all-to-all-done = bf16[64,4,2,2,256]{4,2,1,3,0:T(2,128)(2,1)S(1)} async-done(((bf16[64,4,2,2,256]{4,2,1,3,0:T(2,128)(2,1)}), bf16[64,4,2,2,256]{4,2,1,3,0:T(2,128)(2,1)S(1)}, u32[]{:S(2)}, u32[]{:S(2)}) %all-to-all-start) | async-done | bytes 524320 | tf_op jit(solution)/shard_map/all_to_all | solution.py:71
  293.7 0.5 copy.35
  294.2 0.2 all_to_all.32
  294.4 0.5 bitcast_select_fusion
  294.9 3.0 collective-permute-start
  297.9 2.9 collective-permute-start.1
  300.8 2.4 collective-permute-done
  303.2 3.0 collective-permute-done.1
  306.2 0.6 select_maximum_fusion
  306.9 0.2 slice_dynamic-update-slice_fusion.16
  307.1 0.2 slice_dynamic-update-slice_fusion.15
  307.3 0.2 slice_dynamic-update-slice_fusion.13
  307.5 0.2 slice_dynamic-update-slice_fusion.12
  307.7 0.2 slice_dynamic-update-slice_fusion.10
  307.9 0.2 slice_dynamic-update-slice_fusion.9
  308.2 0.2 slice_dynamic-update-slice_fusion.7
  308.5 0.2 slice_dynamic-update-slice_fusion.5
  308.8 0.2 slice_dynamic-update-slice_fusion.3
  309.0 4.0 broadcast_select_fusion
  313.0 0.8 copy-done.1
  313.8 0.8 fusion.40
  314.6 3.1 collective-permute-start.2
  317.7 3.5 collective-permute-start.3
  321.2 2.0 collective-permute-done.2
  323.2 5.1 collective-permute-done.3
  328.3 1.3 pad_maximum_fusion
  329.6 0.2 conditional.1
  329.8 0.5 copy.34
  330.4 1.0 pad_maximum_fusion.1
  331.3 13.0 %all_to_all.41 = bf16[2,64,4,2,2,256]{5,3,2,4,1,0:T(2,128)(2,1)S(1)} all-to-all(bf16[2,64,4,2,2,256]{5,3,2,4,1,0:T(2,128)(2,1)S(1)} %pad_maximum_fusion.1), channel_id=1, replica_groups=mesh['section'=2,'slab'=32,'dp'=4] {'section'}, dimensions={0} | all-to-all | bytes 2097152 | tf_op jit(solution)/shard_map/all_to_all | solution.py:99
  344.3 2.2 copy.28
  346.5 20.5 %all-to-all-start.2 = ((bf16[2,64,4,2,2,256]{5,3,2,4,0,1:T(2,128)(2,1)}), bf16[2,64,4,2,2,256]{5,3,2,4,0,1:T(2,128)(2,1)S(1)}, u32[]{:S(2)}, u32[]{:S(2)}) async-start(bf16[2,64,4,2,2,256]{5,3,2,4,0,1:T(2,128)(2,1)} %copy.28), calls=%async_computation.2 | async-start | bytes 2097152 | tf_op jit(solution)/shard_map/all_to_all | solution.py:98
  367.1 0.3 all-reduce.4.cloned.1.call-start
  367.5 1.0 all_to_all.37
  368.5 18.5 %all-to-all-done.2 = bf16[2,64,4,2,2,256]{5,3,2,4,0,1:T(2,128)(2,1)S(1)} async-done(((bf16[2,64,4,2,2,256]{5,3,2,4,0,1:T(2,128)(2,1)}), bf16[2,64,4,2,2,256]{5,3,2,4,0,1:T(2,128)(2,1)S(1)}, u32[]{:S(2)}, u32[]{:S(2)}) %all-to-all-start.2) | async-done | bytes 1048608 | tf_op jit(solution)/shard_map/all_to_all | solution.py:98
  387.0 1.1 copy.33
  388.2 0.4 slice_convert_fusion
  388.6 0.7 reshape.96
  389.4 9.2 %fusion.24 = f32[4608,256]{1,0:T(8,128)} fusion(bf16[1024,4608]{1,0:T(8,128)(2,1)} %bitcast.56, bf16[1024,256]{1,0:T(8,128)(2,1)S(1)} %copy-done.2, f32[1024,256]{1,0:T(8,128)S(1)} %reshape.96, f32[1024,256]{1,0:T(8,128)} %get-tuple-element.31, bf16[1024,256]{1,0:T(8,128)(2,1)} %all_to_all.37, bf16[1024,256]{1,0:T(8,128)(2,1)S(1)} %gather_fusion, ...), kind=kOutput, calls=%fused_computation.58 | convolution fusion | flops 2418802688 | bytes 17827842 | tf_op jit(solution)/shard_map/dot_general | solution.py:112
  398.6 241.3 %all-reduce.4.cloned.1.call-done = f32[4608,256]{1,0:T(8,128)} async-done(((f32[4608,256]{1,0:T(8,128)}), f32[4608,256]{1,0:T(8,128)}) %all-reduce.4.cloned.1.call-update) | async-done | bytes 4718608 | tf_op jit(solution)/shard_map/psum | solution.py:115
  639.9 4.9 broadcast_multiply_fusion
  (30 shorter events, 0.8 us)
Async XLA Ops:
  6.5 287.9 %copy-start.3 = (bf16[1,2,4,2,64,256]{5,4,3,2,1,0:T(8,128)(2,1)S(1)}, bf16[1,2,4,2,64,256]{5,4,3,2,1,0:T(8,128)(2,1)}, u32[]{:S(2)}) copy-start(bf16[1,2,4,2,64,256]{5,4,3,2,1,0:T(8,128)(2,1)} %param.6) | copy-start | bytes 1572868
  6.5 253.2 %all-gather.2.cloned.1.call-start = ((), (), s32[]{:S(2)}) async-start(), calls=%async_computation.3 | async-start | bytes 17301504 | tf_op jit(solution)/shard_map/all_gather | solution.py:68
  272.9 20.8 %all-to-all-start = ((bf16[64,4,2,2,256]{4,2,1,3,0:T(2,128)(2,1)}), bf16[64,4,2,2,256]{4,2,1,3,0:T(2,128)(2,1)S(1)}, u32[]{:S(2)}, u32[]{:S(2)}) async-start(bf16[64,4,2,2,256]{4,2,1,3,0:T(2,128)(2,1)} %copy.24), calls=%async_computation | async-start | bytes 1048576 | tf_op jit(solution)/shard_map/all_to_all | solution.py:71
  294.9 8.3 %collective-permute-start = (bf16[1,4,2,64,256]{4,3,2,1,0:T(8,128)(2,1)S(1)}, bf16[1,4,2,64,256]{4,3,2,1,0:T(8,128)(2,1)S(1)}, u32[]{:S(2)}, u32[]{:S(2)}) collective-permute-start(bf16[1,4,2,64,256]{4,3,2,1,0:T(8,128)(2,1)S(1)} %get-tuple-element.27), channel_id=1, source_target_pairs={{0,4},{4,8},{8,12},{12,16},{16,20},{20,24},{24,28},{28,32},{32,36}... | collective-permute-start | bytes 786440 | tf_op jit(solution)/shard_map/ppermute | solution.py:19
  297.9 8.3 %collective-permute-start.1 = (bf16[1,4,2,64,256]{4,3,2,1,0:T(8,128)(2,1)S(1)}, bf16[1,4,2,64,256]{4,3,2,1,0:T(8,128)(2,1)S(1)}, u32[]{:S(2)}, u32[]{:S(2)}) collective-permute-start(bf16[1,4,2,64,256]{4,3,2,1,0:T(8,128)(2,1)S(1)} %get-tuple-element.28), channel_id=1, source_target_pairs={{4,0},{8,4},{12,8},{16,12},{20,16},{24,20},{28,24},{32,28},{36,32}... | collective-permute-start | bytes 786440 | tf_op jit(solution)/shard_map/ppermute | solution.py:21
  306.8 2.2 copy-start
  306.9 2.2 copy-start.4
  309.0 4.0 copy-start.6
  313.0 0.8 copy-start.1
  314.6 8.6 %collective-permute-start.2 = (bf16[1,4,2,64,256]{4,3,2,1,0:T(8,128)(2,1)}, bf16[1,4,2,64,256]{4,3,2,1,0:T(8,128)(2,1)}, u32[]{:S(2)}, u32[]{:S(2)}) collective-permute-start(bf16[1,4,2,64,256]{4,3,2,1,0:T(8,128)(2,1)} %bitcast.14), channel_id=1, source_target_pairs={{0,4},{4,8},{8,12},{12,16},{16,20},{20,24},{24,28},{28,32},{32,36}... | collective-permute-start | bytes 786440 | tf_op jit(solution)/shard_map/ppermute | solution.py:19
  317.7 10.6 %collective-permute-start.3 = (bf16[1,4,2,64,256]{4,3,2,1,0:T(8,128)(2,1)}, bf16[1,4,2,64,256]{4,3,2,1,0:T(8,128)(2,1)}, u32[]{:S(2)}, u32[]{:S(2)}) collective-permute-start(bf16[1,4,2,64,256]{4,3,2,1,0:T(8,128)(2,1)} %bitcast.16), channel_id=1, source_target_pairs={{4,0},{8,4},{12,8},{16,12},{20,16},{24,20},{28,24},{32,28},{36,32}... | collective-permute-start | bytes 786440 | tf_op jit(solution)/shard_map/ppermute | solution.py:21
  329.8 59.5 %copy-start.2 = (bf16[1024,256]{1,0:T(8,128)(2,1)S(1)}, bf16[1024,256]{1,0:T(8,128)(2,1)}, u32[]{:S(2)}) copy-start(bf16[1024,256]{1,0:T(8,128)(2,1)} %copy-done.1) | copy-start | bytes 1572868
  346.5 40.5 %all-to-all-start.2 = ((bf16[2,64,4,2,2,256]{5,3,2,4,0,1:T(2,128)(2,1)}), bf16[2,64,4,2,2,256]{5,3,2,4,0,1:T(2,128)(2,1)S(1)}, u32[]{:S(2)}, u32[]{:S(2)}) async-start(bf16[2,64,4,2,2,256]{5,3,2,4,0,1:T(2,128)(2,1)} %copy.28), calls=%async_computation.2 | async-start | bytes 2097152 | tf_op jit(solution)/shard_map/all_to_all | solution.py:98
  367.1 272.8 %all-reduce.4.cloned.1.call-start = ((), (), s32[]{:S(2)}) async-start(), calls=%async_computation.4 | async-start | bytes 9437184 | tf_op jit(solution)/shard_map/psum | solution.py:115
Sparse Core Ops, SparseCore 0:
  10.8 248.9 all-gather.1
  398.7 241.1 all-reduce.3
where the time goes:
time: 652 us
  waiting for transfers between devices  540 us (83%)
  starting transfers between devices  39.1 us (6%)
  local copies, waits for them, and re-layouts  23 us (4%)
  between operations  13.8 us (2%)
  matrix products  13.1 us (2%)
  blocking collectives  13 us (2%)
  other arithmetic  9.82 us (2%)
    all_gather x1, waiting for transfers between devices, on_device(): lax.all_gather(codebook, 'slab', axis=0, tiled=True)  252 us
    psum x1, waiting for transfers between devices, on_device(): summed = lax.psum(partial_grad, ('slab', 'dp'))  241 us
    all_to_all x1, starting transfers between devices, on_device(): lax.all_to_all(lax.all_to_all(jnp.stack([flipped, flipped]), 'section', s...  20.5 us
    all_to_all x1, waiting for transfers between devices, on_device(): lax.all_to_all(lax.all_to_all(jnp.stack([flipped, flipped]), 'section', s...  18.5 us
    all_to_all x1, waiting for transfers between devices, on_device(): lax.all_to_all(turned, 'slab', split_axis=0, concat_axis=3, tiled=True)  14.9 us
  transfers between devices with their start and end apart: 8, of which 8 were waited for; matrix products, arithmetic and copies ran while one was open for 0% of the time, Pallas kernels for 0%

commit v1 on v0

v1 whole, which is shorter than its diff:
```python
import math

import jax
import jax.numpy as jnp
from jax import lax
from jax.sharding import Mesh, PartitionSpec as P

COMMIT = 0.5
SLAB = ("zh", "y", "x")
Z = ("zh", "dp")
F32 = jnp.float32
BF16 = jnp.bfloat16
F16 = jnp.float16
TINY = 2.0**-100


def silu_slope(pre_act):
    sig = jax.nn.sigmoid(pre_act)
    return sig * (1.0 + pre_act * (1.0 - sig))


def columns(padded, offset_sign, row_count, frame_count, across):
    pieces = []
    for tap_t in range(2):
        for tap_r in range(3):
            for tap_q in range(3):
                shift_t = 1 + offset_sign * (tap_t - 1)
                shift_r = 1 + offset_sign * (tap_r - 1)
                shift_q = 1 + offset_sign * (tap_q - 1)
                pieces.append(
                    padded[
                        shift_r : shift_r + row_count,
                        :,
                        shift_t : shift_t + frame_count,
                        shift_q : shift_q + across,
                        :,
                    ]
                )
    return jnp.concatenate(pieces, axis=-1)


def tap_columns(rimmed, offset_sign):
    rows, _, frames, across, channels = rimmed.shape
    padded = jnp.pad(rimmed, ((0, 0), (0, 0), (1, 1), (1, 1), (0, 0)))
    return columns(padded, offset_sign, rows - 2, frames, across).reshape(-1, 18 * channels)


def neighbours(lower, upper):
    count = lax.axis_size(SLAB)
    above = lax.ppermute(lower, SLAB, [(i, i + 1) for i in range(count - 1)])
    below = lax.ppermute(upper, SLAB, [(i + 1, i) for i in range(count - 1)])
    return above, below


def exchange(cells, axes):
    return lax.all_to_all(cells, axes, split_axis=0, concat_axis=0, tiled=True)


def on_device(fields, kernels, codebook, codes):
    section_id = lax.axis_index("section")
    decoder = section_id == 1
    slab_id = lax.axis_index(SLAB)
    slabs = lax.axis_size(SLAB)
    own_field = fields[0]
    kernel = kernels[0]
    kernel = jnp.where(decoder, jnp.swapaxes(kernel, 1, 2), kernel)
    row_count, batch_count, frame_count, across, channels = own_field.shape
    book = codebook.shape[0]
    positions = row_count * batch_count * frame_count * across
    slots = max(16, 2 * positions // slabs)

    edge = jnp.full((1,) + codes.shape[1:], -1, codes.dtype)
    shifted = jnp.concatenate([edge, codes, edge], axis=0)
    pairs = lax.dynamic_slice_in_dim(shifted, section_id * row_count, codes.shape[0], 0)
    wanted = pairs.reshape(slabs, positions)
    owner = jnp.where(wanted >= 0, wanted // book, -1)
    before = (
        lax.broadcasted_iota(jnp.int32, (positions, positions), 0)
        < lax.broadcasted_iota(jnp.int32, (positions, positions), 1)
    ).astype(BF16)

    mine = owner == slab_id
    rank = jnp.dot(mine.astype(BF16), before, preferred_element_type=F32).astype(jnp.int32)
    rank = jnp.where(mine, rank, -1)
    local = wanted - slab_id * book
    slot_ids = lax.broadcasted_iota(jnp.int32, (1, slots, 1), 1)
    asked = jnp.sum(jnp.where(rank[:, None, :] == slot_ids, local[:, None, :], 0), axis=-1)
    picks = (
        asked.reshape(-1, 1) == lax.broadcasted_iota(jnp.int32, (1, book), 1)
    ).astype(BF16)
    words = jnp.dot(picks, codebook, preferred_element_type=F32).astype(BF16)
    words = words.reshape(slabs, slots, channels)

    turned = jnp.transpose(own_field, (3, 1, 2, 0, 4)).reshape(slabs, -1, channels)
    arrived = exchange(jnp.concatenate([words, turned], axis=1), SLAB)
    looked = arrived[:, :slots].reshape(slabs * slots, channels)
    cotangent = arrived[:, slots:].reshape(
        slabs, row_count, batch_count, frame_count, row_count, channels
    )
    cotangent = jnp.transpose(cotangent, (1, 2, 3, 0, 4, 5)).reshape(positions, channels)

    own_wanted = lax.dynamic_index_in_dim(wanted, slab_id, 0, keepdims=False)
    own_owner = lax.dynamic_index_in_dim(owner, slab_id, 0, keepdims=False)
    from_each = own_owner[None, :] == lax.broadcasted_iota(jnp.int32, (slabs, 1), 0)
    place = jnp.dot(from_each.astype(BF16), before, preferred_element_type=F32).astype(jnp.int32)
    place = jnp.sum(jnp.where(from_each, place, 0), axis=0)
    place = jnp.where(own_wanted >= 0, own_owner * slots + place, -1)
    gather = (
        place[:, None] == lax.broadcasted_iota(jnp.int32, (1, slabs * slots), 1)
    ).astype(BF16)
    fast = jnp.dot(gather, looked, preferred_element_type=F32).astype(BF16)

    every_owner = jnp.where(shifted >= 0, shifted // book, -1).reshape(slabs + 1, 1, positions)
    counts = jnp.sum(
        (every_owner == lax.broadcasted_iota(jnp.int32, (1, slabs, 1), 1)).astype(F32), axis=-1
    )
    crowded = jnp.full((lax.axis_size("dp"), 8, 128), jnp.max(counts) - slots)
    crowded = jnp.max(exchange(crowded, "dp")) > 0

    def whole_book(_):
        every = lax.all_gather(codebook, SLAB, axis=0, tiled=True)
        taken = jnp.take(every, jnp.maximum(own_wanted, 0), axis=0)
        return jnp.where(own_wanted[:, None] >= 0, taken, 0).astype(BF16)

    pair = lax.cond(crowded, whole_book, lambda quick: quick, fast)
    other = lax.ppermute(pair, "section", [(0, 1), (1, 0)])
    quant = jnp.concatenate(
        [jnp.where(decoder, other, pair), jnp.where(decoder, pair, other)], axis=0
    ).reshape(row_count + 2, batch_count, frame_count, across, channels)
    above, below = neighbours(own_field[-1:], own_field[:1])
    rimmed = jnp.concatenate([above, own_field, below], axis=0)
    tap_cols = tap_columns(jnp.where(decoder, quant, rimmed), 1)
    pre_act = jnp.dot(tap_cols, kernel.reshape(-1, channels), preferred_element_type=F32)

    dec_grad = (cotangent.astype(F32) * silu_slope(pre_act)).astype(BF16)
    shaped = dec_grad.reshape(own_field.shape)
    above, below = neighbours(shaped[-1:], shaped[:1])
    grad_cols = tap_columns(jnp.concatenate([above, shaped, below], axis=0), -1)
    kernel_t = jnp.swapaxes(kernel, -1, -2).reshape(-1, channels)
    back_dec = jnp.dot(grad_cols, kernel_t, preferred_element_type=F32).astype(BF16)
    returned = lax.ppermute(back_dec, "section", [(1, 0)])
    own_quant = quant[1:-1].reshape(positions, channels)
    enc_grad = (
        returned.astype(F32) + COMMIT * (pre_act - own_quant.astype(F32))
    ).astype(BF16)
    weight_side = jnp.where(decoder, dec_grad, enc_grad)
    partial_grad = lax.dot_general(
        tap_cols, weight_side, (((0,), (0,)), ((), ())), preferred_element_type=F32
    )

    total = (
        row_count * slabs * across * batch_count * lax.axis_size("dp") * frame_count
    )
    nx, ny, nz = lax.axis_size("x"), lax.axis_size("y"), lax.axis_size(Z)
    ci = channels // nx // ny
    part = partial_grad.reshape(18, nx, ny * ci * channels // 128, 128)
    part = jnp.transpose(part, (1, 0, 2, 3))
    part = jnp.sum(exchange(part, "x").reshape(nx, 18, ny, -1, 128), axis=0)
    part = jnp.transpose(part, (1, 0, 2, 3))
    part = jnp.sum(exchange(part, "y"), axis=0)
    part = jnp.sum(exchange(part.reshape(nz, -1, 128), Z).reshape(nz, -1, 128), axis=0)
    part = part / math.sqrt(total)

    def collect(piece, axes, count):
        return exchange(jnp.broadcast_to(piece[None], (count,) + piece.shape), axes)

    exponent = jnp.clip(jnp.ceil(jnp.log2(jnp.max(jnp.abs(part)) + TINY)), -100.0, 120.0)
    coded = (part * jnp.exp2(-exponent)).astype(F16)
    share = jnp.concatenate([coded, jnp.full((8, 128), exponent).astype(F16)], axis=0)
    share = collect(share, Z, nz)
    share = collect(share, "y", ny)
    share = collect(share, "x", nx)
    scale = jnp.exp2(share[:, :, :, -1:, :1].astype(F32))
    share = share[:, :, :, :-8].astype(F32) * scale
    share = share.reshape(nx, ny, 18, -1, 128)
    share = jnp.transpose(share, (2, 0, 1, 3, 4)).reshape(2, 3, 3, channels, channels)
    share = jnp.where(decoder, jnp.swapaxes(share, 1, 2), share)
    return share[None]


def solution(mesh):
    sections, slabs, dps = (mesh.shape[a] for a in ("section", "slab", "dp"))
    nx = 4 if slabs >= 16 else 2
    inner = Mesh(
        mesh.devices.reshape(sections, slabs // (nx * nx), nx, nx, dps),
        ("section", "zh", "y", "x", "dp"),
    )
    placed = (
        P("section", SLAB, "dp", None, None, None),
        P("section", None, None, None, None, None),
        P(SLAB, None),
        P(None, "dp", None, None),
    )
    return jax.shard_map(
        on_device,
        mesh=inner,
        in_specs=placed,
        out_specs=P("section", None, None, None, None, None),
        check_vma=False,
    )
```

time: 652 us -> 331 us (0.51)
  waiting for transfers between devices: 540 us -> 25.5 us
  blocking collectives: 13 us -> 163 us
  other arithmetic: 9.82 us -> 27.2 us
  local copies, waits for them, and re-layouts: 23 us -> 39.6 us
    all_gather x1 -> x0, waiting for transfers between devices: 252 us -> none  [on_device(): lax.all_gather(codebook, 'slab', axis=0, tiled=True)]
    psum x1 -> x0, waiting for transfers between devices: 241 us -> none  [on_device(): summed = lax.psum(partial_grad, ('slab', 'dp'))]
    all_to_all x1 -> x6, blocking collectives: 13 us -> 163 us  [exchange(): return lax.all_to_all(cells, axes, split_axis=0, concat_axis=0, tiled=True)]
    all_to_all x2, waiting for transfers between devices: 33.4 us -> 16.9 us  [exchange(): return lax.all_to_all(cells, axes, split_axis=0, concat_axis=0, tiled=True)]
    reshape x0 -> x5, local copies, waits for them, and re-layouts: none -> 15.4 us  [the longest x2 8.65 us: on_device(): part = partial_grad.reshape(18, nx, ny * ci * channels // 128, 128)]
    ppermute x4 -> x6, starting transfers between devices: 12.4 us -> 24.9 us  [the longest x2 17.4 us: neighbours(): below = lax.ppermute(upper, SLAB, [(i + 1, i) for i in range(count - 1)])]
    gather x1 -> x0, local copies, waits for them, and re-layouts: 11.4 us -> none  [pick_rows(): taken = jnp.take(book_piece, jnp.clip(wanted, 0, book_count - 1), axis=0)]
    all_to_all x2, starting transfers between devices: 26.5 us -> 17.5 us  [exchange(): return lax.all_to_all(cells, axes, split_axis=0, concat_axis=0, tiled=True)]
  transfers between devices with their start and end apart: 8 -> 8, of which waited for: 8 -> 4; matrix products, arithmetic and copies ran while one was open for 0% -> 9% of each run, Pallas kernels for 0% -> 0%
where the time goes in v1:
time: 331 us; the launch traced here: 330 us
  blocking collectives  163 us (49%)
  starting transfers between devices  42.4 us (13%)
  local copies, waits for them, and re-layouts  39.6 us (12%)
  other arithmetic  27.2 us (8%)
  waiting for transfers between devices  25.5 us (8%)
  matrix products  16.1 us (5%)
  between operations  16.1 us (5%)
    all_to_all x6, blocking collectives, exchange(): return lax.all_to_all(cells, axes, split_axis=0, concat_axis=0, tiled=True)  163 us
    all_to_all x2, starting transfers between devices, exchange(): return lax.all_to_all(cells, axes, split_axis=0, concat_axis=0, tiled=True)  17.5 us
    ppermute x2, starting transfers between devices, neighbours(): below = lax.ppermute(upper, SLAB, [(i + 1, i) for i in range(count - 1)])  17.4 us
    all_to_all x2, waiting for transfers between devices, exchange(): return lax.all_to_all(cells, axes, split_axis=0, concat_axis=0, tiled=True)  16.9 us
    reshape x2, local copies, waits for them, and re-layouts, on_device(): part = partial_grad.reshape(18, nx, ny * ci * channels // 128, 128)  8.65 us
    convert_element_type x3, local copies, waits for them, and re-layouts, on_device(): dec_grad = (cotangent.astype(F32) * silu_slope(pre_act)).astype(BF16)  8.45 us
    broadcast_in_dim x1, other arithmetic, on_device(): return share[None]  6.7 us
  transfers between devices with their start and end apart: 8, of which 4 were waited for; matrix products, arithmetic and copies ran while one was open for 9% of the time, Pallas kernels for 0%

profile of v1, /device:TPU:2, one launch (start us, length us, event | category | flops | bytes accessed | tf_op | source)
XLA Modules:
  0.0 329.8 jit_solution(10398770500378840560)
XLA Ops:
  6.5 1.1 pad_add_fusion
  8.5 0.6 reduce_max.27
  10.4 5.9 %all-to-all-start = ((f32[4,8,128]{2,1,0:T(8,128)}), f32[4,8,128]{2,1,0:T(8,128)S(1)}, u32[]{:S(2)}, u32[]{:S(2)}) async-start(f32[4,8,128]{2,1,0:T(8,128)} %broadcast_in_dim.80), calls=%async_computation | async-start | bytes 32768 | tf_op jit(solution)/shard_map/all_to_all | solution.py:56
  16.3 1.6 copy.36
  18.9 1.2 select_reduce_fusion
  20.1 2.7 fusion.10
  22.8 1.2 pad_maximum_fusion
  24.1 11.6 %all-to-all-start.1 = ((bf16[32,96,256]{2,1,0:T(8,128)(2,1)}), bf16[32,96,256]{2,1,0:T(8,128)(2,1)S(1)}, u32[]{:S(2)}, u32[]{:S(2)}) async-start(bf16[32,96,256]{2,1,0:T(8,128)(2,1)} %pad_maximum_fusion), calls=%async_computation.1 | async-start | bytes 3145728 | tf_op jit(solution)/shard_map/all_to_all | solution.py:56
  35.7 0.8 slice_bitcast_fusion.1
  36.6 2.1 collective-permute-start.2
  38.7 3.7 %collective-permute-start.1 = (bf16[1,4,2,64,256]{4,3,2,1,0:T(8,128)(2,1)}, bf16[1,4,2,64,256]{4,3,2,1,0:T(8,128)(2,1)}, u32[]{:S(2)}, u32[]{:S(2)}) collective-permute-start(bf16[1,4,2,64,256]{4,3,2,1,0:T(8,128)(2,1)} %get-tuple-element.38), channel_id=1, source_target_pairs={{0,4},{4,8},{8,12},{12,16},{16,20},{20,24},{24,28},{28,32},{32,36}... | collective-permute-start | bytes 786440 | tf_op jit(solution)/shard_map/ppermute | solution.py:50
  42.8 0.7 reduce_max.28
  44.1 16.9 %all-to-all-done.1 = bf16[32,96,256]{2,1,0:T(8,128)(2,1)S(1)} async-done(((bf16[32,96,256]{2,1,0:T(8,128)(2,1)}), bf16[32,96,256]{2,1,0:T(8,128)(2,1)S(1)}, u32[]{:S(2)}, u32[]{:S(2)}) %all-to-all-start.1) | async-done | bytes 1572896 | tf_op jit(solution)/shard_map/all_to_all | solution.py:56
  61.1 1.5 fusion.14
  62.9 3.1 bitcast_select_fusion.1
  66.1 2.1 slice_convert_fusion
  68.2 2.8 reshape.154
  71.0 2.7 copy.50
  73.7 2.9 reshape.153
  76.7 1.3 broadcast_select_fusion.1
  78.0 0.7 copy-done.3
  78.8 1.2 maximum_select_fusion
  81.8 4.0 %multiply_convert_fusion = (bf16[1024,256]{1,0:T(8,128)(2,1)S(1)}, f32[1024,256]{1,0:T(8,128)}) fusion(f32[1024,256]{1,0:T(8,128)S(1)} %copy-done.5, bf16[1024,4608]{1,0:T(8,128)(2,1)S(1)} %bitcast.104, bf16[4608,256]{1,0:T(8,128)(2,1)S(1)} %bitcast.72), kind=kOutput, calls=%fused_computation.65 | convolution fusion | flops 2418278400 | bytes 14417920 | tf_op jit(solution)/shard_map/dot_general | solution.py:133
  85.8 0.8 fusion.57
  86.6 15.3 %collective-permute-start.4 = (bf16[1,4,2,64,256]{4,3,2,1,0:T(8,128)(2,1)}, bf16[1,4,2,64,256]{4,3,2,1,0:T(8,128)(2,1)}, u32[]{:S(2)}, u32[]{:S(2)}) collective-permute-start(bf16[1,4,2,64,256]{4,3,2,1,0:T(8,128)(2,1)} %bitcast.16), channel_id=1, source_target_pairs={{4,0},{8,4},{12,8},{16,12},{20,16},{24,20},{28,24},{32,28},{36,32}... | collective-permute-start | bytes 786440 | tf_op jit(solution)/shard_map/ppermute | solution.py:51
  101.9 1.9 collective-permute-start.3
  103.8 2.4 copy.39
  106.2 2.2 collective-permute-done.4
  108.4 4.1 %collective-permute-done.3 = bf16[1,4,2,64,256]{4,3,2,1,0:T(8,128)(2,1)} collective-permute-done((bf16[1,4,2,64,256]{4,3,2,1,0:T(8,128)(2,1)}, bf16[1,4,2,64,256]{4,3,2,1,0:T(8,128)(2,1)}, u32[]{:S(2)}, u32[]{:S(2)}) %collective-permute-start.3) | collective-permute-done | bytes 262176 | tf_op jit(solution)/shard_map/ppermute | solution.py:50
  112.5 1.5 select_maximum_fusion
  114.1 2.2 fusion.56
  116.7 1.3 pad_maximum_fusion.2
  118.4 2.6 convolution_convert_fusion
  121.0 1.6 collective-permute-start.5
  122.7 2.3 collective-permute-done.5
  125.0 4.6 %fusion.21 = f32[4608,256]{1,0:T(8,128)} fusion(bf16[1024,4608]{1,0:T(8,128)(2,1)S(1)} %bitcast.107, bf16[1024,256]{1,0:T(8,128)(2,1)S(1)} %get-tuple-element.42, f32[1024,256]{1,0:T(8,128)S(1)} %copy-done.8, bf16[1024,256]{1,0:T(8,128)(2,1)S(1)} %collective-permute-done.5, bf16[1024,256]{1,0:T(8,128)(2,1)S(1)} %get-tuple-element.32, ...), kind=kOutput, calls=%fused_computation.67 | convolution fusion | flops 2418540544 | bytes 17301504 | tf_op jit(solution)/shard_map/dot_general | solution.py:147
  129.6 5.8 %reshape.149 = f32[18,4,128,128]{3,2,1,0:T(8,128)} reshape(f32[4608,256]{1,0:T(8,128)} %fusion.21) | data formatting | bytes 9437184 | tf_op jit(solution)/shard_map/reshape | solution.py:156
  135.3 2.9 copy.49
  138.2 56.8 %all_to_all.40 = f32[4,18,128,128]{3,2,1,0:T(8,128)} all-to-all(f32[4,18,128,128]{3,2,1,0:T(8,128)S(1)} %bitcast.71), channel_id=1, replica_groups=mesh['section'=2,'zh'=2,'y'=4,'x'=4,'dp'=4] {'x'}, dimensions={0} | all-to-all | bytes 9437184 | tf_op jit(solution)/shard_map/all_to_all | solution.py:56
  195.0 2.8 reduce_sum.59
  198.0 18.1 %all_to_all.41 = f32[4,18,32,128]{3,2,1,0:T(8,128)S(1)} all-to-all(f32[4,18,32,128]{3,2,1,0:T(8,128)S(1)} %copy.41), channel_id=1, replica_groups=mesh['section'=2,'zh'=2,'y'=4,'x'=4,'dp'=4] {'y'}, dimensions={0} | all-to-all | bytes 2359296 | tf_op jit(solution)/shard_map/all_to_all | solution.py:56
  216.1 35.6 %all_to_all.42 = f32[8,72,128]{2,1,0:T(8,128)S(1)} all-to-all(f32[8,72,128]{2,1,0:T(8,128)S(1)} %bitcast.99), channel_id=1, replica_groups=mesh['section'=2,'zh'=2,'y'=4,'x'=4,'dp'=4] {'zh','dp'}, dimensions={0} | all-to-all | bytes 589824 | tf_op jit(solution)/shard_map/all_to_all | solution.py:56
  253.1 11.8 %all_to_all.43 = f16[8,80,128]{2,1,0:T(8,128)(2,1)S(1)} all-to-all(f16[8,80,128]{2,1,0:T(8,128)(2,1)S(1)} %broadcast_in_dim.84), channel_id=1, replica_groups=mesh['section'=2,'zh'=2,'y'=4,'x'=4,'dp'=4] {'zh','dp'}, dimensions={0} | all-to-all | bytes 327680 | tf_op jit(solution)/shard_map/all_to_all | solution.py:56
  265.1 11.2 %all_to_all.44 = f16[4,8,80,128]{3,2,1,0:T(8,128)(2,1)S(1)} all-to-all(f16[4,8,80,128]{3,2,1,0:T(8,128)(2,1)S(1)} %broadcast_in_dim.85), channel_id=1, replica_groups=mesh['section'=2,'zh'=2,'y'=4,'x'=4,'dp'=4] {'y'}, dimensions={0} | all-to-all | bytes 1310720 | tf_op jit(solution)/shard_map/all_to_all | solution.py:56
  276.8 29.4 %all_to_all.45 = f16[4,4,8,80,128]{4,3,2,1,0:T(8,128)(2,1)S(1)} all-to-all(f16[4,4,8,80,128]{4,3,2,1,0:T(8,128)(2,1)S(1)} %broadcast_in_dim.86), channel_id=1, replica_groups=mesh['section'=2,'zh'=2,'y'=4,'x'=4,'dp'=4] {'x'}, dimensions={0} | all-to-all | bytes 5242880 | tf_op jit(solution)/shard_map/all_to_all | solution.py:56
  307.0 2.9 copy.42
  310.0 6.3 %reshape.152 = f32[2,3,3,256,256]{4,3,2,1,0:T(8,128)} reshape(f32[18,4,4,32,128]{4,3,2,1,0:T(8,128)} %copy.42) | data formatting | bytes 9437184 | tf_op jit(solution)/shard_map/reshape | solution.py:176
  316.2 6.7 %fusion.2 = f32[1,2,3,3,256,256]{5,4,3,2,1,0:T(8,128)} fusion(f32[2,3,3,256,256]{4,3,2,1,0:T(8,128)} %reshape.152, pred[]{:T(512)S(6)} %eq.76), kind=kLoop, calls=%fused_computation.31 | loop fusion | flops 1179648 | bytes 9437185 | tf_op jit(solution)/shard_map/broadcast_in_dim | solution.py:178
  (93 shorter events, 8.1 us)
Async XLA Ops:
  10.4 13.7 %all-to-all-start = ((f32[4,8,128]{2,1,0:T(8,128)}), f32[4,8,128]{2,1,0:T(8,128)S(1)}, u32[]{:S(2)}, u32[]{:S(2)}) async-start(f32[4,8,128]{2,1,0:T(8,128)} %broadcast_in_dim.80), calls=%async_computation | async-start | bytes 32768 | tf_op jit(solution)/shard_map/all_to_all | solution.py:56
  18.1 17.6 %copy-start.1 = (bf16[1,2,4,2,64,256]{5,4,3,2,1,0:T(8,128)(2,1)S(1)}, bf16[1,2,4,2,64,256]{5,4,3,2,1,0:T(8,128)(2,1)}, u32[]{:S(2)}) copy-start(bf16[1,2,4,2,64,256]{5,4,3,2,1,0:T(8,128)(2,1)} %param.6) | copy-start | bytes 1572868
  24.1 36.9 %all-to-all-start.1 = ((bf16[32,96,256]{2,1,0:T(8,128)(2,1)}), bf16[32,96,256]{2,1,0:T(8,128)(2,1)S(1)}, u32[]{:S(2)}, u32[]{:S(2)}) async-start(bf16[32,96,256]{2,1,0:T(8,128)(2,1)} %pad_maximum_fusion), calls=%async_computation.1 | async-start | bytes 3145728 | tf_op jit(solution)/shard_map/all_to_all | solution.py:56
  36.6 41.5 %collective-permute-start.2 = (bf16[1,4,2,64,256]{4,3,2,1,0:T(8,128)(2,1)}, bf16[1,4,2,64,256]{4,3,2,1,0:T(8,128)(2,1)}, u32[]{:S(2)}, u32[]{:S(2)}) collective-permute-start(bf16[1,4,2,64,256]{4,3,2,1,0:T(8,128)(2,1)} %get-tuple-element.39), channel_id=1, source_target_pairs={{4,0},{8,4},{12,8},{16,12},{20,16},{24,20},{28,24},{32,28},{36,32}... | collective-permute-start | bytes 786440 | tf_op jit(solution)/shard_map/ppermute | solution.py:51
  38.7 39.3 %collective-permute-start.1 = (bf16[1,4,2,64,256]{4,3,2,1,0:T(8,128)(2,1)}, bf16[1,4,2,64,256]{4,3,2,1,0:T(8,128)(2,1)}, u32[]{:S(2)}, u32[]{:S(2)}) collective-permute-start(bf16[1,4,2,64,256]{4,3,2,1,0:T(8,128)(2,1)} %get-tuple-element.38), channel_id=1, source_target_pairs={{0,4},{4,8},{8,12},{12,16},{16,20},{20,24},{24,28},{28,32},{32,36}... | collective-permute-start | bytes 786440 | tf_op jit(solution)/shard_map/ppermute | solution.py:50
  61.0 1.6 copy-start
  62.7 14.0 %copy-start.6 = (bf16[1024,256]{1,0:T(8,128)(2,1)}, bf16[1024,256]{1,0:T(8,128)(2,1)S(1)}, u32[]{:S(2)}) copy-start(bf16[1024,256]{1,0:T(8,128)(2,1)S(1)} %get-tuple-element.46) | copy-start | bytes 1572868
  62.7 14.0 %collective-permute-start = (bf16[1024,256]{1,0:T(8,128)(2,1)S(1)}, bf16[1024,256]{1,0:T(8,128)(2,1)}, u32[]{:S(2)}, u32[]{:S(2)}) collective-permute-start(bf16[1024,256]{1,0:T(8,128)(2,1)S(1)} %get-tuple-element.46), channel_id=1, source_target_pairs={{0,128},{128,0},{1,129},{129,1},{2,130},{130,2},{3,131},{131,3},{4... | collective-permute-start | bytes 1572872 | tf_op jit(solution)/shard_map/ppermute | solution.py:126
  77.9 0.8 copy-start.3
  80.4 1.5 copy-start.5
  81.8 4.0 %copy-start.7 = (bf16[2,4,2,64,4608]{4,3,2,1,0:T(8,128)(2,1)}, bf16[2,4,2,64,4608]{4,3,2,1,0:T(8,128)(2,1)S(1)}, u32[]{:S(2)}) copy-start(bf16[2,4,2,64,4608]{4,3,2,1,0:T(8,128)(2,1)S(1)} %fusion.39) | copy-start | bytes 28311556
  86.6 21.8 %collective-permute-start.4 = (bf16[1,4,2,64,256]{4,3,2,1,0:T(8,128)(2,1)}, bf16[1,4,2,64,256]{4,3,2,1,0:T(8,128)(2,1)}, u32[]{:S(2)}, u32[]{:S(2)}) collective-permute-start(bf16[1,4,2,64,256]{4,3,2,1,0:T(8,128)(2,1)} %bitcast.16), channel_id=1, source_target_pairs={{4,0},{8,4},{12,8},{16,12},{20,16},{24,20},{28,24},{32,28},{36,32}... | collective-permute-start | bytes 786440 | tf_op jit(solution)/shard_map/ppermute | solution.py:51
  101.9 10.6 %collective-permute-start.3 = (bf16[1,4,2,64,256]{4,3,2,1,0:T(8,128)(2,1)}, bf16[1,4,2,64,256]{4,3,2,1,0:T(8,128)(2,1)}, u32[]{:S(2)}, u32[]{:S(2)}) collective-permute-start(bf16[1,4,2,64,256]{4,3,2,1,0:T(8,128)(2,1)} %bitcast.14), channel_id=1, source_target_pairs={{0,4},{4,8},{8,12},{12,16},{16,20},{20,24},{24,28},{28,32},{32,36}... | collective-permute-start | bytes 786440 | tf_op jit(solution)/shard_map/ppermute | solution.py:50
  116.5 1.9 copy-start.2
  118.3 6.6 %slice-start = ((s8[9437184]{0:T(1024)(128)(4,1)}), s8[4194304]{0:T(1024)(128)(4,1)S(1)}, s32[]{:S(2)}) async-start(s8[9437184]{0:T(1024)(128)(4,1)} %bitcast.105), calls=%async_computation.9 | async-start | bytes 8388608
  118.4 6.6 %copy-start.4 = (bf16[1024,256]{1,0:T(8,128)(2,1)S(1)}, bf16[1024,256]{1,0:T(8,128)(2,1)}, u32[]{:S(2)}) copy-start(bf16[1024,256]{1,0:T(8,128)(2,1)} %copy-done.3) | copy-start | bytes 1572868
  118.4 6.6 %slice-start.1 = ((s8[9437184]{0:T(1024)(128)(4,1)}), s8[4194304]{0:T(1024)(128)(4,1)S(1)}, s32[]{:S(2)}) async-start(s8[9437184]{0:T(1024)(128)(4,1)} %bitcast.105), calls=%async_computation.10 | async-start | bytes 8388608
  118.4 6.6 %slice-start.2 = ((s8[9437184]{0:T(1024)(128)(4,1)}), s8[1048576]{0:T(1024)(128)(4,1)S(1)}, s32[]{:S(2)}) async-start(s8[9437184]{0:T(1024)(128)(4,1)} %bitcast.105), calls=%async_computation.11 | async-start | bytes 2097152
  118.4 6.6 %copy-start.8 = (f32[1024,256]{1,0:T(8,128)S(1)}, f32[1024,256]{1,0:T(8,128)}, u32[]{:S(2)}) copy-start(f32[1024,256]{1,0:T(8,128)} %get-tuple-element.43) | copy-start | bytes 3145732
  121.0 3.9 %collective-permute-start.5 = (bf16[1024,256]{1,0:T(8,128)(2,1)S(1)}, bf16[1024,256]{1,0:T(8,128)(2,1)S(1)}, u32[]{:S(2)}, u32[]{:S(2)}) collective-permute-start(bf16[1024,256]{1,0:T(8,128)(2,1)S(1)} %convolution_convert_fusion), channel_id=1, source_target_pairs={{128,0},{129,1},{130,2},{131,3},{132,4},{133,5},{134,6},{135,7},{1... | collective-permute-start | bytes 1572872 | tf_op jit(solution)/shard_map/ppermute | solution.py:141

commit v2 on v1

--- a/solution.py
+++ b/solution.py
@@ -3,6 +3,8 @@
 import jax
 import jax.numpy as jnp
 from jax import lax
+from jax.experimental import pallas as pl
+from jax.experimental.pallas import tpu as pltpu
 from jax.sharding import Mesh, PartitionSpec as P
 
 COMMIT = 0.5
@@ -10,8 +12,10 @@
 Z = ("zh", "dp")
 F32 = jnp.float32
 BF16 = jnp.bfloat16
-F16 = jnp.float16
+I16 = jnp.int16
 TINY = 2.0**-100
+STEPS = 32000.0
+VMEM_LIMIT = 48 * 1024 * 1024
 
 
 def silu_slope(pre_act):
@@ -56,6 +60,133 @@
     return lax.all_to_all(cells, axes, split_axis=0, concat_axis=0, tiled=True)
 
 
+def coded(values):
+    top = jnp.max(jnp.abs(values), axis=tuple(range(values.ndim)), keepdims=True)
+    exponent = jnp.ceil(jnp.log2(top + TINY))
+    return jnp.round(values * (jnp.exp2(-exponent) * STEPS)), exponent
+
+
+def decoded_scale(exponents):
+    return jnp.exp2(exponents.astype(F32)) * (1.0 / STEPS)
+
+
+def framed(piece):
+    steps, exponent = coded(piece)
+    tail = jnp.broadcast_to(exponent, (8, 128))
+    return jnp.concatenate([steps, tail], axis=0).astype(I16)
+
+
+def unframed(rows):
+    wide = rows.astype(F32)
+    return wide[:-8] * (jnp.exp2(wide[-1:]) * (1.0 / STEPS))
+
+
+def pack_plane(grads, parts):
+    taps, ins, outs = grads.shape
+    size = ins // parts
+
+    def body(grads_ref, packed_ref):
+        steps, exponent = coded(grads_ref[...])
+        packed_ref[0, :taps] = steps.astype(I16)
+        packed_ref[0, taps] = jnp.broadcast_to(exponent[0], (size, outs)).astype(I16)
+
+    return pl.pallas_call(
+        body,
+        grid=(parts,),
+        in_specs=[pl.BlockSpec((taps, size, outs), lambda k: (0, k, 0))],
+        out_specs=pl.BlockSpec((1, taps + 1, size, outs), lambda k: (k, 0, 0, 0)),
+        out_shape=jax.ShapeDtypeStruct((parts, taps + 1, size, outs), I16),
+    )(grads)
+
+
+def sum_plane(packed, pieces):
+    senders, taps, size, outs = packed.shape
+    taps = taps - 1
+    half = taps // 2
+
+    def body(packed_ref, framed_ref, total):
+        scales = [decoded_scale(packed_ref[s, taps])[:1, :1] for s in range(senders)]
+        for tap in range(taps):
+            acc = packed_ref[0, tap].astype(F32) * scales[0]
+            for s in range(1, senders):
+                acc += packed_ref[s, tap].astype(F32) * scales[s]
+            total[tap] = acc
+        place = 0
+        for frame in range(2):
+            for oct_ in range(size // 8):
+                for lane in range(outs // 128):
+                    piece = total[
+                        frame * half : (frame + 1) * half,
+                        oct_ * 8 : oct_ * 8 + 8,
+                        lane * 128 : lane * 128 + 128,
+                    ]
+                    framed_ref[place] = framed(piece.reshape(half * 8, 128))
+                    place += 1
+
+    return pl.pallas_call(
+        body,
+        out_shape=jax.ShapeDtypeStruct((pieces, half * 8 + 8, 128), I16),
+        scratch_shapes=[pltpu.VMEM((taps, size, outs), F32)],
+        compiler_params=pltpu.CompilerParams(vmem_limit_bytes=VMEM_LIMIT),
+    )(packed)
+
+
+def sum_line(framed_parts, factor):
+    def body(parts_ref, out_ref):
+        acc = unframed(parts_ref[0])
+        for s in range(1, framed_parts.shape[0]):
+            acc += unframed(parts_ref[s])
+        result = framed(acc * factor)
+        for s in range(framed_parts.shape[0]):
+            out_ref[s] = result
+
+    return pl.pallas_call(
+        body, out_shape=jax.ShapeDtypeStruct(framed_parts.shape, I16)
+    )(framed_parts)
+
+
+def unpack(plane, section_id, channels):
+    parts, pieces, rows, _ = plane.shape
+    size = channels // parts
+
+    def body(section_ref, plane_ref, out_ref):
+        def write(turned):
+            place = 0
+            for frame in range(2):
+                for oct_ in range(size // 8):
+                    for lane in range(channels // 128):
+                        piece = unframed(plane_ref[0, place]).reshape(3, 3, 8, 128)
+                        for r in range(3):
+                            for q in range(3):
+                                out_ref[
+                                    frame,
+                                    q if turned else r,
+                                    r if turned else q,
+                                    oct_ * 8 : oct_ * 8 + 8,
+                                    lane * 128 : lane * 128 + 128,
+                                ] = piece[r, q]
+                        place += 1
+
+        @pl.when(section_ref[0] == 0)
+        def _():
+            write(False)
+
+        @pl.when(section_ref[0] == 1)
+        def _():
+            write(True)
+
+    return pl.pallas_call(
+        body,
+        grid_spec=pltpu.PrefetchScalarGridSpec(
+            num_scalar_prefetch=1,
+            grid=(parts,),
+            in_specs=[pl.BlockSpec((1, pieces, rows, 128), lambda k, _: (k, 0, 0, 0))],
+            out_specs=pl.BlockSpec((2, 3, 3, size, channels), lambda k, _: (0, 0, 0, k, 0)),
+        ),
+        out_shape=jax.ShapeDtypeStruct((2, 3, 3, channels, channels), F32),
+    )(section_id.reshape(1).astype(jnp.int32), plane)
+
+
 def on_device(fields, kernels, codebook, codes):
     section_id = lax.axis_index("section")
     decoder = section_id == 1
@@ -152,30 +283,11 @@
         row_count * slabs * across * batch_count * lax.axis_size("dp") * frame_count
     )
     nx, ny, nz = lax.axis_size("x"), lax.axis_size("y"), lax.axis_size(Z)
-    ci = channels // nx // ny
-    part = partial_grad.reshape(18, nx, ny * ci * channels // 128, 128)
-    part = jnp.transpose(part, (1, 0, 2, 3))
-    part = jnp.sum(exchange(part, "x").reshape(nx, 18, ny, -1, 128), axis=0)
-    part = jnp.transpose(part, (1, 0, 2, 3))
-    part = jnp.sum(exchange(part, "y"), axis=0)
-    part = jnp.sum(exchange(part.reshape(nz, -1, 128), Z).reshape(nz, -1, 128), axis=0)
-    part = part / math.sqrt(total)
-
-    def collect(piece, axes, count):
-        return exchange(jnp.broadcast_to(piece[None], (count,) + piece.shape), axes)
-
-    exponent = jnp.clip(jnp.ceil(jnp.log2(jnp.max(jnp.abs(part)) + TINY)), -100.0, 120.0)
-    coded = (part * jnp.exp2(-exponent)).astype(F16)
-    share = jnp.concatenate([coded, jnp.full((8, 128), exponent).astype(F16)], axis=0)
-    share = collect(share, Z, nz)
-    share = collect(share, "y", ny)
-    share = collect(share, "x", nx)
-    scale = jnp.exp2(share[:, :, :, -1:, :1].astype(F32))
-    share = share[:, :, :, :-8].astype(F32) * scale
-    share = share.reshape(nx, ny, 18, -1, 128)
-    share = jnp.transpose(share, (2, 0, 1, 3, 4)).reshape(2, 3, 3, channels, channels)
-    share = jnp.where(decoder, jnp.swapaxes(share, 1, 2), share)
-    return share[None]
+    plane = exchange(pack_plane(partial_grad.reshape(18, channels, channels), nx * ny), ("y", "x"))
+    line = exchange(sum_plane(plane, nz), Z)
+    line = exchange(sum_line(line, 1.0 / math.sqrt(total)), Z)
+    plane = exchange(jnp.broadcast_to(line[None], (nx * ny,) + line.shape), ("y", "x"))
+    return unpack(plane, section_id, channels)[None]
 
 
 def solution(mesh):

time: 331 us -> 296 us (0.89)
  blocking collectives: 163 us -> 119 us
  Pallas kernels: 0 us -> 24 us
  other arithmetic: 27.2 us -> 16 us
  local copies, waits for them, and re-layouts: 39.6 us -> 34.2 us
  matrix products: 16.1 us -> 20.4 us
    all_to_all x6 -> x4, blocking collectives: 163 us -> 119 us  [exchange(): return lax.all_to_all(cells, axes, split_axis=0, concat_axis=0, tiled=True)]
    pallas_call x0 -> x4, Pallas kernels: none -> 24 us  [the longest x1 11.3 us: pack_plane(): pl.pallas_call(body, grid=(parts,), in_specs=[pl.BlockSpec((taps, size, o...]
    broadcast_in_dim x1 -> x0, other arithmetic: 6.7 us -> none  [on_device(): return share[None]]
    dot_general x1, matrix products: 4.58 us -> 8.82 us  [on_device(): lax.dot_general(tap_cols, weight_side, (((0,), (0,)), ((), ())), preferre...]
    reshape x3 -> x1, local copies, waits for them, and re-layouts: 14.9 us -> 12.6 us  [tap_columns(): columns(padded, offset_sign, rows - 2, frames, across)]
  transfers between devices with their start and end apart: 8 -> 8, of which waited for: 4 -> 3; matrix products, arithmetic and copies ran while one was open for 9% -> 14% of each run, Pallas kernels for 0% -> 0%
where the time goes in v2:
time: 296 us; the launch traced here: 295 us
  blocking collectives  119 us (40%)
  starting transfers between devices  42.4 us (14%)
  local copies, waits for them, and re-layouts  34.2 us (12%)
  Pallas kernels  24 us (8%)
  waiting for transfers between devices  23.4 us (8%)
  matrix products  20.4 us (7%)
  other arithmetic  16 us (5%)
  between operations  15.2 us (5%)
    all_to_all x4, blocking collectives, exchange(): return lax.all_to_all(cells, axes, split_axis=0, concat_axis=0, tiled=True)  119 us
    all_to_all x2, starting transfers between devices, exchange(): return lax.all_to_all(cells, axes, split_axis=0, concat_axis=0, tiled=True)  17.5 us
    ppermute x2, starting transfers between devices, neighbours(): below = lax.ppermute(upper, SLAB, [(i + 1, i) for i in range(count - 1)])  17.4 us
    all_to_all x2, waiting for transfers between devices, exchange(): return lax.all_to_all(cells, axes, split_axis=0, concat_axis=0, tiled=True)  17.1 us
    reshape x1, local copies, waits for them, and re-layouts, tap_columns(): columns(padded, offset_sign, rows - 2, frames, across)  12.6 us
    pallas_call x1, Pallas kernels, pack_plane(): pl.pallas_call(body, grid=(parts,), in_specs=[pl.BlockSpec((taps, size, o...  11.3 us
    pallas_call x1, Pallas kernels, unpack(): pl.pallas_call(body, grid_spec=pltpu.PrefetchScalarGridSpec(num_scalar_pr...  10.2 us
    dot_general x1, matrix products, on_device(): lax.dot_general(tap_cols, weight_side, (((0,), (0,)), ((), ())), preferre...  8.82 us
  transfers between devices with their start and end apart: 8, of which 3 were waited for; matrix products, arithmetic and copies ran while one was open for 14% of the time, Pallas kernels for 0%

profile of v2, /device:TPU:2, one launch (start us, length us, event | category | flops | bytes accessed | tf_op | source)
XLA Modules:
  0.0 294.5 jit_solution(4498321751454378612)
XLA Ops:
  6.5 1.1 pad_add_fusion
  8.0 0.5 convert_reduce_fusion
  8.5 0.6 reduce_max.18
  9.8 0.6 broadcast_in_dim.67
  10.4 5.9 %all-to-all-start = ((f32[4,8,128]{2,1,0:T(8,128)}), f32[4,8,128]{2,1,0:T(8,128)S(1)}, u32[]{:S(2)}, u32[]{:S(2)}) async-start(f32[4,8,128]{2,1,0:T(8,128)} %broadcast_in_dim.67), calls=%async_computation | async-start | bytes 32768 | tf_op jit(solution)/shard_map/all_to_all | solution.py:60
  16.3 1.7 copy.19
  18.5 0.4 fusion.17
  18.9 1.2 select_reduce_fusion
  20.2 2.7 fusion.9
  22.9 1.2 pad_maximum_fusion
  24.2 11.6 %all-to-all-start.1 = ((bf16[32,96,256]{2,1,0:T(8,128)(2,1)}), bf16[32,96,256]{2,1,0:T(8,128)(2,1)S(1)}, u32[]{:S(2)}, u32[]{:S(2)}) async-start(bf16[32,96,256]{2,1,0:T(8,128)(2,1)} %pad_maximum_fusion), calls=%async_computation.1 | async-start | bytes 3145728 | tf_op jit(solution)/shard_map/all_to_all | solution.py:60
  35.8 0.8 slice_bitcast_fusion.1
  36.6 2.1 collective-permute-start.2
  38.8 3.7 %collective-permute-start.1 = (bf16[1,4,2,64,256]{4,3,2,1,0:T(8,128)(2,1)}, bf16[1,4,2,64,256]{4,3,2,1,0:T(8,128)(2,1)}, u32[]{:S(2)}, u32[]{:S(2)}) collective-permute-start(bf16[1,4,2,64,256]{4,3,2,1,0:T(8,128)(2,1)} %get-tuple-element.38), channel_id=1, source_target_pairs={{0,4},{4,8},{8,12},{12,16},{16,20},{20,24},{24,28},{28,32},{32,36}... | collective-permute-start | bytes 786440 | tf_op jit(solution)/shard_map/ppermute | solution.py:54
  42.9 0.6 reduce_max.19
  44.0 17.1 %all-to-all-done.1 = bf16[32,96,256]{2,1,0:T(8,128)(2,1)S(1)} async-done(((bf16[32,96,256]{2,1,0:T(8,128)(2,1)}), bf16[32,96,256]{2,1,0:T(8,128)(2,1)S(1)}, u32[]{:S(2)}, u32[]{:S(2)}) %all-to-all-start.1) | async-done | bytes 1572896 | tf_op jit(solution)/shard_map/all_to_all | solution.py:60
  61.2 1.5 fusion.13
  63.0 3.1 %bitcast_select_fusion = bf16[2,3,3,256,256]{4,3,2,1,0:T(8,128)(2,1)S(1)} fusion(bf16[1,2,3,3,256,256]{5,4,3,2,1,0:T(8,128)(2,1)} %param.7, pred[]{:T(512)S(6)} %eq.76), kind=kLoop, calls=%fused_computation.46 | loop fusion | flops 1179648 | bytes 4718593 | tf_op jit(solution)/shard_map/jit(_where)/select_n | solution.py:197
  66.2 2.2 slice_convert_fusion
  68.3 2.8 reshape.140
  71.1 2.7 copy.27
  73.9 2.9 reshape.139
  76.8 1.3 broadcast_select_fusion.1
  78.2 0.7 copy-done.4
  78.9 1.2 maximum_select_fusion
  81.9 4.0 %multiply_convert_fusion = (bf16[1024,256]{1,0:T(8,128)(2,1)S(1)}, f32[1024,256]{1,0:T(8,128)}) fusion(f32[1024,256]{1,0:T(8,128)S(1)} %copy-done.6, bf16[1024,4608]{1,0:T(8,128)(2,1)S(1)} %bitcast.60, bf16[4608,256]{1,0:T(8,128)(2,1)S(1)} %bitcast.62), kind=kOutput, calls=%fused_computation.61 | convolution fusion | flops 2418278400 | bytes 14417920 | tf_op jit(solution)/shard_map/dot_general | solution.py:264
  85.9 0.8 fusion.54
  86.8 15.3 %collective-permute-start.4 = (bf16[1,4,2,64,256]{4,3,2,1,0:T(8,128)(2,1)}, bf16[1,4,2,64,256]{4,3,2,1,0:T(8,128)(2,1)}, u32[]{:S(2)}, u32[]{:S(2)}) collective-permute-start(bf16[1,4,2,64,256]{4,3,2,1,0:T(8,128)(2,1)} %bitcast.19), channel_id=1, source_target_pairs={{4,0},{8,4},{12,8},{16,12},{20,16},{24,20},{28,24},{32,28},{36,32}... | collective-permute-start | bytes 786440 | tf_op jit(solution)/shard_map/ppermute | solution.py:55
  102.0 1.9 collective-permute-start.3
  104.0 2.4 copy.23
  106.4 2.2 collective-permute-done.4
  108.6 4.1 %collective-permute-done.3 = bf16[1,4,2,64,256]{4,3,2,1,0:T(8,128)(2,1)} collective-permute-done((bf16[1,4,2,64,256]{4,3,2,1,0:T(8,128)(2,1)}, bf16[1,4,2,64,256]{4,3,2,1,0:T(8,128)(2,1)}, u32[]{:S(2)}, u32[]{:S(2)}) %collective-permute-start.3) | collective-permute-done | bytes 262176 | tf_op jit(solution)/shard_map/ppermute | solution.py:54
  112.7 1.5 select_maximum_fusion
  114.2 2.2 fusion.53
  116.9 1.3 pad_maximum_fusion.2
  118.6 2.6 convolution_convert_fusion
  121.2 1.6 collective-permute-start.5
  122.8 12.6 %copy.20 = bf16[1024,4608]{0,1:T(8,128)(2,1)} copy(bf16[1024,4608]{1,0:T(8,128)(2,1)} %bitcast.61) | data formatting | bytes 18874368 | tf_op jit(solution)/shard_map/reshape | solution.py:49
  135.5 8.8 %fusion.21.grads_ref = f32[18,256,256]{2,1,0:T(8,128)} fusion(bf16[18,256,1024]{2,1,0:T(8,128)(2,1)} %bitcast.64, bf16[1024,256]{1,0:T(8,128)(2,1)S(1)} %get-tuple-element.42, f32[1024,256]{1,0:T(8,128)} %get-tuple-element.43, bf16[1024,256]{1,0:T(8,128)(2,1)S(1)} %collective-permute-done.5, bf16[1024,256]{1,0:T(8,128)(2,1)S(1)} %get-tuple-element.32, ...), kind=kOutput, calls=%fused_computation.64 | convolution fusion | flops 2418540544 | bytes 17301504 | tf_op jit(solution)/shard_map/dot_general | solution.py:278
  144.3 11.3 %shard_map.46 = s16[16,19,16,256]{3,2,1,0:T(8,128)(2,1)} custom-call(f32[18,256,256]{2,1,0:T(8,128)} %fusion.21.grads_ref), custom_call_target="tpu_custom_call" | custom-call | tf_op jit(solution)/shard_map/pallas_call | solution.py:93
  155.5 37.9 %all_to_all.30.packed_ref = s16[16,19,16,256]{3,2,1,0:T(8,128)(2,1)S(1)} all-to-all(s16[16,19,16,256]{3,2,1,0:T(8,128)(2,1)} %shard_map.46), channel_id=1, replica_groups=mesh['section'=2,'zh'=2,'y'=4,'x'=4,'dp'=4] {'y','x'}, dimensions={0} | all-to-all | bytes 4980736 | tf_op jit(solution)/shard_map/all_to_all | solution.py:60
  193.5 0.8 shard_map.47
  194.3 33.1 %all_to_all.31.parts_ref = s16[8,80,128]{2,1,0:T(8,128)(2,1)} all-to-all(s16[8,80,128]{2,1,0:T(8,128)(2,1)S(1)} %shard_map.47), channel_id=1, replica_groups=mesh['section'=2,'zh'=2,'y'=4,'x'=4,'dp'=4] {'zh','dp'}, dimensions={0} | all-to-all | bytes 327680 | tf_op jit(solution)/shard_map/all_to_all | solution.py:60
  227.4 1.8 shard_map.48
  229.2 12.7 %all_to_all.32 = s16[8,80,128]{2,1,0:T(8,128)(2,1)S(1)} all-to-all(s16[8,80,128]{2,1,0:T(8,128)(2,1)} %shard_map.48), channel_id=1, replica_groups=mesh['section'=2,'zh'=2,'y'=4,'x'=4,'dp'=4] {'zh','dp'}, dimensions={0} | all-to-all | bytes 327680 | tf_op jit(solution)/shard_map/all_to_all | solution.py:60
  241.9 0.5 broadcast_in_dim.71
  242.4 35.1 %all_to_all.33.plane_ref = s16[16,8,80,128]{3,2,1,0:T(8,128)(2,1)} all-to-all(s16[16,8,80,128]{3,2,1,0:T(8,128)(2,1)S(1)} %broadcast_in_dim.71), channel_id=1, replica_groups=mesh['section'=2,'zh'=2,'y'=4,'x'=4,'dp'=4] {'y','x'}, dimensions={0} | all-to-all | bytes 5242880 | tf_op jit(solution)/shard_map/all_to_all | solution.py:60
  277.5 10.2 %shard_map.49 = f32[2,3,3,256,256]{4,3,2,1,0:T(8,128)} custom-call(s32[1]{0:T(128)} %bitcast.section_ref, s16[16,8,80,128]{3,2,1,0:T(8,128)(2,1)} %all_to_all.33.plane_ref), custom_call_target="tpu_custom_call" | custom-call | tf_op jit(solution)/shard_map/pallas_call | solution.py:178
  (71 shorter events, 4.3 us)
Async XLA Ops:
  10.4 13.8 %all-to-all-start = ((f32[4,8,128]{2,1,0:T(8,128)}), f32[4,8,128]{2,1,0:T(8,128)S(1)}, u32[]{:S(2)}, u32[]{:S(2)}) async-start(f32[4,8,128]{2,1,0:T(8,128)} %broadcast_in_dim.67), calls=%async_computation | async-start | bytes 32768 | tf_op jit(solution)/shard_map/all_to_all | solution.py:60
  16.3 19.5 %copy-start.2 = (bf16[1,2,4,2,64,256]{5,4,3,2,1,0:T(8,128)(2,1)S(1)}, bf16[1,2,4,2,64,256]{5,4,3,2,1,0:T(8,128)(2,1)}, u32[]{:S(2)}) copy-start(bf16[1,2,4,2,64,256]{5,4,3,2,1,0:T(8,128)(2,1)} %param.6) | copy-start | bytes 1572868
  24.2 37.0 %all-to-all-start.1 = ((bf16[32,96,256]{2,1,0:T(8,128)(2,1)}), bf16[32,96,256]{2,1,0:T(8,128)(2,1)S(1)}, u32[]{:S(2)}, u32[]{:S(2)}) async-start(bf16[32,96,256]{2,1,0:T(8,128)(2,1)} %pad_maximum_fusion), calls=%async_computation.1 | async-start | bytes 3145728 | tf_op jit(solution)/shard_map/all_to_all | solution.py:60
  36.6 41.5 %collective-permute-start.2 = (bf16[1,4,2,64,256]{4,3,2,1,0:T(8,128)(2,1)}, bf16[1,4,2,64,256]{4,3,2,1,0:T(8,128)(2,1)}, u32[]{:S(2)}, u32[]{:S(2)}) collective-permute-start(bf16[1,4,2,64,256]{4,3,2,1,0:T(8,128)(2,1)} %get-tuple-element.39), channel_id=1, source_target_pairs={{4,0},{8,4},{12,8},{16,12},{20,16},{24,20},{28,24},{32,28},{36,32}... | collective-permute-start | bytes 786440 | tf_op jit(solution)/shard_map/ppermute | solution.py:55
  38.8 39.4 %collective-permute-start.1 = (bf16[1,4,2,64,256]{4,3,2,1,0:T(8,128)(2,1)}, bf16[1,4,2,64,256]{4,3,2,1,0:T(8,128)(2,1)}, u32[]{:S(2)}, u32[]{:S(2)}) collective-permute-start(bf16[1,4,2,64,256]{4,3,2,1,0:T(8,128)(2,1)} %get-tuple-element.38), channel_id=1, source_target_pairs={{0,4},{4,8},{8,12},{12,16},{16,20},{20,24},{24,28},{28,32},{32,36}... | collective-permute-start | bytes 786440 | tf_op jit(solution)/shard_map/ppermute | solution.py:54
  61.1 1.6 copy-start.1
  62.7 14.1 %copy-start.7 = (bf16[1024,256]{1,0:T(8,128)(2,1)}, bf16[1024,256]{1,0:T(8,128)(2,1)S(1)}, u32[]{:S(2)}) copy-start(bf16[1024,256]{1,0:T(8,128)(2,1)S(1)} %get-tuple-element.46) | copy-start | bytes 1572868
  62.7 14.0 %collective-permute-start = (bf16[1024,256]{1,0:T(8,128)(2,1)S(1)}, bf16[1024,256]{1,0:T(8,128)(2,1)}, u32[]{:S(2)}, u32[]{:S(2)}) collective-permute-start(bf16[1024,256]{1,0:T(8,128)(2,1)S(1)} %get-tuple-element.46), channel_id=1, source_target_pairs={{0,128},{128,0},{1,129},{129,1},{2,130},{130,2},{3,131},{131,3},{4... | collective-permute-start | bytes 1572872 | tf_op jit(solution)/shard_map/ppermute | solution.py:257
  78.1 0.8 copy-start.4
  80.4 1.5 copy-start.6
  81.9 4.0 %copy-start = (bf16[2,4,2,64,4608]{4,3,2,1,0:T(8,128)(2,1)}, bf16[2,4,2,64,4608]{4,3,2,1,0:T(8,128)(2,1)S(1)}, u32[]{:S(2)}) copy-start(bf16[2,4,2,64,4608]{4,3,2,1,0:T(8,128)(2,1)S(1)} %fusion.39) | copy-start | bytes 28311556
  86.8 21.8 %collective-permute-start.4 = (bf16[1,4,2,64,256]{4,3,2,1,0:T(8,128)(2,1)}, bf16[1,4,2,64,256]{4,3,2,1,0:T(8,128)(2,1)}, u32[]{:S(2)}, u32[]{:S(2)}) collective-permute-start(bf16[1,4,2,64,256]{4,3,2,1,0:T(8,128)(2,1)} %bitcast.19), channel_id=1, source_target_pairs={{4,0},{8,4},{12,8},{16,12},{20,16},{24,20},{28,24},{32,28},{36,32}... | collective-permute-start | bytes 786440 | tf_op jit(solution)/shard_map/ppermute | solution.py:55
  102.0 10.6 %collective-permute-start.3 = (bf16[1,4,2,64,256]{4,3,2,1,0:T(8,128)(2,1)}, bf16[1,4,2,64,256]{4,3,2,1,0:T(8,128)(2,1)}, u32[]{:S(2)}, u32[]{:S(2)}) collective-permute-start(bf16[1,4,2,64,256]{4,3,2,1,0:T(8,128)(2,1)} %bitcast.17), channel_id=1, source_target_pairs={{0,4},{4,8},{8,12},{12,16},{16,20},{20,24},{24,28},{28,32},{32,36}... | collective-permute-start | bytes 786440 | tf_op jit(solution)/shard_map/ppermute | solution.py:54
  116.5 2.0 copy-start.3
  121.2 14.3 %copy-start.5 = (bf16[1024,256]{1,0:T(8,128)(2,1)S(1)}, bf16[1024,256]{1,0:T(8,128)(2,1)}, u32[]{:S(2)}) copy-start(bf16[1024,256]{1,0:T(8,128)(2,1)} %copy-done.4) | copy-start | bytes 1572868
  121.2 14.3 %collective-permute-start.5 = (bf16[1024,256]{1,0:T(8,128)(2,1)S(1)}, bf16[1024,256]{1,0:T(8,128)(2,1)S(1)}, u32[]{:S(2)}, u32[]{:S(2)}) collective-permute-start(bf16[1024,256]{1,0:T(8,128)(2,1)S(1)} %convolution_convert_fusion), channel_id=1, source_target_pairs={{128,0},{129,1},{130,2},{131,3},{132,4},{133,5},{134,6},{135,7},{1... | collective-permute-start | bytes 1572872 | tf_op jit(solution)/shard_map/ppermute | solution.py:272

commit v3 on v2

v3 whole, which is shorter than its diff:
```python
import math

import jax
import jax.numpy as jnp
from jax import lax
from jax.experimental import pallas as pl
from jax.experimental.pallas import tpu as pltpu
from jax.sharding import Mesh, PartitionSpec as P

COMMIT = 0.5
SLAB = ("zh", "y", "x")
Z = ("zh", "dp")
F32 = jnp.float32
BF16 = jnp.bfloat16
I16 = jnp.int16
TINY = 2.0**-100
STEPS = 32000.0
VMEM_LIMIT = 48 * 1024 * 1024


def silu_slope(pre_act):
    sig = jax.nn.sigmoid(pre_act)
    return sig * (1.0 + pre_act * (1.0 - sig))


def neighbours(lower, upper):
    count = lax.axis_size(SLAB)
    above = lax.ppermute(lower, SLAB, [(i, i + 1) for i in range(count - 1)])
    below = lax.ppermute(upper, SLAB, [(i + 1, i) for i in range(count - 1)])
    return above, below


def exchange(cells, axes):
    return lax.all_to_all(cells, axes, split_axis=0, concat_axis=0, tiled=True)


def coded(values):
    top = jnp.max(jnp.abs(values), axis=tuple(range(values.ndim)), keepdims=True)
    exponent = jnp.ceil(jnp.log2(top + TINY))
    return jnp.round(values * (jnp.exp2(-exponent) * STEPS)), exponent


def decoded_scale(exponents):
    return jnp.exp2(exponents.astype(F32)) * (1.0 / STEPS)


def framed(piece):
    steps, exponent = coded(piece)
    tail = jnp.broadcast_to(exponent, (8, 128))
    return jnp.concatenate([steps, tail], axis=0).astype(I16)


def unframed(rows):
    wide = rows.astype(F32)
    return wide[:-8] * (jnp.exp2(wide[-1:]) * (1.0 / STEPS))


def shifted_columns(block, across, tap):
    if tap == 1:
        return block
    count = block.shape[0]
    wide = block.astype(F32)
    column = lax.broadcasted_iota(jnp.int32, block.shape, 0) % across
    if tap == 0:
        wide = jnp.where(column == 0, 0.0, pltpu.roll(wide, 1, 0))
    else:
        wide = jnp.where(column == across - 1, 0.0, pltpu.roll(wide, count - 1, 0))
    return wide.astype(block.dtype)


def call(body, outs, *args, flops=0, scratch=()):
    size = sum(math.prod(a.shape) * a.dtype.itemsize for a in args) + sum(
        math.prod(o.shape) * o.dtype.itemsize for o in outs
    )
    return pl.pallas_call(
        body,
        in_specs=[pl.BlockSpec(memory_space=pltpu.SMEM)]
        + [pl.BlockSpec(memory_space=pltpu.VMEM)] * (len(args) - 1),
        out_specs=[pl.BlockSpec(memory_space=pltpu.VMEM)] * len(outs),
        out_shape=list(outs),
        scratch_shapes=list(scratch),
        cost_estimate=pl.CostEstimate(flops=flops, bytes_accessed=size, transcendentals=0),
        compiler_params=pltpu.CompilerParams(vmem_limit_bytes=VMEM_LIMIT),
    )(*args)


def shift_source(section, pair, other, own, above, below, across):
    frames, rows, count, channels = own.shape

    def body(section_ref, pair_ref, other_ref, own_ref, above_ref, below_ref, out_ref):
        def write(frame, row, block):
            for tap in range(3):
                out_ref[tap, frame, row] = shifted_columns(block, across, tap)

        @pl.when(section_ref[0] == 0)
        def _():
            for frame in range(frames):
                write(frame, 0, above_ref[frame])
                for row in range(rows):
                    write(frame, row + 1, own_ref[frame, row])
                write(frame, rows + 1, below_ref[frame])

        @pl.when(section_ref[0] == 1)
        def _():
            for frame in range(frames):
                for row in range(2):
                    write(frame, row, other_ref[frame, row])
                    write(frame, row + 2, pair_ref[frame, row])

    out = jax.ShapeDtypeStruct((3, frames, rows + 2, count, channels), BF16)
    return call(body, [out], section, pair, other, own, above, below)[0]


def turn_source(section, source):
    taps, frames, rows, count, channels = source.shape

    def body(section_ref, source_ref, out_ref):
        for tap in range(taps):
            for frame in range(frames):
                for row in range(rows):
                    start = (frame * rows + row) * count
                    out_ref[tap, :, start : start + count] = source_ref[tap, frame, row].T

    out = jax.ShapeDtypeStruct((taps, channels, frames * rows * count), BF16)
    return call(body, [out], section, source)[0]


def tap_index(section_ref, row_tap, column_tap):
    decoder = section_ref[0] == 1
    return jnp.where(decoder, column_tap, row_tap), jnp.where(decoder, row_tap, column_tap)


def convolve(section, source, kernel, cotangent):
    _, frames, rimmed, count, channels = source.shape
    rows = rimmed - 2
    span = rows * count

    def body(section_ref, source_ref, kernel_ref, cot_ref, pre_ref, grad_ref):
        for frame in range(frames):
            acc = jnp.zeros((span, channels), F32)
            for r in range(3):
                for q in range(3):
                    i, j = tap_index(section_ref, r, q)
                    for back in range(frame + 1):
                        cells = source_ref[q, frame - back, r : r + rows].reshape(span, channels)
                        acc += jnp.dot(
                            cells, kernel_ref[1 - back, i, j], preferred_element_type=F32
                        )
            pre_ref[frame] = acc
            grad_ref[frame] = (cot_ref[frame].astype(F32) * silu_slope(acc)).astype(BF16)

    shape = (frames, span, channels)
    return call(
        body,
        [jax.ShapeDtypeStruct(shape, F32), jax.ShapeDtypeStruct(shape, BF16)],
        section,
        source,
        kernel,
        cotangent,
        flops=54 * span * channels * channels,
    )


def convolve_back(section, grad, above, below, kernel, across):
    frames, rows, count, channels = grad.shape
    span = rows * count

    def body(section_ref, grad_ref, above_ref, below_ref, kernel_ref, out_ref, shifted):
        for frame in range(frames):
            blocks = [above_ref[frame]] + [grad_ref[frame, r] for r in range(rows)]
            for row, block in enumerate(blocks + [below_ref[frame]]):
                for tap in range(3):
                    shifted[tap, frame, row] = shifted_columns(block, across, tap)
        for frame in range(frames):
            acc = jnp.zeros((span, channels), F32)
            for r in range(3):
                for q in range(3):
                    i, j = tap_index(section_ref, r, q)
                    for ahead in range(frames - frame):
                        cells = shifted[2 - q, frame + ahead, 2 - r : 2 - r + rows]
                        acc += lax.dot_general(
                            cells.reshape(span, channels),
                            kernel_ref[1 - ahead, i, j],
                            (((1,), (1,)), ((), ())),
                            preferred_element_type=F32,
                        )
            out_ref[frame] = acc.astype(BF16).reshape(rows, count, channels)

    return call(
        body,
        [jax.ShapeDtypeStruct(grad.shape, BF16)],
        section,
        grad,
        above,
        below,
        kernel,
        flops=54 * span * channels * channels,
        scratch=[pltpu.VMEM((3, frames, rows + 2, count, channels), BF16)],
    )[0]


def kernel_grads(section, turned, pre_act, dec_grad, returned, pair, other, parts):
    _, channels, _ = turned.shape
    frames, rows, count, _ = returned.shape
    span = rows * count
    size = channels // parts

    def body(
        section_ref, turned_ref, pre_ref, dec_ref, returned_ref, pair_ref, other_ref,
        out_ref, side, grads,
    ):
        @pl.when(section_ref[0] == 0)
        def _():
            for frame in range(frames):
                for row, quant in enumerate((pair_ref[frame, 1], other_ref[frame, 0])):
                    at = slice(row * count, (row + 1) * count)
                    side[frame, at] = (
                        returned_ref[frame, row].astype(F32)
                        + COMMIT * (pre_ref[frame, at] - quant.astype(F32))
                    ).astype(BF16)

        @pl.when(section_ref[0] == 1)
        def _():
            side[...] = dec_ref[...]

        top = jnp.zeros((8, channels), F32)
        for r in range(3):
            for q in range(3):
                i, j = tap_index(section_ref, r, q)
                tap = i * 3 + j
                first = turned_ref[q, :, r * count : r * count + span]
                start = (rows + 2 + r) * count
                second = turned_ref[q, :, start : start + span]
                late = jnp.dot(first, side[1], preferred_element_type=F32)
                same = jnp.dot(first, side[0], preferred_element_type=F32)
                same += jnp.dot(second, side[1], preferred_element_type=F32)
                for at, values in ((tap, late), (9 + tap, same)):
                    grads[at] = values
                    seen = jnp.max(jnp.abs(values).reshape(-1, 8, channels), axis=0)
                    top = jnp.maximum(top, seen)
        exponent = jnp.ceil(jnp.log2(jnp.max(top, axis=(0, 1), keepdims=True) + TINY))
        factor = jnp.exp2(-exponent) * STEPS

        @pl.loop(0, 18)
        def _(tap):
            steps = jnp.round(grads[tap] * factor).astype(I16)
            out_ref[:, tap] = steps.reshape(parts, size, channels)

        tail = jnp.broadcast_to(exponent, (size, channels)).astype(I16)
        for part in range(parts):
            out_ref[part, 18] = tail

    return call(
        body,
        [jax.ShapeDtypeStruct((parts, 19, size, channels), I16)],
        section,
        turned,
        pre_act,
        dec_grad,
        returned,
        pair,
        other,
        flops=54 * span * channels * channels,
        scratch=[
            pltpu.VMEM((frames, span, channels), BF16),
            pltpu.VMEM((18, channels, channels), F32),
        ],
    )[0]


def sum_plane(packed, pieces):
    senders, taps, size, outs = packed.shape
    taps = taps - 1
    half = taps // 2

    def body(packed_ref, framed_ref, total):
        scales = [decoded_scale(packed_ref[s, taps])[:1, :1] for s in range(senders)]
        for tap in range(taps):
            acc = packed_ref[0, tap].astype(F32) * scales[0]
            for s in range(1, senders):
                acc += packed_ref[s, tap].astype(F32) * scales[s]
            total[tap] = acc
        place = 0
        for frame in range(2):
            for oct_ in range(size // 8):
                for lane in range(outs // 128):
                    piece = total[
                        frame * half : (frame + 1) * half,
                        oct_ * 8 : oct_ * 8 + 8,
                        lane * 128 : lane * 128 + 128,
                    ]
                    framed_ref[place] = framed(piece.reshape(half * 8, 128))
                    place += 1

    return pl.pallas_call(
        body,
        out_shape=jax.ShapeDtypeStruct((pieces, half * 8 + 8, 128), I16),
        scratch_shapes=[pltpu.VMEM((taps, size, outs), F32)],
        compiler_params=pltpu.CompilerParams(vmem_limit_bytes=VMEM_LIMIT),
    )(packed)


def sum_line(framed_parts, factor):
    def body(parts_ref, out_ref):
        acc = unframed(parts_ref[0])
        for s in range(1, framed_parts.shape[0]):
            acc += unframed(parts_ref[s])
        result = framed(acc * factor)
        for s in range(framed_parts.shape[0]):
            out_ref[s] = result

    return pl.pallas_call(
        body, out_shape=jax.ShapeDtypeStruct(framed_parts.shape, I16)
    )(framed_parts)


def unpack(plane, channels):
    parts, pieces, rows, _ = plane.shape
    size = channels // parts
    group = 4

    def body(plane_ref, out_ref):
        for part in range(group):
            place = 0
            for frame in range(2):
                for oct_ in range(size // 8):
                    for lane in range(channels // 128):
                        piece = unframed(plane_ref[part, place]).reshape(3, 3, 8, 128)
                        row = part * size + oct_ * 8
                        out_ref[frame, :, :, row : row + 8, lane * 128 : lane * 128 + 128] = piece
                        place += 1

    return pl.pallas_call(
        body,
        grid=(parts // group,),
        in_specs=[pl.BlockSpec((group, pieces, rows, 128), lambda k: (k, 0, 0, 0))],
        out_specs=pl.BlockSpec((2, 3, 3, group * size, channels), lambda k: (0, 0, 0, k, 0)),
        out_shape=jax.ShapeDtypeStruct((2, 3, 3, channels, channels), F32),
        compiler_params=pltpu.CompilerParams(vmem_limit_bytes=VMEM_LIMIT),
    )(plane)


def on_device(fields, kernels, codebook, codes):
    section_id = lax.axis_index("section")
    section = section_id.reshape(1).astype(jnp.int32)
    slab_id = lax.axis_index(SLAB)
    slabs = lax.axis_size(SLAB)
    own_field = fields[0]
    kernel = kernels[0]
    row_count, batch_count, frame_count, across, channels = own_field.shape
    book = codebook.shape[0]
    positions = row_count * batch_count * frame_count * across
    slots = max(16, 2 * positions // slabs)
    cells = (frame_count, row_count, batch_count * across, channels)

    edge = jnp.full((1,) + codes.shape[1:], -1, codes.dtype)
    shifted = jnp.concatenate([edge, codes, edge], axis=0)
    shifted = shifted.reshape(slabs + 1, row_count, batch_count, frame_count, across)
    shifted = jnp.transpose(shifted, (0, 3, 1, 2, 4)).reshape(slabs + 1, positions)
    wanted = lax.dynamic_slice_in_dim(shifted, section_id, slabs, 0)
    owner = jnp.where(wanted >= 0, wanted // book, -1)
    before = (
        lax.broadcasted_iota(jnp.int32, (positions, positions), 0)
        < lax.broadcasted_iota(jnp.int32, (positions, positions), 1)
    ).astype(BF16)

    mine = owner == slab_id
    rank = jnp.dot(mine.astype(BF16), before, preferred_element_type=F32).astype(jnp.int32)
    rank = jnp.where(mine, rank, -1)
    local = wanted - slab_id * book
    slot_ids = lax.broadcasted_iota(jnp.int32, (1, slots, 1), 1)
    asked = jnp.sum(jnp.where(rank[:, None, :] == slot_ids, local[:, None, :], 0), axis=-1)
    picks = (
        asked.reshape(-1, 1) == lax.broadcasted_iota(jnp.int32, (1, book), 1)
    ).astype(BF16)
    words = jnp.dot(picks, codebook, preferred_element_type=F32).astype(BF16)
    words = words.reshape(slabs, slots, channels)

    turned = own_field.reshape(row_count, batch_count, frame_count, slabs, row_count, channels)
    turned = jnp.transpose(turned, (3, 2, 4, 1, 0, 5)).reshape(slabs, -1, channels)
    arrived = exchange(jnp.concatenate([words, turned], axis=1), SLAB)
    looked = arrived[:, :slots].reshape(slabs * slots, channels)
    sent = lax.broadcasted_iota(jnp.int32, (positions, 1), 0)
    group, column = sent // across, sent % across
    sent = (column // row_count) * (positions // slabs) + group * row_count + column % row_count
    sent = (sent == lax.broadcasted_iota(jnp.int32, (1, positions), 1)).astype(BF16)
    cotangent = jnp.dot(
        sent, arrived[:, slots:].reshape(positions, channels), preferred_element_type=F32
    ).astype(BF16)
    cotangent = cotangent.reshape(frame_count, -1, channels)

    own_wanted = lax.dynamic_index_in_dim(wanted, slab_id, 0, keepdims=False)
    own_owner = lax.dynamic_index_in_dim(owner, slab_id, 0, keepdims=False)
    from_each = own_owner[None, :] == lax.broadcasted_iota(jnp.int32, (slabs, 1), 0)
    place = jnp.dot(from_each.astype(BF16), before, preferred_element_type=F32).astype(jnp.int32)
    place = jnp.sum(jnp.where(from_each, place, 0), axis=0)
    place = jnp.where(own_wanted >= 0, own_owner * slots + place, -1)
    gather = (
        place[:, None] == lax.broadcasted_iota(jnp.int32, (1, slabs * slots), 1)
    ).astype(BF16)
    fast = jnp.dot(gather, looked, preferred_element_type=F32).astype(BF16)

    every_owner = jnp.where(shifted >= 0, shifted // book, -1)[:, None, :]
    counts = jnp.sum(
        (every_owner == lax.broadcasted_iota(jnp.int32, (1, slabs, 1), 1)).astype(F32), axis=-1
    )
    crowded = jnp.full((lax.axis_size("dp"), 8, 128), jnp.max(counts) - slots)
    crowded = jnp.max(exchange(crowded, "dp")) > 0

    def whole_book(_):
        every = lax.all_gather(codebook, SLAB, axis=0, tiled=True)
        taken = jnp.take(every, jnp.maximum(own_wanted, 0), axis=0)
        return jnp.where(own_wanted[:, None] >= 0, taken, 0).astype(BF16)

    pair = lax.cond(crowded, whole_book, lambda quick: quick, fast)
    other = lax.ppermute(pair, "section", [(0, 1), (1, 0)])
    pair, other = pair.reshape(cells), other.reshape(cells)
    own = jnp.transpose(own_field, (2, 0, 1, 3, 4)).reshape(cells)
    above, below = neighbours(own[:, -1], own[:, 0])
    source = shift_source(section, pair, other, own, above, below, across)
    pre_act, dec_grad = convolve(section, source, kernel, cotangent)

    shaped = dec_grad.reshape(cells)
    above, below = neighbours(shaped[:, -1], shaped[:, 0])
    source = turn_source(section, source)
    back_dec = convolve_back(section, shaped, above, below, kernel, across)
    returned = lax.ppermute(back_dec, "section", [(1, 0)])

    total = (
        row_count * slabs * across * batch_count * lax.axis_size("dp") * frame_count
    )
    nx, ny, nz = lax.axis_size("x"), lax.axis_size("y"), lax.axis_size(Z)
    packed = kernel_grads(
        section, source, pre_act, dec_grad, returned, pair, other, nx * ny
    )
    plane = exchange(packed, ("y", "x"))
    line = exchange(sum_plane(plane, nz), Z)
    line = exchange(sum_line(line, 1.0 / math.sqrt(total)), Z)
    plane = exchange(jnp.broadcast_to(line[None], (nx * ny,) + line.shape), ("y", "x"))
    return unpack(plane, channels)[None]


def solution(mesh):
    sections, slabs, dps = (mesh.shape[a] for a in ("section", "slab", "dp"))
    nx = 4 if slabs >= 16 else 2
    inner = Mesh(
        mesh.devices.reshape(sections, slabs // (nx * nx), nx, nx, dps),
        ("section", "zh", "y", "x", "dp"),
    )
    placed = (
        P("section", SLAB, "dp", None, None, None),
        P("section", None, None, None, None, None),
        P(SLAB, None),
        P(None, "dp", None, None),
    )
    return jax.shard_map(
        on_device,
        mesh=inner,
        in_specs=placed,
        out_specs=P("section", None, None, None, None, None),
        check_vma=False,
    )
```

time: 296 us -> 252 us (0.85)
  local copies, waits for them, and re-layouts: 34.2 us -> 7.08 us
  matrix products: 20.4 us -> 4.81 us
  waiting for transfers between devices: 23.4 us -> 34.4 us
  other arithmetic: 16 us -> 5.49 us
  blocking collectives: 119 us -> 128 us
  starting transfers between devices: 42.4 us -> 36.7 us
  Pallas kernels: 24 us -> 19.7 us
    dot_general x3 -> x1, matrix products: 15.4 us -> 0.84 us  [on_device(): jnp.dot(sent, arrived[:, slots:].reshape(positions, channels), preferred_...]
    reshape x3 -> x4, local copies, waits for them, and re-layouts: 13.1 us -> 0.5 us  [the longest x1 0.2 us: on_device(): jnp.transpose(turned, (3, 2, 4, 1, 0, 5)).reshape(slabs, -1, channels)]
    all_to_all x4, blocking collectives: 119 us -> 128 us  [exchange(): return lax.all_to_all(cells, axes, split_axis=0, concat_axis=0, tiled=True)]
    convert_element_type x3 -> x0, local copies, waits for them, and re-layouts: 8.47 us -> none  [on_device(): dec_grad = (cotangent.astype(F32) * silu_slope(pre_act)).astype(BF16)]
    all_to_all x2, waiting for transfers between devices: 17.1 us -> 23.4 us  [exchange(): return lax.all_to_all(cells, axes, split_axis=0, concat_axis=0, tiled=True)]
    select_n x4 -> x1, other arithmetic: 5.68 us -> 0.1 us  [on_device(): every_owner = jnp.where(shifted >= 0, shifted // book, -1)[:, None, :]]
    ppermute x2, starting transfers between devices: 17.4 us -> 12.8 us  [neighbours(): below = lax.ppermute(upper, SLAB, [(i + 1, i) for i in range(count - 1)])]
    pallas_call x2 -> x6, Pallas kernels: 21.4 us -> 17.1 us  [the longest x5 14.4 us: call(): pl.pallas_call(body, in_specs=[pl.BlockSpec(memory_space=pltpu.SMEM)] + [...]
  transfers between devices with their start and end apart: 8 -> 8, of which waited for: 3 -> 5; matrix products, arithmetic and copies ran while one was open for 14% -> 3% of each run, Pallas kernels for 0% -> 1%
where the time goes in v3:
time: 252 us
  blocking collectives  128 us (51%)
  starting transfers between devices  36.7 us (15%)
  waiting for transfers between devices  34.4 us (14%)
  Pallas kernels  19.7 us (8%)
  between operations  15 us (6%)
  local copies, waits for them, and re-layouts  7.08 us (3%)
  other arithmetic  5.49 us (2%)
  matrix products  4.81 us (2%)
    all_to_all x4, blocking collectives, exchange(): return lax.all_to_all(cells, axes, split_axis=0, concat_axis=0, tiled=True)  128 us
    all_to_all x2, waiting for transfers between devices, exchange(): return lax.all_to_all(cells, axes, split_axis=0, concat_axis=0, tiled=True)  23.4 us
    all_to_all x2, starting transfers between devices, exchange(): return lax.all_to_all(cells, axes, split_axis=0, concat_axis=0, tiled=True)  17.5 us
    pallas_call x5, Pallas kernels, call(): pl.pallas_call(body, in_specs=[pl.BlockSpec(memory_space=pltpu.SMEM)] + [...  14.4 us
    ppermute x2, starting transfers between devices, neighbours(): below = lax.ppermute(upper, SLAB, [(i + 1, i) for i in range(count - 1)])  12.8 us
    ppermute x2, waiting for transfers between devices, neighbours(): above = lax.ppermute(lower, SLAB, [(i, i + 1) for i in range(count - 1)])  7.93 us
  transfers between devices with their start and end apart: 8, of which 5 were waited for; matrix products, arithmetic and copies ran while one was open for 3% of the time, Pallas kernels for 1%

profile of v3, /device:TPU:2, one launch (start us, length us, event | category | flops | bytes accessed | tf_op | source)
XLA Modules:
  0.0 251.6 jit_solution(2668345266531842395)
XLA Ops:
  6.5 1.1 pad_add_fusion
  7.6 0.1 copy.27
  7.7 0.2 reshape.215
  7.9 0.1 fusion.17
  8.0 0.5 convert_reduce_fusion
  8.5 0.6 reduce_max.18
  9.8 0.6 broadcast_in_dim.80
  10.4 5.9 %all-to-all-start = ((f32[4,8,128]{2,1,0:T(8,128)}), f32[4,8,128]{2,1,0:T(8,128)S(1)}, u32[]{:S(2)}, u32[]{:S(2)}) async-start(f32[4,8,128]{2,1,0:T(8,128)} %broadcast_in_dim.80), calls=%async_computation | async-start | bytes 32768 | tf_op jit(solution)/shard_map/all_to_all | solution.py:34
  16.3 1.2 reshape_squeeze.3
  17.5 0.5 copy.18
  18.1 0.2 reshape.217
  18.3 0.1 fusion.20
  18.4 0.4 fusion.14
  18.8 1.2 select_reduce_fusion
  20.0 0.1 eq.103
  20.1 1.7 fusion.7
  21.8 1.3 pad_maximum_fusion
  23.1 11.6 %all-to-all-start.1 = ((bf16[32,96,256]{2,1,0:T(8,128)(2,1)}), bf16[32,96,256]{2,1,0:T(8,128)(2,1)S(1)}, u32[]{:S(2)}, u32[]{:S(2)}) async-start(bf16[32,96,256]{2,1,0:T(8,128)(2,1)} %pad_maximum_fusion), calls=%async_computation.1 | async-start | bytes 3145728 | tf_op jit(solution)/shard_map/all_to_all | solution.py:34
  34.8 0.4 fusion.15
  35.2 0.6 reduce_max.19
  36.5 23.4 %all-to-all-done.1 = bf16[32,96,256]{2,1,0:T(8,128)(2,1)S(1)} async-done(((bf16[32,96,256]{2,1,0:T(8,128)(2,1)}), bf16[32,96,256]{2,1,0:T(8,128)(2,1)S(1)}, u32[]{:S(2)}, u32[]{:S(2)}) %all-to-all-start.1) | async-done | bytes 1572896 | tf_op jit(solution)/shard_map/all_to_all | solution.py:34
  60.0 1.5 fusion.10
  61.5 0.1 collective-permute-start
  61.7 3.1 %collective-permute-start.1 = (bf16[2,256,256]{2,1,0:T(8,128)(2,1)S(1)}, bf16[2,256,256]{2,1,0:T(8,128)(2,1)S(1)}, u32[]{:S(2)}, u32[]{:S(2)}) collective-permute-start(bf16[2,256,256]{2,1,0:T(8,128)(2,1)S(1)} %get-tuple-element.28), channel_id=1, source_target_pairs={{0,4},{4,8},{8,12},{12,16},{16,20},{20,24},{24,28},{28,32},{32,36}... | collective-permute-start | bytes 786440 | tf_op jit(solution)/shard_map/ppermute | solution.py:28
  64.8 8.8 %collective-permute-start.2 = (bf16[2,256,256]{2,1,0:T(8,128)(2,1)S(1)}, bf16[2,256,256]{2,1,0:T(8,128)(2,1)S(1)}, u32[]{:S(2)}, u32[]{:S(2)}) collective-permute-start(bf16[2,256,256]{2,1,0:T(8,128)(2,1)S(1)} %get-tuple-element.27), channel_id=1, source_target_pairs={{4,0},{8,4},{12,8},{16,12},{20,16},{24,20},{28,24},{32,28},{36,32}... | collective-permute-start | bytes 786440 | tf_op jit(solution)/shard_map/ppermute | solution.py:29
  73.7 0.8 fusion.9
  74.6 3.9 %collective-permute-done.1.above_ref = bf16[2,256,256]{2,1,0:T(8,128)(2,1)S(1)} collective-permute-done((bf16[2,256,256]{2,1,0:T(8,128)(2,1)S(1)}, bf16[2,256,256]{2,1,0:T(8,128)(2,1)S(1)}, u32[]{:S(2)}, u32[]{:S(2)}) %collective-permute-start.1) | collective-permute-done | bytes 262176 | tf_op jit(solution)/shard_map/ppermute | solution.py:28
  78.4 1.2 collective-permute-done.2.below_ref
  79.6 0.5 shard_map.46.source_ref
  80.2 1.7 copy-done.1
  81.8 4.0 %shard_map.48 = (f32[2,512,256]{2,1,0:T(8,128)S(1)}, bf16[2,512,256]{2,1,0:T(8,128)(2,1)S(1)}) custom-call(s32[1]{0:T(128)} %bitcast.2.section_ref, bf16[3,2,4,256,256]{4,3,2,1,0:T(8,128)(2,1)} %copy-done.1, bf16[2,3,3,256,256]{4,3,2,1,0:T(8,128)(2,1)S(1)} %bitcast.43, bf16[2,512,256]{2,1,0:T(8,128)(2,1)S(1)} %bitcast.45), custom_call_target="tpu_custom_call" | custom-call | flops 1811939328 | bytes 7602180 | tf_op jit(solution)/shard_map/pallas_call | solution.py:75
  85.9 1.9 collective-permute-start.3
  87.8 3.9 %collective-permute-start.4 = (bf16[2,256,256]{2,1,0:T(8,128)(2,1)S(1)}, bf16[2,256,256]{2,1,0:T(8,128)(2,1)S(1)}, u32[]{:S(2)}, u32[]{:S(2)}) collective-permute-start(bf16[2,256,256]{2,1,0:T(8,128)(2,1)S(1)} %get-tuple-element.25), channel_id=1, source_target_pairs={{4,0},{8,4},{12,8},{16,12},{20,16},{24,20},{28,24},{32,28},{36,32}... | collective-permute-start | bytes 786440 | tf_op jit(solution)/shard_map/ppermute | solution.py:29
  91.7 4.1 %collective-permute-done.3.above_ref = bf16[2,256,256]{2,1,0:T(8,128)(2,1)S(1)} collective-permute-done((bf16[2,256,256]{2,1,0:T(8,128)(2,1)S(1)}, bf16[2,256,256]{2,1,0:T(8,128)(2,1)S(1)}, u32[]{:S(2)}, u32[]{:S(2)}) %collective-permute-start.3) | collective-permute-done | bytes 262176 | tf_op jit(solution)/shard_map/ppermute | solution.py:28
  95.8 1.8 collective-permute-done.4.below_ref
  97.6 2.0 shard_map.49
  99.7 1.3 collective-permute-start.5
  101.0 2.8 %shard_map.47.turned_ref = bf16[3,256,2048]{2,1,0:T(8,128)(2,1)S(1)} custom-call(s32[1]{0:T(128)} %bitcast.2.section_ref, bf16[3,2,4,256,256]{4,3,2,1,0:T(8,128)(2,1)} %copy-done.1), custom_call_target="tpu_custom_call" | custom-call | bytes 6291460 | tf_op jit(solution)/shard_map/pallas_call | solution.py:75
  103.8 1.7 copy-done
  105.4 5.0 %shard_map.50 = s16[16,19,16,256]{3,2,1,0:T(8,128)(2,1)S(1)} custom-call(s32[1]{0:T(128)} %bitcast.2.section_ref, bf16[3,256,2048]{2,1,0:T(8,128)(2,1)} %copy-done, f32[2,512,256]{2,1,0:T(8,128)S(1)} %get-tuple-element.21.pre_ref, bf16[2,512,256]{2,1,0:T(8,128)(2,1)S(1)} %get-tuple-element.22.dec_ref, ...), custom_call_target="tpu_custom_call" | custom-call | flops 1811939328 | bytes 8781828 | tf_op jit(solution)/shard_map/pallas_call | solution.py:75
  110.5 57.5 %all_to_all.30.packed_ref = s16[16,19,16,256]{3,2,1,0:T(8,128)(2,1)S(1)} all-to-all(s16[16,19,16,256]{3,2,1,0:T(8,128)(2,1)S(1)} %shard_map.50), channel_id=1, replica_groups=mesh['section'=2,'zh'=2,'y'=4,'x'=4,'dp'=4] {'y','x'}, dimensions={0} | all-to-all | bytes 4980736 | tf_op jit(solution)/shard_map/all_to_all | solution.py:34
  168.0 0.8 shard_map.51
  168.8 24.1 %all_to_all.31.parts_ref = s16[8,80,128]{2,1,0:T(8,128)(2,1)} all-to-all(s16[8,80,128]{2,1,0:T(8,128)(2,1)S(1)} %shard_map.51), channel_id=1, replica_groups=mesh['section'=2,'zh'=2,'y'=4,'x'=4,'dp'=4] {'zh','dp'}, dimensions={0} | all-to-all | bytes 327680 | tf_op jit(solution)/shard_map/all_to_all | solution.py:34
  192.9 1.8 shard_map.52
  194.7 12.7 %all_to_all.32 = s16[8,80,128]{2,1,0:T(8,128)(2,1)S(1)} all-to-all(s16[8,80,128]{2,1,0:T(8,128)(2,1)} %shard_map.52), channel_id=1, replica_groups=mesh['section'=2,'zh'=2,'y'=4,'x'=4,'dp'=4] {'zh','dp'}, dimensions={0} | all-to-all | bytes 327680 | tf_op jit(solution)/shard_map/all_to_all | solution.py:34
  207.4 0.5 broadcast_in_dim.84
  207.9 34.1 %all_to_all.33.plane_ref = s16[16,8,80,128]{3,2,1,0:T(8,128)(2,1)S(1)} all-to-all(s16[16,8,80,128]{3,2,1,0:T(8,128)(2,1)S(1)} %broadcast_in_dim.84), channel_id=1, replica_groups=mesh['section'=2,'zh'=2,'y'=4,'x'=4,'dp'=4] {'y','x'}, dimensions={0} | all-to-all | bytes 5242880 | tf_op jit(solution)/shard_map/all_to_all | solution.py:34
  242.0 2.7 %shard_map.53 = f32[2,3,3,256,256]{4,3,2,1,0:T(8,128)} custom-call(s16[16,8,80,128]{3,2,1,0:T(8,128)(2,1)S(1)} %all_to_all.33.plane_ref), custom_call_target="tpu_custom_call" | custom-call | tf_op jit(solution)/shard_map/pallas_call | solution.py:333
  (24 shorter events, 0.4 us)
Async XLA Ops:
  7.7 12.4 %copy-start.4 = (bf16[1024,256]{1,0:T(8,128)(2,1)S(1)}, bf16[1024,256]{1,0:T(8,128)(2,1)}, u32[]{:S(2)}) copy-start(bf16[1024,256]{1,0:T(8,128)(2,1)} %param.8) | copy-start | bytes 1572868
  10.4 12.6 %all-to-all-start = ((f32[4,8,128]{2,1,0:T(8,128)}), f32[4,8,128]{2,1,0:T(8,128)S(1)}, u32[]{:S(2)}, u32[]{:S(2)}) async-start(f32[4,8,128]{2,1,0:T(8,128)} %broadcast_in_dim.80), calls=%async_computation | async-start | bytes 32768 | tf_op jit(solution)/shard_map/all_to_all | solution.py:34
  21.8 12.9 %copy-start.3 = (bf16[1,2,4,2,64,256]{5,4,3,2,1,0:T(8,128)(2,1)S(1)}, bf16[1,2,4,2,64,256]{5,4,3,2,1,0:T(8,128)(2,1)}, u32[]{:S(2)}) copy-start(bf16[1,2,4,2,64,256]{5,4,3,2,1,0:T(8,128)(2,1)} %param.6) | copy-start | bytes 1572868
  23.1 36.8 %all-to-all-start.1 = ((bf16[32,96,256]{2,1,0:T(8,128)(2,1)}), bf16[32,96,256]{2,1,0:T(8,128)(2,1)S(1)}, u32[]{:S(2)}, u32[]{:S(2)}) async-start(bf16[32,96,256]{2,1,0:T(8,128)(2,1)} %pad_maximum_fusion), calls=%async_computation.1 | async-start | bytes 3145728 | tf_op jit(solution)/shard_map/all_to_all | solution.py:34
  61.5 18.1 %collective-permute-start = (bf16[1024,256]{1,0:T(8,128)(2,1)S(1)}, bf16[1024,256]{1,0:T(8,128)(2,1)S(1)}, u32[]{:S(2)}, u32[]{:S(2)}) collective-permute-start(bf16[1024,256]{1,0:T(8,128)(2,1)S(1)} %get-tuple-element.20), channel_id=1, source_target_pairs={{0,128},{128,0},{1,129},{129,1},{2,130},{130,2},{3,131},{131,3},{4... | collective-permute-start | bytes 1572872 | tf_op jit(solution)/shard_map/ppermute | solution.py:416
  61.7 16.8 %collective-permute-start.1 = (bf16[2,256,256]{2,1,0:T(8,128)(2,1)S(1)}, bf16[2,256,256]{2,1,0:T(8,128)(2,1)S(1)}, u32[]{:S(2)}, u32[]{:S(2)}) collective-permute-start(bf16[2,256,256]{2,1,0:T(8,128)(2,1)S(1)} %get-tuple-element.28), channel_id=1, source_target_pairs={{0,4},{4,8},{8,12},{12,16},{16,20},{20,24},{24,28},{28,32},{32,36}... | collective-permute-start | bytes 786440 | tf_op jit(solution)/shard_map/ppermute | solution.py:28
  64.8 14.9 %collective-permute-start.2 = (bf16[2,256,256]{2,1,0:T(8,128)(2,1)S(1)}, bf16[2,256,256]{2,1,0:T(8,128)(2,1)S(1)}, u32[]{:S(2)}, u32[]{:S(2)}) collective-permute-start(bf16[2,256,256]{2,1,0:T(8,128)(2,1)S(1)} %get-tuple-element.27), channel_id=1, source_target_pairs={{4,0},{8,4},{12,8},{16,12},{20,16},{24,20},{28,24},{32,28},{36,32}... | collective-permute-start | bytes 786440 | tf_op jit(solution)/shard_map/ppermute | solution.py:29
  74.6 7.3 %copy-start.2 = (bf16[1,2,3,3,256,256]{5,4,3,2,1,0:T(8,128)(2,1)S(1)}, bf16[1,2,3,3,256,256]{5,4,3,2,1,0:T(8,128)(2,1)}, u32[]{:S(2)}) copy-start(bf16[1,2,3,3,256,256]{5,4,3,2,1,0:T(8,128)(2,1)} %param.7) | copy-start | bytes 7077892
  80.2 1.7 copy-start.1
  85.9 9.9 %collective-permute-start.3 = (bf16[2,256,256]{2,1,0:T(8,128)(2,1)S(1)}, bf16[2,256,256]{2,1,0:T(8,128)(2,1)S(1)}, u32[]{:S(2)}, u32[]{:S(2)}) collective-permute-start(bf16[2,256,256]{2,1,0:T(8,128)(2,1)S(1)} %get-tuple-element.26), channel_id=1, source_target_pairs={{0,4},{4,8},{8,12},{12,16},{16,20},{20,24},{24,28},{28,32},{32,36}... | collective-permute-start | bytes 786440 | tf_op jit(solution)/shard_map/ppermute | solution.py:28
  87.8 9.8 %collective-permute-start.4 = (bf16[2,256,256]{2,1,0:T(8,128)(2,1)S(1)}, bf16[2,256,256]{2,1,0:T(8,128)(2,1)S(1)}, u32[]{:S(2)}, u32[]{:S(2)}) collective-permute-start(bf16[2,256,256]{2,1,0:T(8,128)(2,1)S(1)} %get-tuple-element.25), channel_id=1, source_target_pairs={{4,0},{8,4},{12,8},{16,12},{20,16},{24,20},{28,24},{32,28},{36,32}... | collective-permute-start | bytes 786440 | tf_op jit(solution)/shard_map/ppermute | solution.py:29
  99.7 5.8 %collective-permute-start.5 = (bf16[2,2,256,256]{3,2,1,0:T(8,128)(2,1)S(1)}, bf16[2,2,256,256]{3,2,1,0:T(8,128)(2,1)S(1)}, u32[]{:S(2)}, u32[]{:S(2)}) collective-permute-start(bf16[2,2,256,256]{3,2,1,0:T(8,128)(2,1)S(1)} %shard_map.49), channel_id=1, source_target_pairs={{128,0},{129,1},{130,2},{131,3},{132,4},{133,5},{134,6},{135,7},{1... | collective-permute-start | bytes 1572872 | tf_op jit(solution)/shard_map/ppermute | solution.py:427
  103.8 1.7 copy-start

commit v4 on v3

--- a/solution.py
+++ b/solution.py
@@ -9,13 +9,14 @@
 
 COMMIT = 0.5
 SLAB = ("zh", "y", "x")
+PLANE = ("y", "x")
 Z = ("zh", "dp")
 F32 = jnp.float32
 BF16 = jnp.bfloat16
 I16 = jnp.int16
 TINY = 2.0**-100
 STEPS = 32000.0
-VMEM_LIMIT = 48 * 1024 * 1024
+VMEM_LIMIT = 24 * 1024 * 1024
 
 
 def silu_slope(pre_act):
@@ -340,83 +341,126 @@
     )(plane)
 
 
+def front(own_field, codebook, codes):
+    section_id = lax.axis_index("section")
+    slab_id = lax.axis_index(SLAB)
+    slabs = lax.axis_size(SLAB)
+    near = lax.axis_index("zh")
+    plane_id = lax.axis_index(PLANE)
+    planes = lax.axis_size(PLANE)
+    halves = slabs // planes
+    row_count, batch_count, frame_count, across, channels = own_field.shape
+    book = codebook.shape[0]
+    positions = row_count * batch_count * frame_count * across
+    mean = positions // planes
+    slots = int(mean + 6 * math.sqrt(mean) + 15) // 16 * 16
+    cells = (frame_count, row_count, batch_count * across, channels)
+
+    half = book // 2
+    got = lax.ppermute(
+        lax.dynamic_slice_in_dim(codebook, section_id * half, half, 0), "zh", [(0, 1), (1, 0)]
+    )
+    table = jnp.concatenate(
+        [codebook, got, lax.ppermute(got, "section", [(0, 1), (1, 0)])], axis=0
+    )
+
+    turned = own_field.reshape(
+        row_count, batch_count, frame_count, halves, planes, row_count, channels
+    )
+    turned = jnp.transpose(turned, (3, 4, 2, 5, 1, 0, 6)).reshape(halves, planes, -1, channels)
+    kept = lax.dynamic_index_in_dim(turned, near, 0, keepdims=False)
+    passed = lax.dynamic_index_in_dim(turned, 1 - near, 0, keepdims=False)
+    passed = lax.ppermute(passed, ("section", "zh"), [(2, 3), (3, 2)])
+
+    own = jnp.transpose(own_field, (2, 0, 1, 3, 4)).reshape(cells)
+    above, below = neighbours(own[:, -1], own[:, 0])
+
+    edge = jnp.full((1,) + codes.shape[1:], -1, codes.dtype)
+    shifted = jnp.concatenate([edge, codes, edge], axis=0)
+    shifted = shifted.reshape(slabs + 1, row_count, batch_count, frame_count, across)
+    shifted = jnp.transpose(shifted, (0, 3, 1, 2, 4)).reshape(slabs + 1, positions)
+    holder = jnp.where(shifted >= 0, shifted // book % planes, -1)
+
+    counts = jnp.sum(
+        (holder[:, None, :] == lax.broadcasted_iota(jnp.int32, (1, planes, 1), 1)).astype(F32), axis=-1
+    )
+    crowded = jnp.full((lax.axis_size("dp"), 8, 128), jnp.max(counts) - slots)
+    crowded = exchange(crowded, "dp")
+
+    before = (
+        lax.broadcasted_iota(jnp.int32, (positions, positions), 0)
+        < lax.broadcasted_iota(jnp.int32, (positions, positions), 1)
+    ).astype(BF16)
+
+    start = near * planes + section_id
+    wanted = lax.dynamic_slice_in_dim(shifted, start, planes, 0)
+    mine = lax.dynamic_slice_in_dim(holder, start, planes, 0) == plane_id
+    rank = jnp.dot(mine.astype(BF16), before, preferred_element_type=F32).astype(jnp.int32)
+    rank = jnp.where(mine, rank, -1)
+    within = wanted % book
+    far = book + jnp.where(within // half == section_id, 0, half) + within % half
+    local = jnp.where(wanted // book == slab_id, within, far)
+    slot_ids = lax.broadcasted_iota(jnp.int32, (1, slots, 1), 1)
+    asked = jnp.sum(jnp.where(rank[:, None, :] == slot_ids, local[:, None, :], 0), axis=-1)
+    picks = (
+        asked.reshape(-1, 1) == lax.broadcasted_iota(jnp.int32, (1, 2 * book), 1)
+    ).astype(BF16)
+    table, passed, above, below, crowded = lax.optimization_barrier(
+        (table, passed, above, below, crowded)
+    )
+    words = jnp.dot(picks, table, preferred_element_type=F32).astype(BF16)
+    words = words.reshape(planes, slots, channels)
+
+    arrived = exchange(jnp.concatenate([words, kept, passed], axis=1), PLANE)
+    looked = arrived[:, :slots].reshape(planes * slots, channels)
+
+    place = lax.broadcasted_iota(jnp.int32, (positions, 1), 0)
+    group, column = place // across, place % across
+    source = column // row_count
+    share = positions // slabs
+    place = (source % planes) * (halves * share) + jnp.where(source // planes == near, 0, share)
+    place = place + group * row_count + column % row_count
+    sent = (place == lax.broadcasted_iota(jnp.int32, (1, positions), 1)).astype(BF16)
+    cotangent = jnp.dot(
+        sent, arrived[:, slots:].reshape(positions, channels), preferred_element_type=F32
+    ).astype(BF16)
+
+    own_wanted = lax.dynamic_index_in_dim(shifted, slab_id + section_id, 0, keepdims=False)
+    own_holder = lax.dynamic_index_in_dim(holder, slab_id + section_id, 0, keepdims=False)
+    from_each = own_holder[None, :] == lax.broadcasted_iota(jnp.int32, (planes, 1), 0)
+    order = jnp.dot(from_each.astype(BF16), before, preferred_element_type=F32).astype(jnp.int32)
+    order = jnp.sum(jnp.where(from_each, order, 0), axis=0)
+    order = jnp.where(own_wanted >= 0, own_holder * slots + order, -1)
+    gather = (
+        order[:, None] == lax.broadcasted_iota(jnp.int32, (1, planes * slots), 1)
+    ).astype(BF16)
+    fast = jnp.dot(gather, looked, preferred_element_type=F32).astype(BF16)
+
+    def whole_book(_):
+        every = lax.all_gather(codebook, SLAB, axis=0, tiled=True)
+        taken = jnp.take(every, jnp.maximum(own_wanted, 0), axis=0)
+        return jnp.where(own_wanted[:, None] >= 0, taken, 0).astype(BF16)
+
+    pair = lax.cond(jnp.max(crowded) > 0, whole_book, lambda quick: quick, fast)
+    other = lax.ppermute(pair, "section", [(0, 1), (1, 0)])
+    return (
+        pair.reshape(cells),
+        other.reshape(cells),
+        cotangent.reshape(frame_count, -1, channels),
+        own,
+        above,
+        below,
+    )
+
+
 def on_device(fields, kernels, codebook, codes):
-    section_id = lax.axis_index("section")
-    section = section_id.reshape(1).astype(jnp.int32)
-    slab_id = lax.axis_index(SLAB)
+    section = lax.axis_index("section").reshape(1).astype(jnp.int32)
     slabs = lax.axis_size(SLAB)
     own_field = fields[0]
     kernel = kernels[0]
     row_count, batch_count, frame_count, across, channels = own_field.shape
-    book = codebook.shape[0]
-    positions = row_count * batch_count * frame_count * across
-    slots = max(16, 2 * positions // slabs)
     cells = (frame_count, row_count, batch_count * across, channels)
-
-    edge = jnp.full((1,) + codes.shape[1:], -1, codes.dtype)
-    shifted = jnp.concatenate([edge, codes, edge], axis=0)
-    shifted = shifted.reshape(slabs + 1, row_count, batch_count, frame_count, across)
-    shifted = jnp.transpose(shifted, (0, 3, 1, 2, 4)).reshape(slabs + 1, positions)
-    wanted = lax.dynamic_slice_in_dim(shifted, section_id, slabs, 0)
-    owner = jnp.where(wanted >= 0, wanted // book, -1)
-    before = (
-        lax.broadcasted_iota(jnp.int32, (positions, positions), 0)
-        < lax.broadcasted_iota(jnp.int32, (positions, positions), 1)
-    ).astype(BF16)
-
-    mine = owner == slab_id
-    rank = jnp.dot(mine.astype(BF16), before, preferred_element_type=F32).astype(jnp.int32)
-    rank = jnp.where(mine, rank, -1)
-    local = wanted - slab_id * book
-    slot_ids = lax.broadcasted_iota(jnp.int32, (1, slots, 1), 1)
-    asked = jnp.sum(jnp.where(rank[:, None, :] == slot_ids, local[:, None, :], 0), axis=-1)
-    picks = (
-        asked.reshape(-1, 1) == lax.broadcasted_iota(jnp.int32, (1, book), 1)
-    ).astype(BF16)
-    words = jnp.dot(picks, codebook, preferred_element_type=F32).astype(BF16)
-    words = words.reshape(slabs, slots, channels)
-
-    turned = own_field.reshape(row_count, batch_count, frame_count, slabs, row_count, channels)
-    turned = jnp.transpose(turned, (3, 2, 4, 1, 0, 5)).reshape(slabs, -1, channels)
-    arrived = exchange(jnp.concatenate([words, turned], axis=1), SLAB)
-    looked = arrived[:, :slots].reshape(slabs * slots, channels)
-    sent = lax.broadcasted_iota(jnp.int32, (positions, 1), 0)
-    group, column = sent // across, sent % across
-    sent = (column // row_count) * (positions // slabs) + group * row_count + column % row_count
-    sent = (sent == lax.broadcasted_iota(jnp.int32, (1, positions), 1)).astype(BF16)
-    cotangent = jnp.dot(
-        sent, arrived[:, slots:].reshape(positions, channels), preferred_element_type=F32
-    ).astype(BF16)
-    cotangent = cotangent.reshape(frame_count, -1, channels)
-
-    own_wanted = lax.dynamic_index_in_dim(wanted, slab_id, 0, keepdims=False)
-    own_owner = lax.dynamic_index_in_dim(owner, slab_id, 0, keepdims=False)
-    from_each = own_owner[None, :] == lax.broadcasted_iota(jnp.int32, (slabs, 1), 0)
-    place = jnp.dot(from_each.astype(BF16), before, preferred_element_type=F32).astype(jnp.int32)
-    place = jnp.sum(jnp.where(from_each, place, 0), axis=0)
-    place = jnp.where(own_wanted >= 0, own_owner * slots + place, -1)
-    gather = (
-        place[:, None] == lax.broadcasted_iota(jnp.int32, (1, slabs * slots), 1)
-    ).astype(BF16)
-    fast = jnp.dot(gather, looked, preferred_element_type=F32).astype(BF16)
-
-    every_owner = jnp.where(shifted >= 0, shifted // book, -1)[:, None, :]
-    counts = jnp.sum(
-        (every_owner == lax.broadcasted_iota(jnp.int32, (1, slabs, 1), 1)).astype(F32), axis=-1
-    )
-    crowded = jnp.full((lax.axis_size("dp"), 8, 128), jnp.max(counts) - slots)
-    crowded = jnp.max(exchange(crowded, "dp")) > 0
-
-    def whole_book(_):
-        every = lax.all_gather(codebook, SLAB, axis=0, tiled=True)
-        taken = jnp.take(every, jnp.maximum(own_wanted, 0), axis=0)
-        return jnp.where(own_wanted[:, None] >= 0, taken, 0).astype(BF16)
-
-    pair = lax.cond(crowded, whole_book, lambda quick: quick, fast)
-    other = lax.ppermute(pair, "section", [(0, 1), (1, 0)])
-    pair, other = pair.reshape(cells), other.reshape(cells)
-    own = jnp.transpose(own_field, (2, 0, 1, 3, 4)).reshape(cells)
-    above, below = neighbours(own[:, -1], own[:, 0])
+    pair, other, cotangent, own, above, below = front(own_field, codebook, codes)
     source = shift_source(section, pair, other, own, above, below, across)
     pre_act, dec_grad = convolve(section, source, kernel, cotangent)
 
@@ -433,10 +477,10 @@
     packed = kernel_grads(
         section, source, pre_act, dec_grad, returned, pair, other, nx * ny
     )
-    plane = exchange(packed, ("y", "x"))
+    plane = exchange(packed, PLANE)
     line = exchange(sum_plane(plane, nz), Z)
     line = exchange(sum_line(line, 1.0 / math.sqrt(total)), Z)
-    plane = exchange(jnp.broadcast_to(line[None], (nx * ny,) + line.shape), ("y", "x"))
+    plane = exchange(jnp.broadcast_to(line[None], (nx * ny,) + line.shape), PLANE)
     return unpack(plane, channels)[None]
 
 

time: 252 us -> 238 us (0.944)
  blocking collectives: 128 us -> 117 us
  starting transfers between devices: 36.7 us -> 44.3 us
  waiting for transfers between devices: 34.4 us -> 28.6 us
  Pallas kernels: 19.7 us -> 14 us
    all_to_all x4, blocking collectives: 128 us -> 117 us  [exchange(): return lax.all_to_all(cells, axes, split_axis=0, concat_axis=0, tiled=True)]
    ppermute x1 -> x4, starting transfers between devices: 0.09 us -> 8.49 us  [the longest x1 4.55 us: front(): lax.ppermute(lax.dynamic_slice_in_dim(codebook, section_id * half, half,...]
    ppermute x2, starting transfers between devices: 12.8 us -> 6.68 us  [neighbours(): below = lax.ppermute(upper, SLAB, [(i + 1, i) for i in range(count - 1)])]
    all_to_all x2, waiting for transfers between devices: 23.4 us -> 17.7 us  [exchange(): return lax.all_to_all(cells, axes, split_axis=0, concat_axis=0, tiled=True)]
    pallas_call x5, Pallas kernels: 14.4 us -> 8.7 us  [call(): pl.pallas_call(body, in_specs=[pl.BlockSpec(memory_space=pltpu.SMEM)] + [...]
    all_to_all x2, starting transfers between devices: 17.5 us -> 22.5 us  [exchange(): return lax.all_to_all(cells, axes, split_axis=0, concat_axis=0, tiled=True)]
    ppermute x2, waiting for transfers between devices: 7.93 us -> 4.29 us  [neighbours(): above = lax.ppermute(lower, SLAB, [(i, i + 1) for i in range(count - 1)])]
  transfers between devices with their start and end apart: 8 -> 11, of which waited for: 5 -> 7; matrix products, arithmetic and copies ran while one was open for 3% -> 3% of each run, Pallas kernels for 1% -> 0%
where the time goes in v4:
time: 238 us
  blocking collectives  117 us (49%)
  starting transfers between devices  44.3 us (19%)
  waiting for transfers between devices  28.6 us (12%)
  between operations  14.9 us (6%)
  Pallas kernels  14 us (6%)
  other arithmetic  7.15 us (3%)
  matrix products  5.88 us (2%)
  local copies, waits for them, and re-layouts  5.64 us (2%)
    all_to_all x4, blocking collectives, exchange(): return lax.all_to_all(cells, axes, split_axis=0, concat_axis=0, tiled=True)  117 us
    all_to_all x2, starting transfers between devices, exchange(): return lax.all_to_all(cells, axes, split_axis=0, concat_axis=0, tiled=True)  22.5 us
    all_to_all x2, waiting for transfers between devices, exchange(): return lax.all_to_all(cells, axes, split_axis=0, concat_axis=0, tiled=True)  17.7 us
    pallas_call x5, Pallas kernels, call(): pl.pallas_call(body, in_specs=[pl.BlockSpec(memory_space=pltpu.SMEM)] + [...  8.7 us
    ppermute x2, starting transfers between devices, neighbours(): below = lax.ppermute(upper, SLAB, [(i + 1, i) for i in range(count - 1)])  6.68 us
    ppermute x2, starting transfers between devices, neighbours(): above = lax.ppermute(lower, SLAB, [(i, i + 1) for i in range(count - 1)])  5.32 us
  transfers between devices with their start and end apart: 11, of which 7 were waited for; matrix products, arithmetic and copies ran while one was open for 3% of the time, Pallas kernels for 0%

profile of v4, /device:TPU:2, one launch (start us, length us, event | category | flops | bytes accessed | tf_op | source)
XLA Modules:
  0.0 237.7 jit_solution(2022914248658089426)
XLA Ops:
  6.5 1.1 pad_add_fusion
  8.4 0.6 reduce_max.18
  9.7 0.6 broadcast_in_dim.93
  10.3 5.9 %all-to-all-start = ((f32[4,8,128]{2,1,0:T(8,128)}), f32[4,8,128]{2,1,0:T(8,128)S(1)}, u32[]{:S(2)}, u32[]{:S(2)}) async-start(f32[4,8,128]{2,1,0:T(8,128)} %broadcast_in_dim.93), calls=%async_computation | async-start | bytes 32768 | tf_op jit(solution)/shard_map/all_to_all | solution.py:35
  16.2 1.7 constant_dynamic-slice_fusion.4
  17.8 4.6 %collective-permute-start = (bf16[512,256]{1,0:T(8,128)(2,1)}, bf16[512,256]{1,0:T(8,128)(2,1)}, u32[]{:S(2)}, u32[]{:S(2)}) collective-permute-start(bf16[512,256]{1,0:T(8,128)(2,1)} %constant_dynamic-slice_fusion.4), channel_id=1, source_target_pairs={{0,64},{64,0},{1,65},{65,1},{2,66},{66,2},{3,67},{67,3},{4,68},{68... | collective-permute-start | bytes 786440 | tf_op jit(solution)/shard_map/ppermute | solution.py:360
  22.4 0.8 slice_bitcast_fusion.2
  23.3 2.6 %collective-permute-start.4 = (bf16[2,256,256]{2,1,0:T(8,128)(2,1)}, bf16[2,256,256]{2,1,0:T(8,128)(2,1)S(1)}, u32[]{:S(2)}, u32[]{:S(2)}) collective-permute-start(bf16[2,256,256]{2,1,0:T(8,128)(2,1)} %get-tuple-element.39), channel_id=1, source_target_pairs={{4,0},{8,4},{12,8},{16,12},{20,16},{24,20},{28,24},{32,28},{36,32}... | collective-permute-start | bytes 786440 | tf_op jit(solution)/shard_map/ppermute | solution.py:30
  25.8 3.4 %collective-permute-start.3 = (bf16[2,256,256]{2,1,0:T(8,128)(2,1)}, bf16[2,256,256]{2,1,0:T(8,128)(2,1)S(1)}, u32[]{:S(2)}, u32[]{:S(2)}) collective-permute-start(bf16[2,256,256]{2,1,0:T(8,128)(2,1)} %get-tuple-element.40), channel_id=1, source_target_pairs={{0,4},{4,8},{8,12},{12,16},{16,20},{20,24},{24,28},{28,32},{32,36}... | collective-permute-start | bytes 786440 | tf_op jit(solution)/shard_map/ppermute | solution.py:29
  29.3 0.5 copy.23
  30.0 1.4 collective-permute-start.2
  31.4 0.3 fusion.14
  31.9 0.5 collective-permute-start.1
  32.4 1.0 select_reduce_fusion
  33.5 0.4 collective-permute-done.1
  33.9 1.1 pad_maximum_fusion.1
  35.0 0.4 collective-permute-done.3.above_ref
  35.4 3.0 %fusion.7 = bf16[1792,256]{1,0:T(8,128)(2,1)S(1)} fusion(bf16[2048,256]{1,0:T(8,128)(2,1)S(1)} %pad_maximum_fusion.1, s32[1792]{0:T(1024)S(1)} %eq.136), kind=kOutput, calls=%fused_computation.19 | convolution fusion | flops 1883176960 | bytes 1973248 | tf_op jit(solution)/shard_map/dot_general | solution.py:411
  38.4 2.1 pad_maximum_fusion
  40.6 16.6 %all-to-all-start.1 = ((bf16[16,176,256]{2,1,0:T(8,128)(2,1)}), bf16[16,176,256]{2,1,0:T(8,128)(2,1)S(1)}, u32[]{:S(2)}, u32[]{:S(2)}) async-start(bf16[16,176,256]{2,1,0:T(8,128)(2,1)} %pad_maximum_fusion), calls=%async_computation.1 | async-start | bytes 2883584 | tf_op jit(solution)/shard_map/all_to_all | solution.py:35
  57.2 0.3 fusion.15
  57.5 0.6 reduce_max.19
  58.7 17.7 %all-to-all-done.1 = bf16[16,176,256]{2,1,0:T(8,128)(2,1)S(1)} async-done(((bf16[16,176,256]{2,1,0:T(8,128)(2,1)}), bf16[16,176,256]{2,1,0:T(8,128)(2,1)S(1)}, u32[]{:S(2)}, u32[]{:S(2)}) %all-to-all-start.1) | async-done | bytes 1441824 | tf_op jit(solution)/shard_map/all_to_all | solution.py:35
  76.5 1.4 fusion.10
  77.9 0.3 conditional.1
  78.2 2.1 collective-permute-start.5
  80.4 0.8 fusion.9
  81.2 0.6 collective-permute-done.5
  81.8 0.5 shard_map.46.source_ref
  82.3 0.6 copy-done
  82.9 2.1 shard_map.48
  85.0 4.1 %collective-permute-start.7 = (bf16[2,256,256]{2,1,0:T(8,128)(2,1)S(1)}, bf16[2,256,256]{2,1,0:T(8,128)(2,1)S(1)}, u32[]{:S(2)}, u32[]{:S(2)}) collective-permute-start(bf16[2,256,256]{2,1,0:T(8,128)(2,1)S(1)} %get-tuple-element.35), channel_id=1, source_target_pairs={{4,0},{8,4},{12,8},{16,12},{20,16},{24,20},{28,24},{32,28},{36,32}... | collective-permute-start | bytes 786440 | tf_op jit(solution)/shard_map/ppermute | solution.py:30
  89.2 1.9 collective-permute-start.6
  91.1 4.1 %collective-permute-done.7.below_ref = bf16[2,256,256]{2,1,0:T(8,128)(2,1)S(1)} collective-permute-done((bf16[2,256,256]{2,1,0:T(8,128)(2,1)S(1)}, bf16[2,256,256]{2,1,0:T(8,128)(2,1)S(1)}, u32[]{:S(2)}, u32[]{:S(2)}) %collective-permute-start.7) | collective-permute-done | bytes 262176 | tf_op jit(solution)/shard_map/ppermute | solution.py:30
  95.2 3.9 %collective-permute-done.6.above_ref = bf16[2,256,256]{2,1,0:T(8,128)(2,1)S(1)} collective-permute-done((bf16[2,256,256]{2,1,0:T(8,128)(2,1)S(1)}, bf16[2,256,256]{2,1,0:T(8,128)(2,1)S(1)}, u32[]{:S(2)}, u32[]{:S(2)}) %collective-permute-start.6) | collective-permute-done | bytes 262176 | tf_op jit(solution)/shard_map/ppermute | solution.py:29
  99.0 2.0 shard_map.49
  101.1 1.3 collective-permute-start.8
  102.4 0.9 shard_map.47.turned_ref
  103.3 1.6 collective-permute-done.8.returned_ref
  104.9 3.1 %shard_map.50 = s16[16,19,16,256]{3,2,1,0:T(8,128)(2,1)S(1)} custom-call(s32[1]{0:T(128)} %bitcast.2.section_ref, bf16[3,256,2048]{2,1,0:T(8,128)(2,1)S(1)} %shard_map.47.turned_ref, f32[2,512,256]{2,1,0:T(8,128)S(1)} %get-tuple-element.31.pre_ref, bf16[2,512,256]{2,1,0:T(8,128)(2,1)S(1)} %get-tuple-element.32.dec_ref, ...), custom_call_target="tpu_custom_call" | custom-call | flops 1811939328 | bytes 8781828 | tf_op jit(solution)/shard_map/pallas_call | solution.py:76
  108.0 41.4 %all_to_all.30.packed_ref = s16[16,19,16,256]{3,2,1,0:T(8,128)(2,1)S(1)} all-to-all(s16[16,19,16,256]{3,2,1,0:T(8,128)(2,1)S(1)} %shard_map.50), channel_id=1, replica_groups=mesh['section'=2,'zh'=2,'y'=4,'x'=4,'dp'=4] {'y','x'}, dimensions={0} | all-to-all | bytes 4980736 | tf_op jit(solution)/shard_map/all_to_all | solution.py:35
  149.4 0.8 shard_map.51
  150.2 29.1 %all_to_all.31.parts_ref = s16[8,80,128]{2,1,0:T(8,128)(2,1)} all-to-all(s16[8,80,128]{2,1,0:T(8,128)(2,1)S(1)} %shard_map.51), channel_id=1, replica_groups=mesh['section'=2,'zh'=2,'y'=4,'x'=4,'dp'=4] {'zh','dp'}, dimensions={0} | all-to-all | bytes 327680 | tf_op jit(solution)/shard_map/all_to_all | solution.py:35
  179.3 1.8 shard_map.52
  181.1 12.7 %all_to_all.32 = s16[8,80,128]{2,1,0:T(8,128)(2,1)S(1)} all-to-all(s16[8,80,128]{2,1,0:T(8,128)(2,1)} %shard_map.52), channel_id=1, replica_groups=mesh['section'=2,'zh'=2,'y'=4,'x'=4,'dp'=4] {'zh','dp'}, dimensions={0} | all-to-all | bytes 327680 | tf_op jit(solution)/shard_map/all_to_all | solution.py:35
  193.8 0.5 broadcast_in_dim.100
  194.3 33.9 %all_to_all.33.plane_ref = s16[16,8,80,128]{3,2,1,0:T(8,128)(2,1)S(1)} all-to-all(s16[16,8,80,128]{3,2,1,0:T(8,128)(2,1)S(1)} %broadcast_in_dim.100), channel_id=1, replica_groups=mesh['section'=2,'zh'=2,'y'=4,'x'=4,'dp'=4] {'y','x'}, dimensions={0} | all-to-all | bytes 5242880 | tf_op jit(solution)/shard_map/all_to_all | solution.py:35
  228.2 2.7 %shard_map.53 = f32[2,3,3,256,256]{4,3,2,1,0:T(8,128)} custom-call(s16[16,8,80,128]{3,2,1,0:T(8,128)(2,1)S(1)} %all_to_all.33.plane_ref), custom_call_target="tpu_custom_call" | custom-call | tf_op jit(solution)/shard_map/pallas_call | solution.py:334
  (29 shorter events, 1.5 us)
Async XLA Ops:
  6.5 15.9 %copy-start.3 = (bf16[1,2,4,2,64,256]{5,4,3,2,1,0:T(8,128)(2,1)S(1)}, bf16[1,2,4,2,64,256]{5,4,3,2,1,0:T(8,128)(2,1)}, u32[]{:S(2)}) copy-start(bf16[1,2,4,2,64,256]{5,4,3,2,1,0:T(8,128)(2,1)} %param.6) | copy-start | bytes 1572868
  10.3 24.7 %all-to-all-start = ((f32[4,8,128]{2,1,0:T(8,128)}), f32[4,8,128]{2,1,0:T(8,128)S(1)}, u32[]{:S(2)}, u32[]{:S(2)}) async-start(f32[4,8,128]{2,1,0:T(8,128)} %broadcast_in_dim.93), calls=%async_computation | async-start | bytes 32768 | tf_op jit(solution)/shard_map/all_to_all | solution.py:35
  17.8 14.1 %collective-permute-start = (bf16[512,256]{1,0:T(8,128)(2,1)}, bf16[512,256]{1,0:T(8,128)(2,1)}, u32[]{:S(2)}, u32[]{:S(2)}) collective-permute-start(bf16[512,256]{1,0:T(8,128)(2,1)} %constant_dynamic-slice_fusion.4), channel_id=1, source_target_pairs={{0,64},{64,0},{1,65},{65,1},{2,66},{66,2},{3,67},{67,3},{4,68},{68... | collective-permute-start | bytes 786440 | tf_op jit(solution)/shard_map/ppermute | solution.py:360
  23.3 10.6 %copy-start.1 = (bf16[1024,256]{1,0:T(8,128)(2,1)S(1)}, bf16[1024,256]{1,0:T(8,128)(2,1)}, u32[]{:S(2)}) copy-start(bf16[1024,256]{1,0:T(8,128)(2,1)} %param.8) | copy-start | bytes 1572868
  23.3 11.7 %collective-permute-start.4 = (bf16[2,256,256]{2,1,0:T(8,128)(2,1)}, bf16[2,256,256]{2,1,0:T(8,128)(2,1)S(1)}, u32[]{:S(2)}, u32[]{:S(2)}) collective-permute-start(bf16[2,256,256]{2,1,0:T(8,128)(2,1)} %get-tuple-element.39), channel_id=1, source_target_pairs={{4,0},{8,4},{12,8},{16,12},{20,16},{24,20},{28,24},{32,28},{36,32}... | collective-permute-start | bytes 786440 | tf_op jit(solution)/shard_map/ppermute | solution.py:30
  25.8 9.6 %collective-permute-start.3 = (bf16[2,256,256]{2,1,0:T(8,128)(2,1)}, bf16[2,256,256]{2,1,0:T(8,128)(2,1)S(1)}, u32[]{:S(2)}, u32[]{:S(2)}) collective-permute-start(bf16[2,256,256]{2,1,0:T(8,128)(2,1)} %get-tuple-element.40), channel_id=1, source_target_pairs={{0,4},{4,8},{8,12},{12,16},{16,20},{20,24},{24,28},{28,32},{32,36}... | collective-permute-start | bytes 786440 | tf_op jit(solution)/shard_map/ppermute | solution.py:29
  30.0 5.4 %collective-permute-start.2 = (bf16[16,32,256]{2,1,0:T(8,128)(2,1)S(1)}, bf16[16,32,256]{2,1,0:T(8,128)(2,1)}, u32[]{:S(2)}, u32[]{:S(2)}) collective-permute-start(bf16[16,32,256]{2,1,0:T(8,128)(2,1)S(1)} %bitcast.66), channel_id=1, source_target_pairs={{128,192},{192,128},{129,193},{193,129},{130,194},{194,130},{131,1... | collective-permute-start | bytes 786440 | tf_op jit(solution)/shard_map/ppermute | solution.py:373
  31.9 2.0 collective-permute-start.1
  40.6 35.8 %all-to-all-start.1 = ((bf16[16,176,256]{2,1,0:T(8,128)(2,1)}), bf16[16,176,256]{2,1,0:T(8,128)(2,1)S(1)}, u32[]{:S(2)}, u32[]{:S(2)}) async-start(bf16[16,176,256]{2,1,0:T(8,128)(2,1)} %pad_maximum_fusion), calls=%async_computation.1 | async-start | bytes 2883584 | tf_op jit(solution)/shard_map/all_to_all | solution.py:35
  78.2 3.6 %collective-permute-start.5 = (bf16[1024,256]{1,0:T(8,128)(2,1)S(1)}, bf16[1024,256]{1,0:T(8,128)(2,1)S(1)}, u32[]{:S(2)}, u32[]{:S(2)}) collective-permute-start(bf16[1024,256]{1,0:T(8,128)(2,1)S(1)} %get-tuple-element.28), channel_id=1, source_target_pairs={{0,128},{128,0},{1,129},{129,1},{2,130},{130,2},{3,131},{131,3},{4... | collective-permute-start | bytes 1572872 | tf_op jit(solution)/shard_map/ppermute | solution.py:445
  81.2 1.7 copy-start
  85.0 10.1 %collective-permute-start.7 = (bf16[2,256,256]{2,1,0:T(8,128)(2,1)S(1)}, bf16[2,256,256]{2,1,0:T(8,128)(2,1)S(1)}, u32[]{:S(2)}, u32[]{:S(2)}) collective-permute-start(bf16[2,256,256]{2,1,0:T(8,128)(2,1)S(1)} %get-tuple-element.35), channel_id=1, source_target_pairs={{4,0},{8,4},{12,8},{16,12},{20,16},{24,20},{28,24},{32,28},{36,32}... | collective-permute-start | bytes 786440 | tf_op jit(solution)/shard_map/ppermute | solution.py:30
  89.2 9.8 %collective-permute-start.6 = (bf16[2,256,256]{2,1,0:T(8,128)(2,1)S(1)}, bf16[2,256,256]{2,1,0:T(8,128)(2,1)S(1)}, u32[]{:S(2)}, u32[]{:S(2)}) collective-permute-start(bf16[2,256,256]{2,1,0:T(8,128)(2,1)S(1)} %get-tuple-element.36), channel_id=1, source_target_pairs={{0,4},{4,8},{8,12},{12,16},{16,20},{20,24},{24,28},{28,32},{32,36}... | collective-permute-start | bytes 786440 | tf_op jit(solution)/shard_map/ppermute | solution.py:29
  101.1 3.8 %collective-permute-start.8 = (bf16[2,2,256,256]{3,2,1,0:T(8,128)(2,1)S(1)}, bf16[2,2,256,256]{3,2,1,0:T(8,128)(2,1)S(1)}, u32[]{:S(2)}, u32[]{:S(2)}) collective-permute-start(bf16[2,2,256,256]{3,2,1,0:T(8,128)(2,1)S(1)} %shard_map.49), channel_id=1, source_target_pairs={{128,0},{129,1},{130,2},{131,3},{132,4},{133,5},{134,6},{135,7},{1... | collective-permute-start | bytes 1572872 | tf_op jit(solution)/shard_map/ppermute | solution.py:471

commit v5 on v4

--- a/solution.py
+++ b/solution.py
@@ -45,14 +45,14 @@
     return jnp.exp2(exponents.astype(F32)) * (1.0 / STEPS)
 
 
-def framed(piece):
+def framed(piece, mark):
     steps, exponent = coded(piece)
-    tail = jnp.broadcast_to(exponent, (8, 128))
+    row = lax.broadcasted_iota(jnp.int32, (8, 128), 0)
+    tail = jnp.where(row == 0, mark, exponent)
     return jnp.concatenate([steps, tail], axis=0).astype(I16)
 
 
-def unframed(rows):
-    wide = rows.astype(F32)
+def unframed(wide):
     return wide[:-8] * (jnp.exp2(wide[-1:]) * (1.0 / STEPS))
 
 
@@ -269,12 +269,13 @@
     )[0]
 
 
-def sum_plane(packed, pieces):
+def sum_plane(crowded, packed, pieces):
     senders, taps, size, outs = packed.shape
     taps = taps - 1
     half = taps // 2
 
-    def body(packed_ref, framed_ref, total):
+    def body(crowded_ref, packed_ref, framed_ref, total):
+        mark = jnp.full((1, 128), crowded_ref[0])
         scales = [decoded_scale(packed_ref[s, taps])[:1, :1] for s in range(senders)]
         for tap in range(taps):
             acc = packed_ref[0, tap].astype(F32) * scales[0]
@@ -290,23 +291,30 @@
                         oct_ * 8 : oct_ * 8 + 8,
                         lane * 128 : lane * 128 + 128,
                     ]
-                    framed_ref[place] = framed(piece.reshape(half * 8, 128))
+                    framed_ref[place] = framed(piece.reshape(half * 8, 128), mark)
                     place += 1
 
     return pl.pallas_call(
         body,
+        in_specs=[
+            pl.BlockSpec(memory_space=pltpu.SMEM),
+            pl.BlockSpec(memory_space=pltpu.VMEM),
+        ],
         out_shape=jax.ShapeDtypeStruct((pieces, half * 8 + 8, 128), I16),
         scratch_shapes=[pltpu.VMEM((taps, size, outs), F32)],
         compiler_params=pltpu.CompilerParams(vmem_limit_bytes=VMEM_LIMIT),
-    )(packed)
+    )(crowded, packed)
 
 
 def sum_line(framed_parts, factor):
     def body(parts_ref, out_ref):
-        acc = unframed(parts_ref[0])
+        first = parts_ref[0].astype(F32)
+        acc, mark = unframed(first), first[-8:-7]
         for s in range(1, framed_parts.shape[0]):
-            acc += unframed(parts_ref[s])
-        result = framed(acc * factor)
+            part = parts_ref[s].astype(F32)
+            acc += unframed(part)
+            mark = jnp.maximum(mark, part[-8:-7])
+        result = framed(acc * factor, mark)
         for s in range(framed_parts.shape[0]):
             out_ref[s] = result
 
@@ -326,7 +334,7 @@
             for frame in range(2):
                 for oct_ in range(size // 8):
                     for lane in range(channels // 128):
-                        piece = unframed(plane_ref[part, place]).reshape(3, 3, 8, 128)
+                        piece = unframed(plane_ref[part, place].astype(F32)).reshape(3, 3, 8, 128)
                         row = part * size + oct_ * 8
                         out_ref[frame, :, :, row : row + 8, lane * 128 : lane * 128 + 128] = piece
                         place += 1
@@ -341,20 +349,14 @@
     )(plane)
 
 
-def front(own_field, codebook, codes):
+def routed(codebook, shifted, holder, slots, turned, above, below):
     section_id = lax.axis_index("section")
     slab_id = lax.axis_index(SLAB)
-    slabs = lax.axis_size(SLAB)
     near = lax.axis_index("zh")
     plane_id = lax.axis_index(PLANE)
     planes = lax.axis_size(PLANE)
-    halves = slabs // planes
-    row_count, batch_count, frame_count, across, channels = own_field.shape
-    book = codebook.shape[0]
-    positions = row_count * batch_count * frame_count * across
-    mean = positions // planes
-    slots = int(mean + 6 * math.sqrt(mean) + 15) // 16 * 16
-    cells = (frame_count, row_count, batch_count * across, channels)
+    book, channels = codebook.shape
+    positions = shifted.shape[1]
 
     half = book // 2
     got = lax.ppermute(
@@ -363,29 +365,6 @@
     table = jnp.concatenate(
         [codebook, got, lax.ppermute(got, "section", [(0, 1), (1, 0)])], axis=0
     )
-
-    turned = own_field.reshape(
-        row_count, batch_count, frame_count, halves, planes, row_count, channels
-    )
-    turned = jnp.transpose(turned, (3, 4, 2, 5, 1, 0, 6)).reshape(halves, planes, -1, channels)
-    kept = lax.dynamic_index_in_dim(turned, near, 0, keepdims=False)
-    passed = lax.dynamic_index_in_dim(turned, 1 - near, 0, keepdims=False)
-    passed = lax.ppermute(passed, ("section", "zh"), [(2, 3), (3, 2)])
-
-    own = jnp.transpose(own_field, (2, 0, 1, 3, 4)).reshape(cells)
-    above, below = neighbours(own[:, -1], own[:, 0])
-
-    edge = jnp.full((1,) + codes.shape[1:], -1, codes.dtype)
-    shifted = jnp.concatenate([edge, codes, edge], axis=0)
-    shifted = shifted.reshape(slabs + 1, row_count, batch_count, frame_count, across)
-    shifted = jnp.transpose(shifted, (0, 3, 1, 2, 4)).reshape(slabs + 1, positions)
-    holder = jnp.where(shifted >= 0, shifted // book % planes, -1)
-
-    counts = jnp.sum(
-        (holder[:, None, :] == lax.broadcasted_iota(jnp.int32, (1, planes, 1), 1)).astype(F32), axis=-1
-    )
-    crowded = jnp.full((lax.axis_size("dp"), 8, 128), jnp.max(counts) - slots)
-    crowded = exchange(crowded, "dp")
 
     before = (
         lax.broadcasted_iota(jnp.int32, (positions, positions), 0)
@@ -405,25 +384,11 @@
     picks = (
         asked.reshape(-1, 1) == lax.broadcasted_iota(jnp.int32, (1, 2 * book), 1)
     ).astype(BF16)
-    table, passed, above, below, crowded = lax.optimization_barrier(
-        (table, passed, above, below, crowded)
-    )
+    table, turned = lax.optimization_barrier((table, turned))
     words = jnp.dot(picks, table, preferred_element_type=F32).astype(BF16)
-    words = words.reshape(planes, slots, channels)
-
-    arrived = exchange(jnp.concatenate([words, kept, passed], axis=1), PLANE)
-    looked = arrived[:, :slots].reshape(planes * slots, channels)
-
-    place = lax.broadcasted_iota(jnp.int32, (positions, 1), 0)
-    group, column = place // across, place % across
-    source = column // row_count
-    share = positions // slabs
-    place = (source % planes) * (halves * share) + jnp.where(source // planes == near, 0, share)
-    place = place + group * row_count + column % row_count
-    sent = (place == lax.broadcasted_iota(jnp.int32, (1, positions), 1)).astype(BF16)
-    cotangent = jnp.dot(
-        sent, arrived[:, slots:].reshape(positions, channels), preferred_element_type=F32
-    ).astype(BF16)
+    looked = exchange(words.reshape(planes, slots, channels), PLANE)
+    looked = looked.reshape(planes * slots, channels)
+    looked, above, below = lax.optimization_barrier((looked, above, below))
 
     own_wanted = lax.dynamic_index_in_dim(shifted, slab_id + section_id, 0, keepdims=False)
     own_holder = lax.dynamic_index_in_dim(holder, slab_id + section_id, 0, keepdims=False)
@@ -434,14 +399,56 @@
     gather = (
         order[:, None] == lax.broadcasted_iota(jnp.int32, (1, planes * slots), 1)
     ).astype(BF16)
-    fast = jnp.dot(gather, looked, preferred_element_type=F32).astype(BF16)
-
-    def whole_book(_):
+    pair = jnp.dot(gather, looked, preferred_element_type=F32).astype(BF16)
+    return pair, turned, above, below
+
+
+def front(own_field, codebook, codes, whole):
+    section_id = lax.axis_index("section")
+    slab_id = lax.axis_index(SLAB)
+    slabs = lax.axis_size(SLAB)
+    planes = lax.axis_size(PLANE)
+    row_count, batch_count, frame_count, across, channels = own_field.shape
+    book = codebook.shape[0]
+    positions = row_count * batch_count * frame_count * across
+    mean = positions // planes
+    slots = int(mean + 6 * math.sqrt(mean) + 15) // 16 * 16
+    cells = (frame_count, row_count, batch_count * across, channels)
+
+    turned = own_field.reshape(row_count, batch_count, frame_count, slabs, row_count, channels)
+    turned = jnp.transpose(turned, (3, 2, 4, 1, 0, 5)).reshape(slabs, -1, channels)
+    turned = exchange(turned, SLAB).reshape(positions, channels)
+
+    own = jnp.transpose(own_field, (2, 0, 1, 3, 4)).reshape(cells)
+    above, below = neighbours(own[:, -1], own[:, 0])
+
+    edge = jnp.full((1,) + codes.shape[1:], -1, codes.dtype)
+    shifted = jnp.concatenate([edge, codes, edge], axis=0)
+    shifted = shifted.reshape(slabs + 1, row_count, batch_count, frame_count, across)
+    shifted = jnp.transpose(shifted, (0, 3, 1, 2, 4)).reshape(slabs + 1, positions)
+    holder = jnp.where(shifted >= 0, shifted // book % planes, -1)
+
+    if whole:
+        wanted = lax.dynamic_index_in_dim(shifted, slab_id + section_id, 0, keepdims=False)
         every = lax.all_gather(codebook, SLAB, axis=0, tiled=True)
-        taken = jnp.take(every, jnp.maximum(own_wanted, 0), axis=0)
-        return jnp.where(own_wanted[:, None] >= 0, taken, 0).astype(BF16)
-
-    pair = lax.cond(jnp.max(crowded) > 0, whole_book, lambda quick: quick, fast)
+        taken = jnp.take(every, jnp.maximum(wanted, 0), axis=0)
+        pair = jnp.where(wanted[:, None] >= 0, taken, 0).astype(BF16)
+    else:
+        pair, turned, above, below = routed(
+            codebook, shifted, holder, slots, turned, above, below
+        )
+
+    place = lax.broadcasted_iota(jnp.int32, (positions, 1), 0)
+    group, column = place // across, place % across
+    place = (column // row_count) * (positions // slabs) + group * row_count + column % row_count
+    sent = (place == lax.broadcasted_iota(jnp.int32, (1, positions), 1)).astype(BF16)
+    cotangent = jnp.dot(sent, turned, preferred_element_type=F32).astype(BF16)
+
+    counts = jnp.sum(
+        (holder[:, None, :] == lax.broadcasted_iota(jnp.int32, (1, planes, 1), 1)).astype(F32), axis=-1
+    )
+    crowded = (jnp.max(counts) > slots).astype(F32).reshape(1)
+
     other = lax.ppermute(pair, "section", [(0, 1), (1, 0)])
     return (
         pair.reshape(cells),
@@ -450,17 +457,18 @@
         own,
         above,
         below,
-    )
-
-
-def on_device(fields, kernels, codebook, codes):
+        crowded,
+    )
+
+
+def line_shares(fields, kernels, codebook, codes, whole):
     section = lax.axis_index("section").reshape(1).astype(jnp.int32)
     slabs = lax.axis_size(SLAB)
     own_field = fields[0]
     kernel = kernels[0]
     row_count, batch_count, frame_count, across, channels = own_field.shape
     cells = (frame_count, row_count, batch_count * across, channels)
-    pair, other, cotangent, own, above, below = front(own_field, codebook, codes)
+    pair, other, cotangent, own, above, below, crowded = front(own_field, codebook, codes, whole)
     source = shift_source(section, pair, other, own, above, below, across)
     pre_act, dec_grad = convolve(section, source, kernel, cotangent)
 
@@ -473,15 +481,29 @@
     total = (
         row_count * slabs * across * batch_count * lax.axis_size("dp") * frame_count
     )
-    nx, ny, nz = lax.axis_size("x"), lax.axis_size("y"), lax.axis_size(Z)
     packed = kernel_grads(
-        section, source, pre_act, dec_grad, returned, pair, other, nx * ny
+        section, source, pre_act, dec_grad, returned, pair, other, lax.axis_size(PLANE)
     )
     plane = exchange(packed, PLANE)
-    line = exchange(sum_plane(plane, nz), Z)
-    line = exchange(sum_line(line, 1.0 / math.sqrt(total)), Z)
-    plane = exchange(jnp.broadcast_to(line[None], (nx * ny,) + line.shape), PLANE)
-    return unpack(plane, channels)[None]
+    line = exchange(sum_plane(crowded, plane, lax.axis_size(Z)), Z)
+    return exchange(sum_line(line, 1.0 / math.sqrt(total)), Z)
+
+
+def on_device(fields, kernels, codebook, codes):
+    line = line_shares(fields, kernels, codebook, codes, False)
+    line = lax.cond(
+        jnp.max(line[:, -8]) > 0,
+        lambda frames, *args: line_shares(*args, True),
+        lambda frames, *args: frames,
+        line,
+        fields,
+        kernels,
+        codebook,
+        codes,
+    )
+    planes = lax.axis_size(PLANE)
+    plane = exchange(jnp.broadcast_to(line[None], (planes,) + line.shape), PLANE)
+    return unpack(plane, kernels.shape[-1])[None]
 
 
 def solution(mesh):

time: 238 us -> 232 us (0.975)
  blocking collectives: 117 us -> 56.2 us
  waiting for transfers between devices: 28.6 us -> 71.6 us
  starting transfers between devices: 44.3 us -> 53.8 us
    all_to_all x4 -> x2, blocking collectives: 117 us -> 56.2 us  [exchange(): return lax.all_to_all(cells, axes, split_axis=0, concat_axis=0, tiled=True)]
    all_to_all x2 -> x4, waiting for transfers between devices: 17.7 us -> 52.1 us  [exchange(): return lax.all_to_all(cells, axes, split_axis=0, concat_axis=0, tiled=True)]
    all_to_all x2 -> x4, starting transfers between devices: 22.5 us -> 33.3 us  [exchange(): return lax.all_to_all(cells, axes, split_axis=0, concat_axis=0, tiled=True)]
    ppermute x2, waiting for transfers between devices: 4.29 us -> 12.2 us  [neighbours(): above = lax.ppermute(lower, SLAB, [(i, i + 1) for i in range(count - 1)])]
    ppermute x4 -> x3, starting transfers between devices: 7.68 us -> 8.66 us  [the longest x1 7.28 us: routed(): lax.ppermute(lax.dynamic_slice_in_dim(codebook, section_id * half, half,...]
  transfers between devices with their start and end apart: 11 -> 12, of which waited for: 7 -> 11; matrix products, arithmetic and copies ran while one was open for 3% -> 5% of each run, Pallas kernels for 0% -> 0%
where the time goes in v5:
time: 232 us; the launch traced here: 231 us
  waiting for transfers between devices  71.6 us (31%)
  blocking collectives  56.2 us (24%)
  starting transfers between devices  53.8 us (23%)
  Pallas kernels  15.7 us (7%)
  between operations  15 us (6%)
  matrix products  6.64 us (3%)
  other arithmetic  6.25 us (3%)
  local copies, waits for them, and re-layouts  5.6 us (2%)
    all_to_all x2, blocking collectives, exchange(): return lax.all_to_all(cells, axes, split_axis=0, concat_axis=0, tiled=True)  56.2 us
    all_to_all x4, waiting for transfers between devices, exchange(): return lax.all_to_all(cells, axes, split_axis=0, concat_axis=0, tiled=True)  52.1 us
    all_to_all x4, starting transfers between devices, exchange(): return lax.all_to_all(cells, axes, split_axis=0, concat_axis=0, tiled=True)  33.3 us
    ppermute x2, waiting for transfers between devices, neighbours(): above = lax.ppermute(lower, SLAB, [(i, i + 1) for i in range(count - 1)])  12.2 us
    pallas_call x5, Pallas kernels, call(): pl.pallas_call(body, in_specs=[pl.BlockSpec(memory_space=pltpu.SMEM)] + [...  10.4 us
    ppermute x1, starting transfers between devices, routed(): lax.ppermute(lax.dynamic_slice_in_dim(codebook, section_id * half, half,...  7.28 us
    ppermute x2, starting transfers between devices, neighbours(): above = lax.ppermute(lower, SLAB, [(i, i + 1) for i in range(count - 1)])  6.43 us
    ppermute x2, starting transfers between devices, neighbours(): below = lax.ppermute(upper, SLAB, [(i + 1, i) for i in range(count - 1)])  5.26 us
  transfers between devices with their start and end apart: 12, of which 11 were waited for; matrix products, arithmetic and copies ran while one was open for 5% of the time, Pallas kernels for 0%

profile of v5, /device:TPU:2, one launch (start us, length us, event | category | flops | bytes accessed | tf_op | source)
XLA Modules:
  0.0 231.0 jit_solution(2281675490809406347)
XLA Ops:
  6.5 1.0 constant_dynamic-slice_fusion.1
  7.6 7.3 %collective-permute-start.6 = (bf16[512,256]{1,0:T(8,128)(2,1)S(1)}, bf16[512,256]{1,0:T(8,128)(2,1)S(1)}, u32[]{:S(2)}, u32[]{:S(2)}) collective-permute-start(bf16[512,256]{1,0:T(8,128)(2,1)S(1)} %constant_dynamic-slice_fusion.1), channel_id=1, source_target_pairs={{0,64},{64,0},{1,65},{65,1},{2,66},{66,2},{3,67},{67,3},{4,68},{68... | collective-permute-start | bytes 786440 | tf_op jit(solution)/shard_map/ppermute | solution.py:362
  14.8 1.6 copy.64
  16.5 1.1 copy.66
  17.6 7.6 %all-to-all-start.4 = ((bf16[32,32,256]{2,1,0:T(8,128)(2,1)}), bf16[32,32,256]{2,1,0:T(8,128)(2,1)S(1)}, u32[]{:S(2)}, u32[]{:S(2)}) async-start(bf16[32,32,256]{2,1,0:T(8,128)(2,1)} %copy.66), calls=%async_computation.4 | async-start | bytes 1048576 | tf_op jit(solution)/shard_map/all_to_all | solution.py:35
  25.5 0.2 reshape.452
  25.7 0.2 fusion.43
  26.0 0.3 fusion.39
  26.5 1.0 select_reduce_fusion
  27.5 0.5 collective-permute-done.7
  28.0 1.0 pad_maximum_fusion
  29.0 13.1 %all-to-all-done.4 = bf16[32,32,256]{2,1,0:T(8,128)(2,1)S(1)} async-done(((bf16[32,32,256]{2,1,0:T(8,128)(2,1)}), bf16[32,32,256]{2,1,0:T(8,128)(2,1)S(1)}, u32[]{:S(2)}, u32[]{:S(2)}) %all-to-all-start.4) | async-done | bytes 524320 | tf_op jit(solution)/shard_map/all_to_all | solution.py:35
  42.1 3.7 %fusion.32 = bf16[1792,256]{1,0:T(8,128)(2,1)} fusion(bf16[2048,256]{1,0:T(8,128)(2,1)S(1)} %pad_maximum_fusion, s32[1792]{0:T(1024)S(1)} %eq.153), kind=kOutput, calls=%fused_computation.72 | convolution fusion | flops 1883176960 | bytes 1973248 | tf_op jit(solution)/shard_map/dot_general | solution.py:388
  45.8 5.0 %all-to-all-start.5 = ((bf16[16,112,256]{2,1,0:T(8,128)(2,1)}), bf16[16,112,256]{2,1,0:T(8,128)(2,1)S(1)}, u32[]{:S(2)}, u32[]{:S(2)}) async-start(bf16[16,112,256]{2,1,0:T(8,128)(2,1)} %bitcast.104), calls=%async_computation.5 | async-start | bytes 1835008 | tf_op jit(solution)/shard_map/all_to_all | solution.py:35
  50.9 0.8 slice_bitcast_fusion.6
  51.7 3.4 %collective-permute-start.8 = (bf16[2,256,256]{2,1,0:T(8,128)(2,1)}, bf16[2,256,256]{2,1,0:T(8,128)(2,1)S(1)}, u32[]{:S(2)}, u32[]{:S(2)}) collective-permute-start(bf16[2,256,256]{2,1,0:T(8,128)(2,1)} %get-tuple-element.69), channel_id=1, source_target_pairs={{0,4},{4,8},{8,12},{12,16},{16,20},{20,24},{24,28},{28,32},{32,36}... | collective-permute-start | bytes 786440 | tf_op jit(solution)/shard_map/ppermute | solution.py:29
  55.1 2.5 %collective-permute-start.9 = (bf16[2,256,256]{2,1,0:T(8,128)(2,1)}, bf16[2,256,256]{2,1,0:T(8,128)(2,1)S(1)}, u32[]{:S(2)}, u32[]{:S(2)}) collective-permute-start(bf16[2,256,256]{2,1,0:T(8,128)(2,1)} %get-tuple-element.68), channel_id=1, source_target_pairs={{4,0},{8,4},{12,8},{16,12},{20,16},{24,20},{28,24},{32,28},{36,32}... | collective-permute-start | bytes 786440 | tf_op jit(solution)/shard_map/ppermute | solution.py:30
  57.6 0.3 fusion.40
  58.0 7.5 %collective-permute-done.8.above_ref = bf16[2,256,256]{2,1,0:T(8,128)(2,1)S(1)} collective-permute-done((bf16[2,256,256]{2,1,0:T(8,128)(2,1)}, bf16[2,256,256]{2,1,0:T(8,128)(2,1)S(1)}, u32[]{:S(2)}, u32[]{:S(2)}) %collective-permute-start.8) | collective-permute-done | bytes 262176 | tf_op jit(solution)/shard_map/ppermute | solution.py:29
  65.5 1.2 collective-permute-done.9.below_ref
  66.7 1.4 fusion.35
  68.3 0.8 fusion.34
  69.1 1.0 collective-permute-done.10
  70.1 0.7 shard_map.46.source_ref
  70.8 2.1 shard_map.48
  73.0 3.1 %collective-permute-start.11 = (bf16[2,256,256]{2,1,0:T(8,128)(2,1)S(1)}, bf16[2,256,256]{2,1,0:T(8,128)(2,1)S(1)}, u32[]{:S(2)}, u32[]{:S(2)}) collective-permute-start(bf16[2,256,256]{2,1,0:T(8,128)(2,1)S(1)} %get-tuple-element.67), channel_id=1, source_target_pairs={{0,4},{4,8},{8,12},{12,16},{16,20},{20,24},{24,28},{28,32},{32,36}... | collective-permute-start | bytes 786440 | tf_op jit(solution)/shard_map/ppermute | solution.py:29
  76.1 2.8 %collective-permute-start.12 = (bf16[2,256,256]{2,1,0:T(8,128)(2,1)S(1)}, bf16[2,256,256]{2,1,0:T(8,128)(2,1)S(1)}, u32[]{:S(2)}, u32[]{:S(2)}) collective-permute-start(bf16[2,256,256]{2,1,0:T(8,128)(2,1)S(1)} %get-tuple-element.66), channel_id=1, source_target_pairs={{4,0},{8,4},{12,8},{16,12},{20,16},{24,20},{28,24},{32,28},{36,32}... | collective-permute-start | bytes 786440 | tf_op jit(solution)/shard_map/ppermute | solution.py:30
  78.9 4.7 %collective-permute-done.11.above_ref = bf16[2,256,256]{2,1,0:T(8,128)(2,1)S(1)} collective-permute-done((bf16[2,256,256]{2,1,0:T(8,128)(2,1)S(1)}, bf16[2,256,256]{2,1,0:T(8,128)(2,1)S(1)}, u32[]{:S(2)}, u32[]{:S(2)}) %collective-permute-start.11) | collective-permute-done | bytes 262176 | tf_op jit(solution)/shard_map/ppermute | solution.py:29
  83.6 3.1 %collective-permute-done.12.below_ref = bf16[2,256,256]{2,1,0:T(8,128)(2,1)S(1)} collective-permute-done((bf16[2,256,256]{2,1,0:T(8,128)(2,1)S(1)}, bf16[2,256,256]{2,1,0:T(8,128)(2,1)S(1)}, u32[]{:S(2)}, u32[]{:S(2)}) %collective-permute-start.12) | collective-permute-done | bytes 262176 | tf_op jit(solution)/shard_map/ppermute | solution.py:30
  86.7 2.1 shard_map.49
  88.7 1.3 collective-permute-start.13
  90.0 0.9 shard_map.47.turned_ref
  91.0 1.6 collective-permute-done.13.returned_ref
  92.5 4.6 %shard_map.50 = s16[16,19,16,256]{3,2,1,0:T(8,128)(2,1)} custom-call(s32[1]{0:T(128)} %bitcast.25.section_ref, bf16[3,256,2048]{2,1,0:T(8,128)(2,1)S(1)} %shard_map.47.turned_ref, f32[2,512,256]{2,1,0:T(8,128)S(1)} %get-tuple-element.35.pre_ref, bf16[2,512,256]{2,1,0:T(8,128)(2,1)S(1)} %get-tuple-element.36.dec_ref, ...), custom_call_target="tpu_custom_call" | custom-call | flops 1811939328 | bytes 8781828 | tf_op jit(solution)/shard_map/pallas_call | solution.py:76
  97.1 17.3 %all-to-all-start.6 = ((s16[16,19,16,256]{3,2,1,0:T(8,128)(2,1)}), s16[16,19,16,256]{3,2,1,0:T(8,128)(2,1)S(1)}, u32[]{:S(2)}, u32[]{:S(2)}) async-start(s16[16,19,16,256]{3,2,1,0:T(8,128)(2,1)} %shard_map.50), calls=%async_computation.6 | async-start | bytes 4980736 | tf_op jit(solution)/shard_map/all_to_all | solution.py:35
  114.5 1.8 convert_reduce_fusion.1
  116.3 1.4 reduce_max.27
  118.3 29.6 %all-to-all-done.6.packed_ref = s16[16,19,16,256]{3,2,1,0:T(8,128)(2,1)S(1)} async-done(((s16[16,19,16,256]{3,2,1,0:T(8,128)(2,1)}), s16[16,19,16,256]{3,2,1,0:T(8,128)(2,1)S(1)}, u32[]{:S(2)}, u32[]{:S(2)}) %all-to-all-start.6) | async-done | bytes 2490400 | tf_op jit(solution)/shard_map/all_to_all | solution.py:35
  147.9 0.8 shard_map.51
  148.7 18.6 %all_to_all.51.parts_ref = s16[8,80,128]{2,1,0:T(8,128)(2,1)} all-to-all(s16[8,80,128]{2,1,0:T(8,128)(2,1)S(1)} %shard_map.51), channel_id=1, replica_groups=mesh['section'=2,'zh'=2,'y'=4,'x'=4,'dp'=4] {'zh','dp'}, dimensions={0} | all-to-all | bytes 327680 | tf_op jit(solution)/shard_map/all_to_all | solution.py:35
  167.2 1.8 shard_map.52
  169.0 3.4 %all-to-all-start.8 = ((s16[8,80,128]{2,1,0:T(8,128)(2,1)}), s16[8,80,128]{2,1,0:T(8,128)(2,1)S(1)}, u32[]{:S(2)}, u32[]{:S(2)}) async-start(s16[8,80,128]{2,1,0:T(8,128)(2,1)} %shard_map.52), calls=%async_computation.8 | async-start | bytes 327680 | tf_op jit(solution)/shard_map/all_to_all | solution.py:35
  172.4 9.3 %all-to-all-done.8 = s16[8,80,128]{2,1,0:T(8,128)(2,1)S(1)} async-done(((s16[8,80,128]{2,1,0:T(8,128)(2,1)}), s16[8,80,128]{2,1,0:T(8,128)(2,1)S(1)}, u32[]{:S(2)}, u32[]{:S(2)}) %all-to-all-start.8) | async-done | bytes 163872 | tf_op jit(solution)/shard_map/all_to_all | solution.py:35
  181.8 0.6 slice_reduce_fusion
  183.1 0.3 conditional.1
  183.3 0.5 broadcast_in_dim.81
  183.9 37.6 %all_to_all.52.plane_ref = s16[16,8,80,128]{3,2,1,0:T(8,128)(2,1)S(1)} all-to-all(s16[16,8,80,128]{3,2,1,0:T(8,128)(2,1)S(1)} %broadcast_in_dim.81), channel_id=1, replica_groups=mesh['section'=2,'zh'=2,'y'=4,'x'=4,'dp'=4] {'y','x'}, dimensions={0} | all-to-all | bytes 5242880 | tf_op jit(solution)/shard_map/all_to_all | solution.py:35
  221.5 2.7 %shard_map.53 = f32[2,3,3,256,256]{4,3,2,1,0:T(8,128)} custom-call(s16[16,8,80,128]{3,2,1,0:T(8,128)(2,1)S(1)} %all_to_all.52.plane_ref), custom_call_target="tpu_custom_call" | custom-call | tf_op jit(solution)/shard_map/pallas_call | solution.py:342
  (33 shorter events, 0.9 us)
Async XLA Ops:
  6.5 18.7 %copy-start.3 = (s32[64,4,2,64]{3,2,1,0:T(2,128)S(1)}, s32[64,4,2,64]{3,2,1,0:T(2,128)}, u32[]{:S(2)}) copy-start(s32[64,4,2,64]{3,2,1,0:T(2,128)} %param.9) | copy-start | bytes 393220
  7.6 18.8 %collective-permute-start.6 = (bf16[512,256]{1,0:T(8,128)(2,1)S(1)}, bf16[512,256]{1,0:T(8,128)(2,1)S(1)}, u32[]{:S(2)}, u32[]{:S(2)}) collective-permute-start(bf16[512,256]{1,0:T(8,128)(2,1)S(1)} %constant_dynamic-slice_fusion.1), channel_id=1, source_target_pairs={{0,64},{64,0},{1,65},{65,1},{2,66},{66,2},{3,67},{67,3},{4,68},{68... | collective-permute-start | bytes 786440 | tf_op jit(solution)/shard_map/ppermute | solution.py:362
  16.4 11.6 %copy-start.1 = (bf16[1024,256]{1,0:T(8,128)(2,1)S(1)}, bf16[1024,256]{1,0:T(8,128)(2,1)}, u32[]{:S(2)}) copy-start(bf16[1024,256]{1,0:T(8,128)(2,1)} %param.8) | copy-start | bytes 1572868
  17.6 24.5 %all-to-all-start.4 = ((bf16[32,32,256]{2,1,0:T(8,128)(2,1)}), bf16[32,32,256]{2,1,0:T(8,128)(2,1)S(1)}, u32[]{:S(2)}, u32[]{:S(2)}) async-start(bf16[32,32,256]{2,1,0:T(8,128)(2,1)} %copy.66), calls=%async_computation.4 | async-start | bytes 1048576 | tf_op jit(solution)/shard_map/all_to_all | solution.py:35
  25.8 31.7 %copy-start.5 = (s32[33,1024]{1,0:T(8,128)}, s32[33,1024]{1,0:T(8,128)S(1)}, u32[]{:S(2)}) copy-start(s32[33,1024]{1,0:T(8,128)S(1)} %fusion.43) | copy-start | bytes 405508
  26.3 1.1 copy-start.8
  26.4 1.6 collective-permute-start.7
  42.1 3.7 %copy-start.6 = (bf16[32,32,256]{2,1,0:T(8,128)(2,1)}, bf16[32,32,256]{2,1,0:T(8,128)(2,1)S(1)}, u32[]{:S(2)}) copy-start(bf16[32,32,256]{2,1,0:T(8,128)(2,1)S(1)} %all-to-all-done.4) | copy-start | bytes 1572868
  42.1 8.7 %copy-start = (bf16[1,2,4,2,64,256]{5,4,3,2,1,0:T(8,128)(2,1)S(1)}, bf16[1,2,4,2,64,256]{5,4,3,2,1,0:T(8,128)(2,1)}, u32[]{:S(2)}) copy-start(bf16[1,2,4,2,64,256]{5,4,3,2,1,0:T(8,128)(2,1)} %param.6) | copy-start | bytes 1572868
  45.8 20.9 %all-to-all-start.5 = ((bf16[16,112,256]{2,1,0:T(8,128)(2,1)}), bf16[16,112,256]{2,1,0:T(8,128)(2,1)S(1)}, u32[]{:S(2)}, u32[]{:S(2)}) async-start(bf16[16,112,256]{2,1,0:T(8,128)(2,1)} %bitcast.104), calls=%async_computation.5 | async-start | bytes 1835008 | tf_op jit(solution)/shard_map/all_to_all | solution.py:35
  51.7 13.8 %collective-permute-start.8 = (bf16[2,256,256]{2,1,0:T(8,128)(2,1)}, bf16[2,256,256]{2,1,0:T(8,128)(2,1)S(1)}, u32[]{:S(2)}, u32[]{:S(2)}) collective-permute-start(bf16[2,256,256]{2,1,0:T(8,128)(2,1)} %get-tuple-element.69), channel_id=1, source_target_pairs={{0,4},{4,8},{8,12},{12,16},{16,20},{20,24},{24,28},{28,32},{32,36}... | collective-permute-start | bytes 786440 | tf_op jit(solution)/shard_map/ppermute | solution.py:29
  55.1 11.6 %collective-permute-start.9 = (bf16[2,256,256]{2,1,0:T(8,128)(2,1)}, bf16[2,256,256]{2,1,0:T(8,128)(2,1)S(1)}, u32[]{:S(2)}, u32[]{:S(2)}) collective-permute-start(bf16[2,256,256]{2,1,0:T(8,128)(2,1)} %get-tuple-element.68), channel_id=1, source_target_pairs={{4,0},{8,4},{12,8},{16,12},{20,16},{24,20},{28,24},{32,28},{36,32}... | collective-permute-start | bytes 786440 | tf_op jit(solution)/shard_map/ppermute | solution.py:30
  66.7 1.6 copy-start.7
  68.1 2.0 collective-permute-start.10
  69.1 1.7 copy-start.9
  73.0 10.6 %collective-permute-start.11 = (bf16[2,256,256]{2,1,0:T(8,128)(2,1)S(1)}, bf16[2,256,256]{2,1,0:T(8,128)(2,1)S(1)}, u32[]{:S(2)}, u32[]{:S(2)}) collective-permute-start(bf16[2,256,256]{2,1,0:T(8,128)(2,1)S(1)} %get-tuple-element.67), channel_id=1, source_target_pairs={{0,4},{4,8},{8,12},{12,16},{16,20},{20,24},{24,28},{28,32},{32,36}... | collective-permute-start | bytes 786440 | tf_op jit(solution)/shard_map/ppermute | solution.py:29
  76.1 10.6 %collective-permute-start.12 = (bf16[2,256,256]{2,1,0:T(8,128)(2,1)S(1)}, bf16[2,256,256]{2,1,0:T(8,128)(2,1)S(1)}, u32[]{:S(2)}, u32[]{:S(2)}) collective-permute-start(bf16[2,256,256]{2,1,0:T(8,128)(2,1)S(1)} %get-tuple-element.66), channel_id=1, source_target_pairs={{4,0},{8,4},{12,8},{16,12},{20,16},{24,20},{28,24},{32,28},{36,32}... | collective-permute-start | bytes 786440 | tf_op jit(solution)/shard_map/ppermute | solution.py:30
  88.7 3.8 %collective-permute-start.13 = (bf16[2,2,256,256]{3,2,1,0:T(8,128)(2,1)S(1)}, bf16[2,2,256,256]{3,2,1,0:T(8,128)(2,1)S(1)}, u32[]{:S(2)}, u32[]{:S(2)}) collective-permute-start(bf16[2,2,256,256]{3,2,1,0:T(8,128)(2,1)S(1)} %shard_map.49), channel_id=1, source_target_pairs={{128,0},{129,1},{130,2},{131,3},{132,4},{133,5},{134,6},{135,7},{1... | collective-permute-start | bytes 1572872 | tf_op jit(solution)/shard_map/ppermute | solution.py:479
  97.1 50.7 %all-to-all-start.6 = ((s16[16,19,16,256]{3,2,1,0:T(8,128)(2,1)}), s16[16,19,16,256]{3,2,1,0:T(8,128)(2,1)S(1)}, u32[]{:S(2)}, u32[]{:S(2)}) async-start(s16[16,19,16,256]{3,2,1,0:T(8,128)(2,1)} %shard_map.50), calls=%async_computation.6 | async-start | bytes 4980736 | tf_op jit(solution)/shard_map/all_to_all | solution.py:35
  169.0 12.7 %all-to-all-start.8 = ((s16[8,80,128]{2,1,0:T(8,128)(2,1)}), s16[8,80,128]{2,1,0:T(8,128)(2,1)S(1)}, u32[]{:S(2)}, u32[]{:S(2)}) async-start(s16[8,80,128]{2,1,0:T(8,128)(2,1)} %shard_map.52), calls=%async_computation.8 | async-start | bytes 327680 | tf_op jit(solution)/shard_map/all_to_all | solution.py:35

commit v6 on v5

--- a/solution.py
+++ b/solution.py
@@ -384,11 +384,10 @@
     picks = (
         asked.reshape(-1, 1) == lax.broadcasted_iota(jnp.int32, (1, 2 * book), 1)
     ).astype(BF16)
-    table, turned = lax.optimization_barrier((table, turned))
+    table, turned, above, below = lax.optimization_barrier((table, turned, above, below))
     words = jnp.dot(picks, table, preferred_element_type=F32).astype(BF16)
     looked = exchange(words.reshape(planes, slots, channels), PLANE)
     looked = looked.reshape(planes * slots, channels)
-    looked, above, below = lax.optimization_barrier((looked, above, below))
 
     own_wanted = lax.dynamic_index_in_dim(shifted, slab_id + section_id, 0, keepdims=False)
     own_holder = lax.dynamic_index_in_dim(holder, slab_id + section_id, 0, keepdims=False)

time: 232 us -> 239 us (1.030)
  starting transfers between devices: 53.8 us -> 63.6 us
  waiting for transfers between devices: 71.6 us -> 66 us
    all_to_all x4, starting transfers between devices: 33.3 us -> 43.2 us  [exchange(): return lax.all_to_all(cells, axes, split_axis=0, concat_axis=0, tiled=True)]
    ppermute x2, waiting for transfers between devices: 12.2 us -> 6.99 us  [neighbours(): above = lax.ppermute(lower, SLAB, [(i, i + 1) for i in range(count - 1)])]
  transfers between devices with their start and end apart: 12 -> 12, of which waited for: 11 -> 10; matrix products, arithmetic and copies ran while one was open for 5% -> 5% of each run, Pallas kernels for 0% -> 0%
where the time goes in v6:
time: 239 us; the launch traced here: 238 us
  waiting for transfers between devices  66 us (28%)
  starting transfers between devices  63.6 us (27%)
  blocking collectives  56.9 us (24%)
  Pallas kernels  15.7 us (7%)
  between operations  15.1 us (6%)
  matrix products  7.67 us (3%)
  local copies, waits for them, and re-layouts  6.56 us (3%)
  other arithmetic  6.38 us (3%)
    all_to_all x2, blocking collectives, exchange(): return lax.all_to_all(cells, axes, split_axis=0, concat_axis=0, tiled=True)  56.9 us
    all_to_all x4, waiting for transfers between devices, exchange(): return lax.all_to_all(cells, axes, split_axis=0, concat_axis=0, tiled=True)  52.1 us
    all_to_all x4, starting transfers between devices, exchange(): return lax.all_to_all(cells, axes, split_axis=0, concat_axis=0, tiled=True)  43.2 us
    pallas_call x5, Pallas kernels, call(): pl.pallas_call(body, in_specs=[pl.BlockSpec(memory_space=pltpu.SMEM)] + [...  10.4 us
    ppermute x1, starting transfers between devices, routed(): lax.ppermute(lax.dynamic_slice_in_dim(codebook, section_id * half, half,...  7.28 us
    ppermute x2, waiting for transfers between devices, neighbours(): above = lax.ppermute(lower, SLAB, [(i, i + 1) for i in range(count - 1)])  6.99 us
    ppermute x2, starting transfers between devices, neighbours(): below = lax.ppermute(upper, SLAB, [(i + 1, i) for i in range(count - 1)])  6.42 us
    ppermute x2, starting transfers between devices, neighbours(): above = lax.ppermute(lower, SLAB, [(i, i + 1) for i in range(count - 1)])  5.28 us
  transfers between devices with their start and end apart: 12, of which 10 were waited for; matrix products, arithmetic and copies ran while one was open for 5% of the time, Pallas kernels for 0%

profile of v6, /device:TPU:2, one launch (start us, length us, event | category | flops | bytes accessed | tf_op | source)
XLA Modules:
  0.0 238.2 jit_solution(741668652121986861)
XLA Ops:
  6.5 1.0 constant_dynamic-slice_fusion.1
  7.6 7.3 %collective-permute-start.6 = (bf16[512,256]{1,0:T(8,128)(2,1)S(1)}, bf16[512,256]{1,0:T(8,128)(2,1)S(1)}, u32[]{:S(2)}, u32[]{:S(2)}) collective-permute-start(bf16[512,256]{1,0:T(8,128)(2,1)S(1)} %constant_dynamic-slice_fusion.1), channel_id=1, source_target_pairs={{0,64},{64,0},{1,65},{65,1},{2,66},{66,2},{3,67},{67,3},{4,68},{68... | collective-permute-start | bytes 786440 | tf_op jit(solution)/shard_map/ppermute | solution.py:362
  14.9 1.6 copy.64
  16.5 1.1 copy.66
  17.6 7.8 %all-to-all-start.4 = ((bf16[32,32,256]{2,1,0:T(8,128)(2,1)}), bf16[32,32,256]{2,1,0:T(8,128)(2,1)}, u32[]{:S(2)}, u32[]{:S(2)}) async-start(bf16[32,32,256]{2,1,0:T(8,128)(2,1)} %copy.66), calls=%async_computation.4 | async-start | bytes 1048576 | tf_op jit(solution)/shard_map/all_to_all | solution.py:35
  25.5 0.8 slice_bitcast_fusion.6
  26.3 3.4 %collective-permute-start.8 = (bf16[2,256,256]{2,1,0:T(8,128)(2,1)}, bf16[2,256,256]{2,1,0:T(8,128)(2,1)S(1)}, u32[]{:S(2)}, u32[]{:S(2)}) collective-permute-start(bf16[2,256,256]{2,1,0:T(8,128)(2,1)} %get-tuple-element.67), channel_id=1, source_target_pairs={{0,4},{4,8},{8,12},{12,16},{16,20},{20,24},{24,28},{28,32},{32,36}... | collective-permute-start | bytes 786440 | tf_op jit(solution)/shard_map/ppermute | solution.py:29
  29.7 2.5 %collective-permute-start.9 = (bf16[2,256,256]{2,1,0:T(8,128)(2,1)}, bf16[2,256,256]{2,1,0:T(8,128)(2,1)S(1)}, u32[]{:S(2)}, u32[]{:S(2)}) collective-permute-start(bf16[2,256,256]{2,1,0:T(8,128)(2,1)} %get-tuple-element.66), channel_id=1, source_target_pairs={{4,0},{8,4},{12,8},{16,12},{20,16},{24,20},{28,24},{32,28},{36,32}... | collective-permute-start | bytes 786440 | tf_op jit(solution)/shard_map/ppermute | solution.py:30
  32.4 0.2 reshape.452
  33.0 0.3 fusion.39
  33.4 1.0 select_reduce_fusion
  34.5 0.6 collective-permute-done.7
  35.1 1.1 pad_maximum_fusion
  36.2 2.3 collective-permute-done.8.above_ref
  38.4 2.8 %collective-permute-done.9.below_ref = bf16[2,256,256]{2,1,0:T(8,128)(2,1)S(1)} collective-permute-done((bf16[2,256,256]{2,1,0:T(8,128)(2,1)}, bf16[2,256,256]{2,1,0:T(8,128)(2,1)S(1)}, u32[]{:S(2)}, u32[]{:S(2)}) %collective-permute-start.9) | collective-permute-done | bytes 262176 | tf_op jit(solution)/shard_map/ppermute | solution.py:30
  41.2 1.1 all-to-all-done.4
  42.3 3.7 %fusion.32 = bf16[1792,256]{1,0:T(8,128)(2,1)} fusion(bf16[2048,256]{1,0:T(8,128)(2,1)S(1)} %pad_maximum_fusion, s32[1792]{0:T(1024)S(1)} %eq.153), kind=kOutput, calls=%fused_computation.72 | convolution fusion | flops 1883176960 | bytes 1973248 | tf_op jit(solution)/shard_map/dot_general | solution.py:388
  46.0 15.2 %all-to-all-start.5 = ((bf16[16,112,256]{2,1,0:T(8,128)(2,1)}), bf16[16,112,256]{2,1,0:T(8,128)(2,1)S(1)}, u32[]{:S(2)}, u32[]{:S(2)}) async-start(bf16[16,112,256]{2,1,0:T(8,128)(2,1)} %bitcast.104), calls=%async_computation.5 | async-start | bytes 1835008 | tf_op jit(solution)/shard_map/all_to_all | solution.py:35
  61.3 0.3 fusion.40
  61.7 12.2 %all-to-all-done.5 = bf16[16,112,256]{2,1,0:T(8,128)(2,1)S(1)} async-done(((bf16[16,112,256]{2,1,0:T(8,128)(2,1)}), bf16[16,112,256]{2,1,0:T(8,128)(2,1)S(1)}, u32[]{:S(2)}, u32[]{:S(2)}) %all-to-all-start.5) | async-done | bytes 917536 | tf_op jit(solution)/shard_map/all_to_all | solution.py:35
  73.9 1.4 fusion.35
  75.4 1.9 fusion.34
  77.3 0.7 shard_map.46.source_ref
  78.0 0.9 copy-done.7
  79.0 2.1 shard_map.48
  81.1 1.9 collective-permute-start.11
  83.1 3.9 %collective-permute-start.12 = (bf16[2,256,256]{2,1,0:T(8,128)(2,1)S(1)}, bf16[2,256,256]{2,1,0:T(8,128)(2,1)S(1)}, u32[]{:S(2)}, u32[]{:S(2)}) collective-permute-start(bf16[2,256,256]{2,1,0:T(8,128)(2,1)S(1)} %get-tuple-element.64), channel_id=1, source_target_pairs={{4,0},{8,4},{12,8},{16,12},{20,16},{24,20},{28,24},{32,28},{36,32}... | collective-permute-start | bytes 786440 | tf_op jit(solution)/shard_map/ppermute | solution.py:30
  87.0 4.7 %collective-permute-done.11.above_ref = bf16[2,256,256]{2,1,0:T(8,128)(2,1)S(1)} collective-permute-done((bf16[2,256,256]{2,1,0:T(8,128)(2,1)S(1)}, bf16[2,256,256]{2,1,0:T(8,128)(2,1)S(1)}, u32[]{:S(2)}, u32[]{:S(2)}) %collective-permute-start.11) | collective-permute-done | bytes 262176 | tf_op jit(solution)/shard_map/ppermute | solution.py:29
  91.7 1.9 collective-permute-done.12.below_ref
  93.7 2.1 shard_map.49
  95.8 1.3 collective-permute-start.13
  97.1 0.9 shard_map.47.turned_ref
  98.0 1.6 collective-permute-done.13.returned_ref
  99.6 4.6 %shard_map.50 = s16[16,19,16,256]{3,2,1,0:T(8,128)(2,1)} custom-call(s32[1]{0:T(128)} %bitcast.25.section_ref, bf16[3,256,2048]{2,1,0:T(8,128)(2,1)S(1)} %shard_map.47.turned_ref, f32[2,512,256]{2,1,0:T(8,128)S(1)} %get-tuple-element.33.pre_ref, bf16[2,512,256]{2,1,0:T(8,128)(2,1)S(1)} %get-tuple-element.34.dec_ref, ...), custom_call_target="tpu_custom_call" | custom-call | flops 1811939328 | bytes 8781828 | tf_op jit(solution)/shard_map/pallas_call | solution.py:76
  104.1 16.7 %all-to-all-start.6 = ((s16[16,19,16,256]{3,2,1,0:T(8,128)(2,1)}), s16[16,19,16,256]{3,2,1,0:T(8,128)(2,1)S(1)}, u32[]{:S(2)}, u32[]{:S(2)}) async-start(s16[16,19,16,256]{3,2,1,0:T(8,128)(2,1)} %shard_map.50), calls=%async_computation.6 | async-start | bytes 4980736 | tf_op jit(solution)/shard_map/all_to_all | solution.py:35
  120.9 1.8 convert_reduce_fusion.1
  122.7 1.4 reduce_max.27
  124.8 29.5 %all-to-all-done.6.packed_ref = s16[16,19,16,256]{3,2,1,0:T(8,128)(2,1)S(1)} async-done(((s16[16,19,16,256]{3,2,1,0:T(8,128)(2,1)}), s16[16,19,16,256]{3,2,1,0:T(8,128)(2,1)S(1)}, u32[]{:S(2)}, u32[]{:S(2)}) %all-to-all-start.6) | async-done | bytes 2490400 | tf_op jit(solution)/shard_map/all_to_all | solution.py:35
  154.3 0.8 shard_map.51
  155.1 19.3 %all_to_all.51.parts_ref = s16[8,80,128]{2,1,0:T(8,128)(2,1)} all-to-all(s16[8,80,128]{2,1,0:T(8,128)(2,1)S(1)} %shard_map.51), channel_id=1, replica_groups=mesh['section'=2,'zh'=2,'y'=4,'x'=4,'dp'=4] {'zh','dp'}, dimensions={0} | all-to-all | bytes 327680 | tf_op jit(solution)/shard_map/all_to_all | solution.py:35
  174.4 1.8 shard_map.52
  176.2 3.4 %all-to-all-start.8 = ((s16[8,80,128]{2,1,0:T(8,128)(2,1)}), s16[8,80,128]{2,1,0:T(8,128)(2,1)S(1)}, u32[]{:S(2)}, u32[]{:S(2)}) async-start(s16[8,80,128]{2,1,0:T(8,128)(2,1)} %shard_map.52), calls=%async_computation.8 | async-start | bytes 327680 | tf_op jit(solution)/shard_map/all_to_all | solution.py:35
  179.6 9.3 %all-to-all-done.8 = s16[8,80,128]{2,1,0:T(8,128)(2,1)S(1)} async-done(((s16[8,80,128]{2,1,0:T(8,128)(2,1)}), s16[8,80,128]{2,1,0:T(8,128)(2,1)S(1)}, u32[]{:S(2)}, u32[]{:S(2)}) %all-to-all-start.8) | async-done | bytes 163872 | tf_op jit(solution)/shard_map/all_to_all | solution.py:35
  188.9 0.6 slice_reduce_fusion
  190.2 0.3 conditional.1
  190.5 0.5 broadcast_in_dim.81
  191.0 37.6 %all_to_all.52.plane_ref = s16[16,8,80,128]{3,2,1,0:T(8,128)(2,1)S(1)} all-to-all(s16[16,8,80,128]{3,2,1,0:T(8,128)(2,1)S(1)} %broadcast_in_dim.81), channel_id=1, replica_groups=mesh['section'=2,'zh'=2,'y'=4,'x'=4,'dp'=4] {'y','x'}, dimensions={0} | all-to-all | bytes 5242880 | tf_op jit(solution)/shard_map/all_to_all | solution.py:35
  228.6 2.7 %shard_map.53 = f32[2,3,3,256,256]{4,3,2,1,0:T(8,128)} custom-call(s16[16,8,80,128]{3,2,1,0:T(8,128)(2,1)S(1)} %all_to_all.52.plane_ref), custom_call_target="tpu_custom_call" | custom-call | tf_op jit(solution)/shard_map/pallas_call | solution.py:342
  (29 shorter events, 1.0 us)
Async XLA Ops:
  6.5 18.9 %copy-start = (bf16[1,2,4,2,64,256]{5,4,3,2,1,0:T(8,128)(2,1)S(1)}, bf16[1,2,4,2,64,256]{5,4,3,2,1,0:T(8,128)(2,1)}, u32[]{:S(2)}) copy-start(bf16[1,2,4,2,64,256]{5,4,3,2,1,0:T(8,128)(2,1)} %param.6) | copy-start | bytes 1572868
  7.6 24.6 %copy-start.3 = (s32[64,4,2,64]{3,2,1,0:T(2,128)S(1)}, s32[64,4,2,64]{3,2,1,0:T(2,128)}, u32[]{:S(2)}) copy-start(s32[64,4,2,64]{3,2,1,0:T(2,128)} %param.9) | copy-start | bytes 393220
  7.6 25.7 %collective-permute-start.6 = (bf16[512,256]{1,0:T(8,128)(2,1)S(1)}, bf16[512,256]{1,0:T(8,128)(2,1)S(1)}, u32[]{:S(2)}, u32[]{:S(2)}) collective-permute-start(bf16[512,256]{1,0:T(8,128)(2,1)S(1)} %constant_dynamic-slice_fusion.1), channel_id=1, source_target_pairs={{0,64},{64,0},{1,65},{65,1},{2,66},{66,2},{3,67},{67,3},{4,68},{68... | collective-permute-start | bytes 786440 | tf_op jit(solution)/shard_map/ppermute | solution.py:362
  17.6 17.5 %copy-start.1 = (bf16[1024,256]{1,0:T(8,128)(2,1)S(1)}, bf16[1024,256]{1,0:T(8,128)(2,1)}, u32[]{:S(2)}) copy-start(bf16[1024,256]{1,0:T(8,128)(2,1)} %param.8) | copy-start | bytes 1572868
  17.6 24.7 %all-to-all-start.4 = ((bf16[32,32,256]{2,1,0:T(8,128)(2,1)}), bf16[32,32,256]{2,1,0:T(8,128)(2,1)}, u32[]{:S(2)}, u32[]{:S(2)}) async-start(bf16[32,32,256]{2,1,0:T(8,128)(2,1)} %copy.66), calls=%async_computation.4 | async-start | bytes 1048576 | tf_op jit(solution)/shard_map/all_to_all | solution.py:35
  26.3 12.1 %collective-permute-start.8 = (bf16[2,256,256]{2,1,0:T(8,128)(2,1)}, bf16[2,256,256]{2,1,0:T(8,128)(2,1)S(1)}, u32[]{:S(2)}, u32[]{:S(2)}) collective-permute-start(bf16[2,256,256]{2,1,0:T(8,128)(2,1)} %get-tuple-element.67), channel_id=1, source_target_pairs={{0,4},{4,8},{8,12},{12,16},{16,20},{20,24},{24,28},{28,32},{32,36}... | collective-permute-start | bytes 786440 | tf_op jit(solution)/shard_map/ppermute | solution.py:29
  29.7 11.5 %collective-permute-start.9 = (bf16[2,256,256]{2,1,0:T(8,128)(2,1)}, bf16[2,256,256]{2,1,0:T(8,128)(2,1)S(1)}, u32[]{:S(2)}, u32[]{:S(2)}) collective-permute-start(bf16[2,256,256]{2,1,0:T(8,128)(2,1)} %get-tuple-element.66), channel_id=1, source_target_pairs={{4,0},{8,4},{12,8},{16,12},{20,16},{24,20},{28,24},{32,28},{36,32}... | collective-permute-start | bytes 786440 | tf_op jit(solution)/shard_map/ppermute | solution.py:30
  32.8 28.5 %copy-start.5 = (s32[33,1024]{1,0:T(8,128)}, s32[33,1024]{1,0:T(8,128)S(1)}, u32[]{:S(2)}) copy-start(s32[33,1024]{1,0:T(8,128)S(1)} %fusion.43) | copy-start | bytes 405508
  33.3 1.1 copy-start.6
  33.3 1.8 collective-permute-start.7
  46.0 27.9 %all-to-all-start.5 = ((bf16[16,112,256]{2,1,0:T(8,128)(2,1)}), bf16[16,112,256]{2,1,0:T(8,128)(2,1)S(1)}, u32[]{:S(2)}, u32[]{:S(2)}) async-start(bf16[16,112,256]{2,1,0:T(8,128)(2,1)} %bitcast.104), calls=%async_computation.5 | async-start | bytes 1835008 | tf_op jit(solution)/shard_map/all_to_all | solution.py:35
  75.3 2.1 collective-permute-start.10
  77.3 1.7 copy-start.7
  81.1 10.6 %collective-permute-start.11 = (bf16[2,256,256]{2,1,0:T(8,128)(2,1)S(1)}, bf16[2,256,256]{2,1,0:T(8,128)(2,1)S(1)}, u32[]{:S(2)}, u32[]{:S(2)}) collective-permute-start(bf16[2,256,256]{2,1,0:T(8,128)(2,1)S(1)} %get-tuple-element.65), channel_id=1, source_target_pairs={{0,4},{4,8},{8,12},{12,16},{16,20},{20,24},{24,28},{28,32},{32,36}... | collective-permute-start | bytes 786440 | tf_op jit(solution)/shard_map/ppermute | solution.py:29
  83.1 10.6 %collective-permute-start.12 = (bf16[2,256,256]{2,1,0:T(8,128)(2,1)S(1)}, bf16[2,256,256]{2,1,0:T(8,128)(2,1)S(1)}, u32[]{:S(2)}, u32[]{:S(2)}) collective-permute-start(bf16[2,256,256]{2,1,0:T(8,128)(2,1)S(1)} %get-tuple-element.64), channel_id=1, source_target_pairs={{4,0},{8,4},{12,8},{16,12},{20,16},{24,20},{28,24},{32,28},{36,32}... | collective-permute-start | bytes 786440 | tf_op jit(solution)/shard_map/ppermute | solution.py:30
  95.8 3.8 %collective-permute-start.13 = (bf16[2,2,256,256]{3,2,1,0:T(8,128)(2,1)S(1)}, bf16[2,2,256,256]{3,2,1,0:T(8,128)(2,1)S(1)}, u32[]{:S(2)}, u32[]{:S(2)}) collective-permute-start(bf16[2,2,256,256]{3,2,1,0:T(8,128)(2,1)S(1)} %shard_map.49), channel_id=1, source_target_pairs={{128,0},{129,1},{130,2},{131,3},{132,4},{133,5},{134,6},{135,7},{1... | collective-permute-start | bytes 1572872 | tf_op jit(solution)/shard_map/ppermute | solution.py:478
  104.1 50.1 %all-to-all-start.6 = ((s16[16,19,16,256]{3,2,1,0:T(8,128)(2,1)}), s16[16,19,16,256]{3,2,1,0:T(8,128)(2,1)S(1)}, u32[]{:S(2)}, u32[]{:S(2)}) async-start(s16[16,19,16,256]{3,2,1,0:T(8,128)(2,1)} %shard_map.50), calls=%async_computation.6 | async-start | bytes 4980736 | tf_op jit(solution)/shard_map/all_to_all | solution.py:35
  176.2 12.7 %all-to-all-start.8 = ((s16[8,80,128]{2,1,0:T(8,128)(2,1)}), s16[8,80,128]{2,1,0:T(8,128)(2,1)S(1)}, u32[]{:S(2)}, u32[]{:S(2)}) async-start(s16[8,80,128]{2,1,0:T(8,128)(2,1)} %shard_map.52), calls=%async_computation.8 | async-start | bytes 327680 | tf_op jit(solution)/shard_map/all_to_all | solution.py:35

commit v7 on v5

--- a/solution.py
+++ b/solution.py
@@ -85,45 +85,56 @@
     )(*args)
 
 
-def shift_source(section, pair, other, own, above, below, across):
-    frames, rows, count, channels = own.shape
-
-    def body(section_ref, pair_ref, other_ref, own_ref, above_ref, below_ref, out_ref):
-        def write(frame, row, block):
-            for tap in range(3):
-                out_ref[tap, frame, row] = shifted_columns(block, across, tap)
-
-        @pl.when(section_ref[0] == 0)
+def shift_source(section, pair, other, across):
+    frames, rows, count, channels = pair.shape
+
+    def body(section_ref, pair_ref, other_ref, out_ref):
+        @pl.when(section_ref[0] == 1)
         def _():
             for frame in range(frames):
-                write(frame, 0, above_ref[frame])
                 for row in range(rows):
-                    write(frame, row + 1, own_ref[frame, row])
-                write(frame, rows + 1, below_ref[frame])
-
-        @pl.when(section_ref[0] == 1)
-        def _():
-            for frame in range(frames):
-                for row in range(2):
-                    write(frame, row, other_ref[frame, row])
-                    write(frame, row + 2, pair_ref[frame, row])
-
-    out = jax.ShapeDtypeStruct((3, frames, rows + 2, count, channels), BF16)
-    return call(body, [out], section, pair, other, own, above, below)[0]
-
-
-def turn_source(section, source):
+                    for tap in range(3):
+                        block = shifted_columns(other_ref[frame, row], across, tap)
+                        out_ref[tap, frame, row] = block
+                        block = shifted_columns(pair_ref[frame, row], across, tap)
+                        out_ref[tap, frame, rows + row] = block
+
+    out = jax.ShapeDtypeStruct((3, frames, 2 * rows, count, channels), BF16)
+    return call(body, [out], section, pair, other)[0]
+
+
+def rimmed_block(frame, row, above_ref, cells_ref, below_ref):
+    rows = cells_ref.shape[1]
+    if row == 0:
+        return above_ref[frame]
+    return below_ref[frame] if row > rows else cells_ref[frame, row - 1]
+
+
+def turn_source(section, source, cells, above, below, across):
     taps, frames, rows, count, channels = source.shape
 
-    def body(section_ref, source_ref, out_ref):
-        for tap in range(taps):
+    def body(section_ref, source_ref, cells_ref, above_ref, below_ref, out_ref):
+        def write(block_of):
             for frame in range(frames):
                 for row in range(rows):
                     start = (frame * rows + row) * count
-                    out_ref[tap, :, start : start + count] = source_ref[tap, frame, row].T
+                    for tap in range(taps):
+                        out_ref[tap, :, start : start + count] = block_of(tap, frame, row).T
+
+        def encoder_block(tap, frame, row):
+            block = rimmed_block(frame, row, above_ref, cells_ref, below_ref)
+            return shifted_columns(block, across, tap)
+
+        @pl.when(section_ref[0] == 0)
+        def _():
+            write(encoder_block)
+
+        @pl.when(section_ref[0] == 1)
+        def _():
+            write(lambda tap, frame, row: source_ref[tap, frame, row])
 
     out = jax.ShapeDtypeStruct((taps, channels, frames * rows * count), BF16)
-    return call(body, [out], section, source)[0]
+    return call(body, [out], section, source, cells, above, below)[0]
 
 
 def tap_index(section_ref, row_tap, column_tap):
@@ -131,73 +142,95 @@
     return jnp.where(decoder, column_tap, row_tap), jnp.where(decoder, row_tap, column_tap)
 
 
-def convolve(section, source, kernel, cotangent):
-    _, frames, rimmed, count, channels = source.shape
+def convolved(section_ref, source_ref, kernel_ref, frame):
+    _, _, rimmed, count, channels = source_ref.shape
     rows = rimmed - 2
-    span = rows * count
-
-    def body(section_ref, source_ref, kernel_ref, cot_ref, pre_ref, grad_ref):
-        for frame in range(frames):
-            acc = jnp.zeros((span, channels), F32)
-            for r in range(3):
-                for q in range(3):
-                    i, j = tap_index(section_ref, r, q)
-                    for back in range(frame + 1):
-                        cells = source_ref[q, frame - back, r : r + rows].reshape(span, channels)
-                        acc += jnp.dot(
-                            cells, kernel_ref[1 - back, i, j], preferred_element_type=F32
-                        )
-            pre_ref[frame] = acc
-            grad_ref[frame] = (cot_ref[frame].astype(F32) * silu_slope(acc)).astype(BF16)
-
-    shape = (frames, span, channels)
+    acc = jnp.zeros((rows * count, channels), F32)
+    for r in range(3):
+        for q in range(3):
+            i, j = tap_index(section_ref, r, q)
+            for back in range(frame + 1):
+                cells = source_ref[q, frame - back, r : r + rows].reshape(rows * count, channels)
+                acc += jnp.dot(cells, kernel_ref[1 - back, i, j], preferred_element_type=F32)
+    return acc
+
+
+def decoder_grad(section, source, kernel, cotangent, own):
+    frames, rows, count, channels = own.shape
+
+    def body(section_ref, source_ref, kernel_ref, cot_ref, own_ref, out_ref):
+        @pl.when(section_ref[0] == 0)
+        def _():
+            out_ref[...] = own_ref[...]
+
+        @pl.when(section_ref[0] == 1)
+        def _():
+            for frame in range(frames):
+                slope = silu_slope(convolved(section_ref, source_ref, kernel_ref, frame))
+                grad = (cot_ref[frame].astype(F32) * slope).astype(BF16)
+                out_ref[frame] = grad.reshape(rows, count, channels)
+
     return call(
         body,
-        [jax.ShapeDtypeStruct(shape, F32), jax.ShapeDtypeStruct(shape, BF16)],
+        [jax.ShapeDtypeStruct(own.shape, BF16)],
         section,
         source,
         kernel,
         cotangent,
-        flops=54 * span * channels * channels,
-    )
-
-
-def convolve_back(section, grad, above, below, kernel, across):
-    frames, rows, count, channels = grad.shape
+        own,
+        flops=54 * rows * count * channels * channels,
+    )[0]
+
+
+def back_and_forth(section, cells, above, below, kernel, across):
+    frames, rows, count, channels = cells.shape
     span = rows * count
 
-    def body(section_ref, grad_ref, above_ref, below_ref, kernel_ref, out_ref, shifted):
+    def body(
+        section_ref, cells_ref, above_ref, below_ref, kernel_ref, back_ref, pre_ref, shifted
+    ):
         for frame in range(frames):
-            blocks = [above_ref[frame]] + [grad_ref[frame, r] for r in range(rows)]
-            for row, block in enumerate(blocks + [below_ref[frame]]):
+            for row in range(rows + 2):
+                block = rimmed_block(frame, row, above_ref, cells_ref, below_ref)
                 for tap in range(3):
                     shifted[tap, frame, row] = shifted_columns(block, across, tap)
-        for frame in range(frames):
-            acc = jnp.zeros((span, channels), F32)
-            for r in range(3):
-                for q in range(3):
-                    i, j = tap_index(section_ref, r, q)
-                    for ahead in range(frames - frame):
-                        cells = shifted[2 - q, frame + ahead, 2 - r : 2 - r + rows]
-                        acc += lax.dot_general(
-                            cells.reshape(span, channels),
-                            kernel_ref[1 - ahead, i, j],
-                            (((1,), (1,)), ((), ())),
-                            preferred_element_type=F32,
-                        )
-            out_ref[frame] = acc.astype(BF16).reshape(rows, count, channels)
+
+        @pl.when(section_ref[0] == 0)
+        def _():
+            for frame in range(frames):
+                pre_ref[frame] = convolved(section_ref, shifted, kernel_ref, frame)
+
+        @pl.when(section_ref[0] == 1)
+        def _():
+            for frame in range(frames):
+                acc = jnp.zeros((span, channels), F32)
+                for r in range(3):
+                    for q in range(3):
+                        i, j = tap_index(section_ref, r, q)
+                        for ahead in range(frames - frame):
+                            grads = shifted[2 - q, frame + ahead, 2 - r : 2 - r + rows]
+                            acc += lax.dot_general(
+                                grads.reshape(span, channels),
+                                kernel_ref[1 - ahead, i, j],
+                                (((1,), (1,)), ((), ())),
+                                preferred_element_type=F32,
+                            )
+                back_ref[frame] = acc.astype(BF16).reshape(rows, count, channels)
 
     return call(
         body,
-        [jax.ShapeDtypeStruct(grad.shape, BF16)],
+        [
+            jax.ShapeDtypeStruct(cells.shape, BF16),
+            jax.ShapeDtypeStruct((frames, span, channels), F32),
+        ],
         section,
-        grad,
+        cells,
         above,
         below,
         kernel,
         flops=54 * span * channels * channels,
         scratch=[pltpu.VMEM((3, frames, rows + 2, count, channels), BF16)],
-    )[0]
+    )
 
 
 def kernel_grads(section, turned, pre_act, dec_grad, returned, pair, other, parts):
@@ -222,7 +255,7 @@
 
         @pl.when(section_ref[0] == 1)
         def _():
-            side[...] = dec_ref[...]
+            side[...] = dec_ref[...].reshape(frames, span, channels)
 
         top = jnp.zeros((8, channels), F32)
         for r in range(3):
@@ -349,7 +382,7 @@
     )(plane)
 
 
-def routed(codebook, shifted, holder, slots, turned, above, below):
+def routed(codebook, shifted, holder, slots, turned):
     section_id = lax.axis_index("section")
     slab_id = lax.axis_index(SLAB)
     near = lax.axis_index("zh")
@@ -388,7 +421,6 @@
     words = jnp.dot(picks, table, preferred_element_type=F32).astype(BF16)
     looked = exchange(words.reshape(planes, slots, channels), PLANE)
     looked = looked.reshape(planes * slots, channels)
-    looked, above, below = lax.optimization_barrier((looked, above, below))
 
     own_wanted = lax.dynamic_index_in_dim(shifted, slab_id + section_id, 0, keepdims=False)
     own_holder = lax.dynamic_index_in_dim(holder, slab_id + section_id, 0, keepdims=False)
@@ -400,7 +432,7 @@
         order[:, None] == lax.broadcasted_iota(jnp.int32, (1, planes * slots), 1)
     ).astype(BF16)
     pair = jnp.dot(gather, looked, preferred_element_type=F32).astype(BF16)
-    return pair, turned, above, below
+    return pair, turned
 
 
 def front(own_field, codebook, codes, whole):
@@ -420,7 +452,6 @@
     turned = exchange(turned, SLAB).reshape(positions, channels)
 
     own = jnp.transpose(own_field, (2, 0, 1, 3, 4)).reshape(cells)
-    above, below = neighbours(own[:, -1], own[:, 0])
 
     edge = jnp.full((1,) + codes.shape[1:], -1, codes.dtype)
     shifted = jnp.concatenate([edge, codes, edge], axis=0)
@@ -434,9 +465,7 @@
         taken = jnp.take(every, jnp.maximum(wanted, 0), axis=0)
         pair = jnp.where(wanted[:, None] >= 0, taken, 0).astype(BF16)
     else:
-        pair, turned, above, below = routed(
-            codebook, shifted, holder, slots, turned, above, below
-        )
+        pair, turned = routed(codebook, shifted, holder, slots, turned)
 
     place = lax.broadcasted_iota(jnp.int32, (positions, 1), 0)
     group, column = place // across, place % across
@@ -455,8 +484,6 @@
         other.reshape(cells),
         cotangent.reshape(frame_count, -1, channels),
         own,
-        above,
-        below,
         crowded,
     )
 
@@ -467,22 +494,19 @@
     own_field = fields[0]
     kernel = kernels[0]
     row_count, batch_count, frame_count, across, channels = own_field.shape
-    cells = (frame_count, row_count, batch_count * across, channels)
-    pair, other, cotangent, own, above, below, crowded = front(own_field, codebook, codes, whole)
-    source = shift_source(section, pair, other, own, above, below, across)
-    pre_act, dec_grad = convolve(section, source, kernel, cotangent)
-
-    shaped = dec_grad.reshape(cells)
-    above, below = neighbours(shaped[:, -1], shaped[:, 0])
-    source = turn_source(section, source)
-    back_dec = convolve_back(section, shaped, above, below, kernel, across)
+    pair, other, cotangent, own, crowded = front(own_field, codebook, codes, whole)
+    source = shift_source(section, pair, other, across)
+    cells = decoder_grad(section, source, kernel, cotangent, own)
+    above, below = neighbours(cells[:, -1], cells[:, 0])
+    back_dec, pre_act = back_and_forth(section, cells, above, below, kernel, across)
+    source = turn_source(section, source, cells, above, below, across)
     returned = lax.ppermute(back_dec, "section", [(1, 0)])
 
     total = (
         row_count * slabs * across * batch_count * lax.axis_size("dp") * frame_count
     )
     packed = kernel_grads(
-        section, source, pre_act, dec_grad, returned, pair, other, lax.axis_size(PLANE)
+        section, source, pre_act, cells, returned, pair, other, lax.axis_size(PLANE)
     )
     plane = exchange(packed, PLANE)
     line = exchange(sum_plane(crowded, plane, lax.axis_size(Z)), Z)

time: 232 us -> 225 us (0.970)
  starting transfers between devices: 53.8 us -> 47.1 us
  waiting for transfers between devices: 71.6 us -> 74.7 us
  Pallas kernels: 15.7 us -> 13.3 us
    all_to_all x4, waiting for transfers between devices: 52.1 us -> 65.8 us  [exchange(): return lax.all_to_all(cells, axes, split_axis=0, concat_axis=0, tiled=True)]
    ppermute x2 -> x1, waiting for transfers between devices: 12.2 us -> 3.2 us  [neighbours(): above = lax.ppermute(lower, SLAB, [(i, i + 1) for i in range(count - 1)])]
    ppermute x2 -> x1, starting transfers between devices: 6.43 us -> 1.92 us  [neighbours(): above = lax.ppermute(lower, SLAB, [(i, i + 1) for i in range(count - 1)])]
    pallas_call x5, Pallas kernels: 10.4 us -> 8.04 us  [call(): pl.pallas_call(body, in_specs=[pl.BlockSpec(memory_space=pltpu.SMEM)] + [...]
    ppermute x2 -> x1, starting transfers between devices: 5.26 us -> 4.11 us  [neighbours(): below = lax.ppermute(upper, SLAB, [(i + 1, i) for i in range(count - 1)])]
  transfers between devices with their start and end apart: 12 -> 10, of which waited for: 11 -> 9; matrix products, arithmetic and copies ran while one was open for 5% -> 4% of each run, Pallas kernels for 0% -> 0%
where the time goes in v7:
time: 225 us; the launch traced here: 224 us
  waiting for transfers between devices  74.7 us (33%)
  blocking collectives  57.3 us (25%)
  starting transfers between devices  47.1 us (21%)
  between operations  15 us (7%)
  Pallas kernels  13.3 us (6%)
  matrix products  6.63 us (3%)
  other arithmetic  5.3 us (2%)
  local copies, waits for them, and re-layouts  4.72 us (2%)
    all_to_all x4, waiting for transfers between devices, exchange(): return lax.all_to_all(cells, axes, split_axis=0, concat_axis=0, tiled=True)  65.8 us
    all_to_all x2, blocking collectives, exchange(): return lax.all_to_all(cells, axes, split_axis=0, concat_axis=0, tiled=True)  57.3 us
    all_to_all x4, starting transfers between devices, exchange(): return lax.all_to_all(cells, axes, split_axis=0, concat_axis=0, tiled=True)  32.3 us
    pallas_call x5, Pallas kernels, call(): pl.pallas_call(body, in_specs=[pl.BlockSpec(memory_space=pltpu.SMEM)] + [...  8.04 us
    ppermute x1, starting transfers between devices, routed(): lax.ppermute(lax.dynamic_slice_in_dim(codebook, section_id * half, half,...  7.28 us
  transfers between devices with their start and end apart: 10, of which 9 were waited for; matrix products, arithmetic and copies ran while one was open for 4% of the time, Pallas kernels for 0%

profile of v7, /device:TPU:2, one launch (start us, length us, event | category | flops | bytes accessed | tf_op | source)
XLA Modules:
  0.0 224.2 jit_solution(4168303355282097217)
XLA Ops:
  6.5 1.0 constant_dynamic-slice_fusion.1
  7.6 7.3 %collective-permute-start.4 = (bf16[512,256]{1,0:T(8,128)(2,1)S(1)}, bf16[512,256]{1,0:T(8,128)(2,1)S(1)}, u32[]{:S(2)}, u32[]{:S(2)}) collective-permute-start(bf16[512,256]{1,0:T(8,128)(2,1)S(1)} %constant_dynamic-slice_fusion.1), channel_id=1, source_target_pairs={{0,64},{64,0},{1,65},{65,1},{2,66},{66,2},{3,67},{67,3},{4,68},{68... | collective-permute-start | bytes 786440 | tf_op jit(solution)/shard_map/ppermute | solution.py:395
  14.8 1.6 copy.57
  16.4 0.1 copy.58
  16.5 1.1 copy.59
  17.6 7.6 %all-to-all-start.4 = ((bf16[32,32,256]{2,1,0:T(8,128)(2,1)}), bf16[32,32,256]{2,1,0:T(8,128)(2,1)S(1)}, u32[]{:S(2)}, u32[]{:S(2)}) async-start(bf16[32,32,256]{2,1,0:T(8,128)(2,1)} %copy.59), calls=%async_computation.4 | async-start | bytes 1048576 | tf_op jit(solution)/shard_map/all_to_all | solution.py:35
  25.2 0.1 pad_add_fusion.1
  25.4 0.1 copy.76
  25.5 0.2 reshape.446
  25.7 0.2 fusion.43
  25.9 0.1 fusion.48
  26.0 0.3 fusion.39
  26.3 0.1 collective-permute-start.5
  26.4 1.0 select_reduce_fusion
  27.4 0.1 eq.153
  27.5 0.5 collective-permute-done.5
  28.0 14.0 %all-to-all-done.4 = bf16[32,32,256]{2,1,0:T(8,128)(2,1)S(1)} async-done(((bf16[32,32,256]{2,1,0:T(8,128)(2,1)}), bf16[32,32,256]{2,1,0:T(8,128)(2,1)S(1)}, u32[]{:S(2)}, u32[]{:S(2)}) %all-to-all-start.4) | async-done | bytes 524320 | tf_op jit(solution)/shard_map/all_to_all | solution.py:35
  42.1 3.7 %fusion.32 = bf16[1792,256]{1,0:T(8,128)(2,1)} fusion(bf16[2048,256]{1,0:T(8,128)(2,1)S(1)} %pad_maximum_fusion, s32[1792]{0:T(1024)S(1)} %eq.153), kind=kOutput, calls=%fused_computation.70 | convolution fusion | flops 1883176960 | bytes 1973248 | tf_op jit(solution)/shard_map/dot_general | solution.py:421
  45.8 5.0 %all-to-all-start.5 = ((bf16[16,112,256]{2,1,0:T(8,128)(2,1)}), bf16[16,112,256]{2,1,0:T(8,128)(2,1)S(1)}, u32[]{:S(2)}, u32[]{:S(2)}) async-start(bf16[16,112,256]{2,1,0:T(8,128)(2,1)} %bitcast.27), calls=%async_computation.5 | async-start | bytes 1835008 | tf_op jit(solution)/shard_map/all_to_all | solution.py:35
  50.9 0.3 fusion.40
  51.2 12.8 %all-to-all-done.5 = bf16[16,112,256]{2,1,0:T(8,128)(2,1)S(1)} async-done(((bf16[16,112,256]{2,1,0:T(8,128)(2,1)}), bf16[16,112,256]{2,1,0:T(8,128)(2,1)S(1)}, u32[]{:S(2)}, u32[]{:S(2)}) %all-to-all-start.5) | async-done | bytes 917536 | tf_op jit(solution)/shard_map/all_to_all | solution.py:35
  64.0 1.4 fusion.35
  65.4 0.1 collective-permute-start.6
  65.6 0.8 fusion.34
  66.4 1.0 collective-permute-done.6
  67.5 1.9 collective-permute-start.7
  69.4 4.1 %collective-permute-start.8 = (bf16[2,256,256]{2,1,0:T(8,128)(2,1)S(1)}, bf16[2,256,256]{2,1,0:T(8,128)(2,1)S(1)}, u32[]{:S(2)}, u32[]{:S(2)}) collective-permute-start(bf16[2,256,256]{2,1,0:T(8,128)(2,1)S(1)} %get-tuple-element.58), channel_id=1, source_target_pairs={{4,0},{8,4},{12,8},{16,12},{20,16},{24,20},{28,24},{32,28},{36,32}... | collective-permute-start | bytes 786440 | tf_op jit(solution)/shard_map/ppermute | solution.py:30
  73.6 3.2 %collective-permute-done.7.above_ref = bf16[2,256,256]{2,1,0:T(8,128)(2,1)S(1)} collective-permute-done((bf16[2,256,256]{2,1,0:T(8,128)(2,1)S(1)}, bf16[2,256,256]{2,1,0:T(8,128)(2,1)S(1)}, u32[]{:S(2)}, u32[]{:S(2)}) %collective-permute-start.7) | collective-permute-done | bytes 262176 | tf_op jit(solution)/shard_map/ppermute | solution.py:29
  76.8 2.1 collective-permute-done.8.below_ref
  78.9 2.5 %shard_map.49 = (bf16[2,2,256,256]{3,2,1,0:T(8,128)(2,1)S(1)}, f32[2,512,256]{2,1,0:T(8,128)S(1)}) custom-call(s32[1]{0:T(128)} %bitcast.21.section_ref, bf16[2,2,256,256]{3,2,1,0:T(8,128)(2,1)S(1)} %shard_map.47.cells_ref.dec_ref, bf16[2,256,256]{2,1,0:T(8,128)(2,1)S(1)} %collective-permute-done.7.above_ref, ...), custom_call_target="tpu_custom_call" | custom-call | flops 1811939328 | bytes 4980740 | tf_op jit(solution)/shard_map/pallas_call | solution.py:76
  81.3 1.3 collective-permute-start.9
  82.6 0.9 shard_map.48.turned_ref
  83.6 2.1 collective-permute-done.9.returned_ref
  85.7 4.6 %shard_map.50 = s16[16,19,16,256]{3,2,1,0:T(8,128)(2,1)} custom-call(s32[1]{0:T(128)} %bitcast.21.section_ref, bf16[3,256,2048]{2,1,0:T(8,128)(2,1)S(1)} %shard_map.48.turned_ref, f32[2,512,256]{2,1,0:T(8,128)S(1)} %get-tuple-element.29.pre_ref, bf16[2,2,256,256]{3,2,1,0:T(8,128)(2,1)S(1)} %shard_map.47.cells_ref.dec_ref, ...), custom_call_target="tpu_custom_call" | custom-call | flops 1811939328 | bytes 8781828 | tf_op jit(solution)/shard_map/pallas_call | solution.py:76
  90.3 16.3 %all-to-all-start.6 = ((s16[16,19,16,256]{3,2,1,0:T(8,128)(2,1)}), s16[16,19,16,256]{3,2,1,0:T(8,128)(2,1)S(1)}, u32[]{:S(2)}, u32[]{:S(2)}) async-start(s16[16,19,16,256]{3,2,1,0:T(8,128)(2,1)} %shard_map.50), calls=%async_computation.6 | async-start | bytes 4980736 | tf_op jit(solution)/shard_map/all_to_all | solution.py:35
  106.6 1.8 convert_reduce_fusion.1
  108.4 1.4 reduce_max.27
  110.4 29.6 %all-to-all-done.6.packed_ref = s16[16,19,16,256]{3,2,1,0:T(8,128)(2,1)S(1)} async-done(((s16[16,19,16,256]{3,2,1,0:T(8,128)(2,1)}), s16[16,19,16,256]{3,2,1,0:T(8,128)(2,1)S(1)}, u32[]{:S(2)}, u32[]{:S(2)}) %all-to-all-start.6) | async-done | bytes 2490400 | tf_op jit(solution)/shard_map/all_to_all | solution.py:35
  140.0 0.8 shard_map.51
  140.8 19.7 %all_to_all.51.parts_ref = s16[8,80,128]{2,1,0:T(8,128)(2,1)} all-to-all(s16[8,80,128]{2,1,0:T(8,128)(2,1)S(1)} %shard_map.51), channel_id=1, replica_groups=mesh['section'=2,'zh'=2,'y'=4,'x'=4,'dp'=4] {'zh','dp'}, dimensions={0} | all-to-all | bytes 327680 | tf_op jit(solution)/shard_map/all_to_all | solution.py:35
  160.5 1.8 shard_map.52
  162.2 3.4 %all-to-all-start.8 = ((s16[8,80,128]{2,1,0:T(8,128)(2,1)}), s16[8,80,128]{2,1,0:T(8,128)(2,1)S(1)}, u32[]{:S(2)}, u32[]{:S(2)}) async-start(s16[8,80,128]{2,1,0:T(8,128)(2,1)} %shard_map.52), calls=%async_computation.8 | async-start | bytes 327680 | tf_op jit(solution)/shard_map/all_to_all | solution.py:35
  165.6 9.3 %all-to-all-done.8 = s16[8,80,128]{2,1,0:T(8,128)(2,1)S(1)} async-done(((s16[8,80,128]{2,1,0:T(8,128)(2,1)}), s16[8,80,128]{2,1,0:T(8,128)(2,1)S(1)}, u32[]{:S(2)}, u32[]{:S(2)}) %all-to-all-start.8) | async-done | bytes 163872 | tf_op jit(solution)/shard_map/all_to_all | solution.py:35
  175.0 0.6 slice_reduce_fusion
  176.3 0.3 conditional.1
  176.6 0.5 broadcast_in_dim.81
  177.1 37.6 %all_to_all.52.plane_ref = s16[16,8,80,128]{3,2,1,0:T(8,128)(2,1)S(1)} all-to-all(s16[16,8,80,128]{3,2,1,0:T(8,128)(2,1)S(1)} %broadcast_in_dim.81), channel_id=1, replica_groups=mesh['section'=2,'zh'=2,'y'=4,'x'=4,'dp'=4] {'y','x'}, dimensions={0} | all-to-all | bytes 5242880 | tf_op jit(solution)/shard_map/all_to_all | solution.py:35
  214.7 2.7 %shard_map.53 = f32[2,3,3,256,256]{4,3,2,1,0:T(8,128)} custom-call(s16[16,8,80,128]{3,2,1,0:T(8,128)(2,1)S(1)} %all_to_all.52.plane_ref), custom_call_target="tpu_custom_call" | custom-call | tf_op jit(solution)/shard_map/pallas_call | solution.py:375
  (21 shorter events, 0.3 us)
Async XLA Ops:
  6.5 18.7 %copy-start.5 = (s32[64,4,2,64]{3,2,1,0:T(2,128)S(1)}, s32[64,4,2,64]{3,2,1,0:T(2,128)}, u32[]{:S(2)}) copy-start(s32[64,4,2,64]{3,2,1,0:T(2,128)} %param.9) | copy-start | bytes 393220
  7.6 18.8 %collective-permute-start.4 = (bf16[512,256]{1,0:T(8,128)(2,1)S(1)}, bf16[512,256]{1,0:T(8,128)(2,1)S(1)}, u32[]{:S(2)}, u32[]{:S(2)}) collective-permute-start(bf16[512,256]{1,0:T(8,128)(2,1)S(1)} %constant_dynamic-slice_fusion.1), channel_id=1, source_target_pairs={{0,64},{64,0},{1,65},{65,1},{2,66},{66,2},{3,67},{67,3},{4,68},{68... | collective-permute-start | bytes 786440 | tf_op jit(solution)/shard_map/ppermute | solution.py:395
  16.4 11.6 %copy-start.3 = (bf16[1024,256]{1,0:T(8,128)(2,1)S(1)}, bf16[1024,256]{1,0:T(8,128)(2,1)}, u32[]{:S(2)}) copy-start(bf16[1024,256]{1,0:T(8,128)(2,1)} %param.8) | copy-start | bytes 1572868
  17.6 24.5 %all-to-all-start.4 = ((bf16[32,32,256]{2,1,0:T(8,128)(2,1)}), bf16[32,32,256]{2,1,0:T(8,128)(2,1)S(1)}, u32[]{:S(2)}, u32[]{:S(2)}) async-start(bf16[32,32,256]{2,1,0:T(8,128)(2,1)} %copy.59), calls=%async_computation.4 | async-start | bytes 1048576 | tf_op jit(solution)/shard_map/all_to_all | solution.py:35
  25.8 25.0 %copy-start.7 = (s32[33,1024]{1,0:T(8,128)}, s32[33,1024]{1,0:T(8,128)S(1)}, u32[]{:S(2)}) copy-start(s32[33,1024]{1,0:T(8,128)S(1)} %fusion.43) | copy-start | bytes 405508
  26.3 1.6 collective-permute-start.5
  45.8 18.2 %all-to-all-start.5 = ((bf16[16,112,256]{2,1,0:T(8,128)(2,1)}), bf16[16,112,256]{2,1,0:T(8,128)(2,1)S(1)}, u32[]{:S(2)}, u32[]{:S(2)}) async-start(bf16[16,112,256]{2,1,0:T(8,128)(2,1)} %bitcast.27), calls=%async_computation.5 | async-start | bytes 1835008 | tf_op jit(solution)/shard_map/all_to_all | solution.py:35
  64.0 1.5 copy-start.2
  65.4 2.0 collective-permute-start.6
  65.6 1.8 copy-start
  67.5 9.2 %collective-permute-start.7 = (bf16[2,256,256]{2,1,0:T(8,128)(2,1)S(1)}, bf16[2,256,256]{2,1,0:T(8,128)(2,1)S(1)}, u32[]{:S(2)}, u32[]{:S(2)}) collective-permute-start(bf16[2,256,256]{2,1,0:T(8,128)(2,1)S(1)} %get-tuple-element.59), channel_id=1, source_target_pairs={{0,4},{4,8},{8,12},{12,16},{16,20},{20,24},{24,28},{28,32},{32,36}... | collective-permute-start | bytes 786440 | tf_op jit(solution)/shard_map/ppermute | solution.py:29
  69.4 9.4 %collective-permute-start.8 = (bf16[2,256,256]{2,1,0:T(8,128)(2,1)S(1)}, bf16[2,256,256]{2,1,0:T(8,128)(2,1)S(1)}, u32[]{:S(2)}, u32[]{:S(2)}) collective-permute-start(bf16[2,256,256]{2,1,0:T(8,128)(2,1)S(1)} %get-tuple-element.58), channel_id=1, source_target_pairs={{4,0},{8,4},{12,8},{16,12},{20,16},{24,20},{28,24},{32,28},{36,32}... | collective-permute-start | bytes 786440 | tf_op jit(solution)/shard_map/ppermute | solution.py:30
  81.3 4.4 %collective-permute-start.9 = (bf16[2,2,256,256]{3,2,1,0:T(8,128)(2,1)S(1)}, bf16[2,2,256,256]{3,2,1,0:T(8,128)(2,1)S(1)}, u32[]{:S(2)}, u32[]{:S(2)}) collective-permute-start(bf16[2,2,256,256]{3,2,1,0:T(8,128)(2,1)S(1)} %get-tuple-element.30), channel_id=1, source_target_pairs={{128,0},{129,1},{130,2},{131,3},{132,4},{133,5},{134,6},{135,7},{1... | collective-permute-start | bytes 1572872 | tf_op jit(solution)/shard_map/ppermute | solution.py:503
  90.3 49.7 %all-to-all-start.6 = ((s16[16,19,16,256]{3,2,1,0:T(8,128)(2,1)}), s16[16,19,16,256]{3,2,1,0:T(8,128)(2,1)S(1)}, u32[]{:S(2)}, u32[]{:S(2)}) async-start(s16[16,19,16,256]{3,2,1,0:T(8,128)(2,1)} %shard_map.50), calls=%async_computation.6 | async-start | bytes 4980736 | tf_op jit(solution)/shard_map/all_to_all | solution.py:35
  162.2 12.7 %all-to-all-start.8 = ((s16[8,80,128]{2,1,0:T(8,128)(2,1)}), s16[8,80,128]{2,1,0:T(8,128)(2,1)S(1)}, u32[]{:S(2)}, u32[]{:S(2)}) async-start(s16[8,80,128]{2,1,0:T(8,128)(2,1)} %shard_map.52), calls=%async_computation.8 | async-start | bytes 327680 | tf_op jit(solution)/shard_map/all_to_all | solution.py:35

commit v8 on v7

--- a/solution.py
+++ b/solution.py
@@ -24,10 +24,15 @@
     return sig * (1.0 + pre_act * (1.0 - sig))
 
 
-def neighbours(lower, upper):
-    count = lax.axis_size(SLAB)
-    above = lax.ppermute(lower, SLAB, [(i, i + 1) for i in range(count - 1)])
-    below = lax.ppermute(upper, SLAB, [(i + 1, i) for i in range(count - 1)])
+def neighbours(lower, upper, own_lower, own_upper):
+    slabs = lax.axis_size(SLAB)
+    cut = slabs // lax.axis_size("zh")
+    axes = ("section",) + SLAB
+    early = [(i, i + 1) for i in range(cut - 1, slabs - 1, cut)]
+    late = [(i, i + 1) for i in range(2 * slabs - 1) if i != slabs - 1 and (i, i + 1) not in early]
+    above = lax.ppermute(lower, axes, late), lax.ppermute(own_lower, axes, early)
+    late, early = [(j, i) for i, j in late], [(j, i) for i, j in early]
+    below = lax.ppermute(upper, axes, late), lax.ppermute(own_upper, axes, early)
     return above, below
 
 
@@ -103,17 +108,20 @@
     return call(body, [out], section, pair, other)[0]
 
 
-def rimmed_block(frame, row, above_ref, cells_ref, below_ref):
+def rimmed_block(frame, row, cells_ref, above_refs, below_refs):
     rows = cells_ref.shape[1]
-    if row == 0:
-        return above_ref[frame]
-    return below_ref[frame] if row > rows else cells_ref[frame, row - 1]
+    if 0 < row <= rows:
+        return cells_ref[frame, row - 1]
+    late, early = below_refs if row else above_refs
+    return late[frame] + early[frame]
 
 
 def turn_source(section, source, cells, above, below, across):
     taps, frames, rows, count, channels = source.shape
 
-    def body(section_ref, source_ref, cells_ref, above_ref, below_ref, out_ref):
+    def body(section_ref, source_ref, cells_ref, *refs):
+        above_refs, below_refs, out_ref = refs[:2], refs[2:4], refs[4]
+
         def write(block_of):
             for frame in range(frames):
                 for row in range(rows):
@@ -122,7 +130,7 @@
                         out_ref[tap, :, start : start + count] = block_of(tap, frame, row).T
 
         def encoder_block(tap, frame, row):
-            block = rimmed_block(frame, row, above_ref, cells_ref, below_ref)
+            block = rimmed_block(frame, row, cells_ref, above_refs, below_refs)
             return shifted_columns(block, across, tap)
 
         @pl.when(section_ref[0] == 0)
@@ -134,7 +142,7 @@
             write(lambda tap, frame, row: source_ref[tap, frame, row])
 
     out = jax.ShapeDtypeStruct((taps, channels, frames * rows * count), BF16)
-    return call(body, [out], section, source, cells, above, below)[0]
+    return call(body, [out], section, source, cells, *above, *below)[0]
 
 
 def tap_index(section_ref, row_tap, column_tap):
@@ -186,12 +194,12 @@
     frames, rows, count, channels = cells.shape
     span = rows * count
 
-    def body(
-        section_ref, cells_ref, above_ref, below_ref, kernel_ref, back_ref, pre_ref, shifted
-    ):
+    def body(section_ref, cells_ref, *refs):
+        above_refs, below_refs = refs[:2], refs[2:4]
+        kernel_ref, back_ref, pre_ref, shifted = refs[4:]
         for frame in range(frames):
             for row in range(rows + 2):
-                block = rimmed_block(frame, row, above_ref, cells_ref, below_ref)
+                block = rimmed_block(frame, row, cells_ref, above_refs, below_refs)
                 for tap in range(3):
                     shifted[tap, frame, row] = shifted_columns(block, across, tap)
 
@@ -225,8 +233,8 @@
         ],
         section,
         cells,
-        above,
-        below,
+        *above,
+        *below,
         kernel,
         flops=54 * span * channels * channels,
         scratch=[pltpu.VMEM((3, frames, rows + 2, count, channels), BF16)],
@@ -356,26 +364,51 @@
     )(framed_parts)
 
 
+def spread(line, parts):
+    pieces, rows, _ = line.shape
+    rows -= 8
+
+    def body(line_ref, out_ref):
+        wide = [line_ref[p].astype(F32) for p in range(pieces)]
+        row = lax.broadcasted_iota(jnp.int32, (16, 128), 0)
+        tail = jnp.zeros((16, 128), F32)
+        for p in range(pieces):
+            tail = jnp.where(row == p, wide[p][-1:], tail)
+        result = jnp.concatenate([w[:-8] for w in wide] + [tail], axis=0).astype(I16)
+        for part in range(parts):
+            out_ref[part] = result
+
+    return pl.pallas_call(
+        body, out_shape=jax.ShapeDtypeStruct((parts, pieces * rows + 16, 128), I16)
+    )(line)
+
+
 def unpack(plane, channels):
-    parts, pieces, rows, _ = plane.shape
+    parts, rows, _ = plane.shape
     size = channels // parts
+    pieces = 2 * (size // 8) * (channels // 128)
+    each = (rows - 16) // pieces
     group = 4
 
     def body(plane_ref, out_ref):
         for part in range(group):
+            wide = plane_ref[part].astype(F32)
+            scales = jnp.exp2(wide[-16:]) * (1.0 / STEPS)
             place = 0
             for frame in range(2):
                 for oct_ in range(size // 8):
                     for lane in range(channels // 128):
-                        piece = unframed(plane_ref[part, place].astype(F32)).reshape(3, 3, 8, 128)
+                        piece = wide[place * each : (place + 1) * each] * scales[place : place + 1]
                         row = part * size + oct_ * 8
-                        out_ref[frame, :, :, row : row + 8, lane * 128 : lane * 128 + 128] = piece
+                        out_ref[
+                            frame, :, :, row : row + 8, lane * 128 : lane * 128 + 128
+                        ] = piece.reshape(3, 3, 8, 128)
                         place += 1
 
     return pl.pallas_call(
         body,
         grid=(parts // group,),
-        in_specs=[pl.BlockSpec((group, pieces, rows, 128), lambda k: (k, 0, 0, 0))],
+        in_specs=[pl.BlockSpec((group, rows, 128), lambda k: (k, 0, 0))],
         out_specs=pl.BlockSpec((2, 3, 3, group * size, channels), lambda k: (0, 0, 0, k, 0)),
         out_shape=jax.ShapeDtypeStruct((2, 3, 3, channels, channels), F32),
         compiler_params=pltpu.CompilerParams(vmem_limit_bytes=VMEM_LIMIT),
@@ -447,8 +480,19 @@
     slots = int(mean + 6 * math.sqrt(mean) + 15) // 16 * 16
     cells = (frame_count, row_count, batch_count * across, channels)
 
-    turned = own_field.reshape(row_count, batch_count, frame_count, slabs, row_count, channels)
-    turned = jnp.transpose(turned, (3, 2, 4, 1, 0, 5)).reshape(slabs, -1, channels)
+    spot = lax.broadcasted_iota(jnp.int32, (positions, 1), 0)
+    share = positions // slabs
+    target, spot = spot // share, spot % share
+    frame, spot = spot // (share // frame_count), spot % (share // frame_count)
+    row, spot = spot // (batch_count * row_count), spot % (batch_count * row_count)
+    batch, column = spot // row_count, spot % row_count
+    spot = (column * batch_count + batch) * frame_count + frame
+    spot = spot * across + target * row_count + row
+    cut = (spot == lax.broadcasted_iota(jnp.int32, (1, positions), 1)).astype(BF16)
+    turned = jnp.dot(
+        cut, own_field.reshape(positions, channels), preferred_element_type=F32
+    ).astype(BF16)
+    turned = turned.reshape(slabs, share, channels)
     turned = exchange(turned, SLAB).reshape(positions, channels)
 
     own = jnp.transpose(own_field, (2, 0, 1, 3, 4)).reshape(cells)
@@ -497,7 +541,7 @@
     pair, other, cotangent, own, crowded = front(own_field, codebook, codes, whole)
     source = shift_source(section, pair, other, across)
     cells = decoder_grad(section, source, kernel, cotangent, own)
-    above, below = neighbours(cells[:, -1], cells[:, 0])
+    above, below = neighbours(cells[:, -1], cells[:, 0], own[:, -1], own[:, 0])
     back_dec, pre_act = back_and_forth(section, cells, above, below, kernel, across)
     source = turn_source(section, source, cells, above, below, across)
     returned = lax.ppermute(back_dec, "section", [(1, 0)])
@@ -510,14 +554,15 @@
     )
     plane = exchange(packed, PLANE)
     line = exchange(sum_plane(crowded, plane, lax.axis_size(Z)), Z)
-    return exchange(sum_line(line, 1.0 / math.sqrt(total)), Z)
+    mark = jnp.max(line[:, -8])
+    return exchange(sum_line(line, 1.0 / math.sqrt(total)), Z), mark
 
 
 def on_device(fields, kernels, codebook, codes):
-    line = line_shares(fields, kernels, codebook, codes, False)
+    line, mark = line_shares(fields, kernels, codebook, codes, False)
     line = lax.cond(
-        jnp.max(line[:, -8]) > 0,
-        lambda frames, *args: line_shares(*args, True),
+        mark > 0,
+        lambda frames, *args: line_shares(*args, True)[0],
         lambda frames, *args: frames,
         line,
         fields,
@@ -526,7 +571,7 @@
         codes,
     )
     planes = lax.axis_size(PLANE)
-    plane = exchange(jnp.broadcast_to(line[None], (planes,) + line.shape), PLANE)
+    plane = exchange(spread(line, planes), PLANE)
     return unpack(plane, kernels.shape[-1])[None]
 
 

time: 225 us -> 220 us (0.978)
  waiting for transfers between devices: 74.7 us -> 70.7 us
  blocking collectives: 57.3 us -> 53.4 us
  matrix products: 6.63 us -> 9.37 us
  local copies, waits for them, and re-layouts: 4.72 us -> 2.34 us
    all_to_all x2, blocking collectives: 57.3 us -> 53.4 us  [exchange(): return lax.all_to_all(cells, axes, split_axis=0, concat_axis=0, tiled=True)]
    all_to_all x4, waiting for transfers between devices: 65.8 us -> 62.9 us  [exchange(): return lax.all_to_all(cells, axes, split_axis=0, concat_axis=0, tiled=True)]
    dot_general x0 -> x1, matrix products: none -> 2.73 us  [front(): jnp.dot(cut, own_field.reshape(positions, channels), preferred_element_ty...]
    ppermute x2 -> x4, starting transfers between devices: 6.03 us -> 7.21 us  [the longest x1 3.93 us: neighbours(): lax.ppermute(upper, axes, late)]
    ppermute x2 -> x4, waiting for transfers between devices: 5.31 us -> 5.66 us  [the longest x1 3.72 us: neighbours(): lax.ppermute(lower, axes, late)]
  transfers between devices with their start and end apart: 10 -> 12, of which waited for: 9 -> 8; matrix products, arithmetic and copies ran while one was open for 4% -> 5% of each run, Pallas kernels for 0% -> 1%
where the time goes in v8:
time: 220 us
  waiting for transfers between devices  70.7 us (32%)
  blocking collectives  53.4 us (24%)
  starting transfers between devices  46.4 us (21%)
  Pallas kernels  15.3 us (7%)
  between operations  15 us (7%)
  matrix products  9.37 us (4%)
  other arithmetic  7.01 us (3%)
  local copies, waits for them, and re-layouts  2.34 us (1%)
    all_to_all x4, waiting for transfers between devices, exchange(): return lax.all_to_all(cells, axes, split_axis=0, concat_axis=0, tiled=True)  62.9 us
    all_to_all x2, blocking collectives, exchange(): return lax.all_to_all(cells, axes, split_axis=0, concat_axis=0, tiled=True)  53.4 us
    all_to_all x4, starting transfers between devices, exchange(): return lax.all_to_all(cells, axes, split_axis=0, concat_axis=0, tiled=True)  30.4 us
    pallas_call x5, Pallas kernels, call(): pl.pallas_call(body, in_specs=[pl.BlockSpec(memory_space=pltpu.SMEM)] + [...  8.27 us
    ppermute x1, starting transfers between devices, routed(): lax.ppermute(lax.dynamic_slice_in_dim(codebook, section_id * half, half,...  7.28 us
  transfers between devices with their start and end apart: 12, of which 8 were waited for; matrix products, arithmetic and copies ran while one was open for 5% of the time, Pallas kernels for 1%

profile of v8, /device:TPU:2, one launch (start us, length us, event | category | flops | bytes accessed | tf_op | source)
XLA Modules:
  0.0 219.6 jit_solution(16450382654450622654)
XLA Ops:
  6.5 1.0 constant_dynamic-slice_fusion
  7.6 7.3 %collective-permute-start.6 = (bf16[512,256]{1,0:T(8,128)(2,1)S(1)}, bf16[512,256]{1,0:T(8,128)(2,1)S(1)}, u32[]{:S(2)}, u32[]{:S(2)}) collective-permute-start(bf16[512,256]{1,0:T(8,128)(2,1)S(1)} %constant_dynamic-slice_fusion), channel_id=1, source_target_pairs={{0,64},{64,0},{1,65},{65,1},{2,66},{66,2},{3,67},{67,3},{4,68},{68... | collective-permute-start | bytes 786440 | tf_op jit(solution)/shard_map/ppermute | solution.py:428
  14.9 2.7 %fusion.63 = bf16[1024,256]{1,0:T(8,128)(2,1)} fusion(bf16[1024,256]{1,0:T(8,128)(2,1)} %bitcast.86, s32[1024]{0:T(1024)S(1)} %fusion.103), kind=kOutput, calls=%fused_computation.127 | convolution fusion | flops 538181632 | bytes 1052672 | tf_op jit(solution)/shard_map/dot_general | solution.py:492
  17.6 7.6 %all-to-all-start.4 = ((bf16[32,32,256]{2,1,0:T(8,128)(2,1)}), bf16[32,32,256]{2,1,0:T(8,128)(2,1)S(1)}, u32[]{:S(2)}, u32[]{:S(2)}) async-start(bf16[32,32,256]{2,1,0:T(8,128)(2,1)} %bitcast.25), calls=%async_computation.4 | async-start | bytes 1048576 | tf_op jit(solution)/shard_map/all_to_all | solution.py:40
  25.2 0.1 pad_add_fusion.1
  25.4 0.2 reshape.869
  25.6 0.2 fusion.72
  25.8 0.1 fusion.77
  26.0 0.3 fusion.68
  26.3 0.1 collective-permute-start.7
  26.4 1.0 select_reduce_fusion
  27.4 0.1 eq.187
  27.5 0.5 collective-permute-done.7
  28.0 1.0 pad_maximum_fusion
  29.0 13.1 %all-to-all-done.4 = bf16[32,32,256]{2,1,0:T(8,128)(2,1)S(1)} async-done(((bf16[32,32,256]{2,1,0:T(8,128)(2,1)}), bf16[32,32,256]{2,1,0:T(8,128)(2,1)S(1)}, u32[]{:S(2)}, u32[]{:S(2)}) %all-to-all-start.4) | async-done | bytes 524320 | tf_op jit(solution)/shard_map/all_to_all | solution.py:40
  42.1 3.7 %fusion.59 = bf16[1792,256]{1,0:T(8,128)(2,1)} fusion(bf16[2048,256]{1,0:T(8,128)(2,1)S(1)} %pad_maximum_fusion, s32[1792]{0:T(1024)S(1)} %eq.187), kind=kOutput, calls=%fused_computation.121 | convolution fusion | flops 1883176960 | bytes 1973248 | tf_op jit(solution)/shard_map/dot_general | solution.py:454
  45.8 4.9 %all-to-all-start.5 = ((bf16[16,112,256]{2,1,0:T(8,128)(2,1)}), bf16[16,112,256]{2,1,0:T(8,128)(2,1)S(1)}, u32[]{:S(2)}, u32[]{:S(2)}) async-start(bf16[16,112,256]{2,1,0:T(8,128)(2,1)} %bitcast.95), calls=%async_computation.5 | async-start | bytes 1835008 | tf_op jit(solution)/shard_map/all_to_all | solution.py:40
  50.8 0.3 fusion.69
  51.2 12.9 %all-to-all-done.5 = bf16[16,112,256]{2,1,0:T(8,128)(2,1)S(1)} async-done(((bf16[16,112,256]{2,1,0:T(8,128)(2,1)}), bf16[16,112,256]{2,1,0:T(8,128)(2,1)S(1)}, u32[]{:S(2)}, u32[]{:S(2)}) %all-to-all-start.5) | async-done | bytes 917536 | tf_op jit(solution)/shard_map/all_to_all | solution.py:40
  64.1 1.4 fusion.64
  65.5 0.1 collective-permute-start.8
  65.6 0.7 collective-permute-start.10
  66.3 0.7 collective-permute-start.12
  67.1 0.8 fusion.62
  67.9 0.8 copy-done
  68.7 0.2 shard_map.47.cells_ref.dec_ref
  69.0 1.9 collective-permute-start.9
  70.9 3.9 %collective-permute-start.11 = (bf16[2,256,256]{2,1,0:T(8,128)(2,1)S(1)}, bf16[2,256,256]{2,1,0:T(8,128)(2,1)S(1)}, u32[]{:S(2)}, u32[]{:S(2)}) collective-permute-start(bf16[2,256,256]{2,1,0:T(8,128)(2,1)S(1)} %get-tuple-element.44), channel_id=1, source_target_pairs={{4,0},{8,4},{12,8},{16,12},{20,16},{24,20},{28,24},{32,28},{36,32}... | collective-permute-start | bytes 786440 | tf_op jit(solution)/shard_map/ppermute | solution.py:35
  74.9 3.7 %collective-permute-done.9.refs_0_ = bf16[2,256,256]{2,1,0:T(8,128)(2,1)S(1)} collective-permute-done((bf16[2,256,256]{2,1,0:T(8,128)(2,1)S(1)}, bf16[2,256,256]{2,1,0:T(8,128)(2,1)S(1)}, u32[]{:S(2)}, u32[]{:S(2)}) %collective-permute-start.9) | collective-permute-done | bytes 262176 | tf_op jit(solution)/shard_map/ppermute | solution.py:33
  78.6 1.9 collective-permute-done.11.refs_2_
  80.5 2.5 %shard_map.49 = (bf16[2,2,256,256]{3,2,1,0:T(8,128)(2,1)S(1)}, f32[2,512,256]{2,1,0:T(8,128)S(1)}) custom-call(s32[1]{0:T(128)} %bitcast.22.section_ref, bf16[2,2,256,256]{3,2,1,0:T(8,128)(2,1)S(1)} %shard_map.47.cells_ref.dec_ref, bf16[2,256,256]{2,1,0:T(8,128)(2,1)S(1)} %collective-permute-done.9.refs_0_, ...), custom_call_target="tpu_custom_call" | custom-call | flops 1811939328 | bytes 5505028 | tf_op jit(solution)/shard_map/pallas_call | solution.py:81
  83.0 1.3 collective-permute-start.13
  84.3 1.0 shard_map.48.turned_ref
  85.3 1.7 collective-permute-done.13.returned_ref
  87.0 4.6 %shard_map.50 = s16[16,19,16,256]{3,2,1,0:T(8,128)(2,1)} custom-call(s32[1]{0:T(128)} %bitcast.22.section_ref, bf16[3,256,2048]{2,1,0:T(8,128)(2,1)S(1)} %shard_map.48.turned_ref, f32[2,512,256]{2,1,0:T(8,128)S(1)} %get-tuple-element.29.pre_ref, bf16[2,2,256,256]{3,2,1,0:T(8,128)(2,1)S(1)} %shard_map.47.cells_ref.dec_ref, ...), custom_call_target="tpu_custom_call" | custom-call | flops 1811939328 | bytes 8781828 | tf_op jit(solution)/shard_map/pallas_call | solution.py:81
  91.6 14.5 %all-to-all-start.6 = ((s16[16,19,16,256]{3,2,1,0:T(8,128)(2,1)}), s16[16,19,16,256]{3,2,1,0:T(8,128)(2,1)S(1)}, u32[]{:S(2)}, u32[]{:S(2)}) async-start(s16[16,19,16,256]{3,2,1,0:T(8,128)(2,1)} %shard_map.50), calls=%async_computation.6 | async-start | bytes 4980736 | tf_op jit(solution)/shard_map/all_to_all | solution.py:40
  106.1 1.8 convert_reduce_fusion.1
  108.0 1.4 reduce_max.27
  109.9 29.6 %all-to-all-done.6.packed_ref = s16[16,19,16,256]{3,2,1,0:T(8,128)(2,1)S(1)} async-done(((s16[16,19,16,256]{3,2,1,0:T(8,128)(2,1)}), s16[16,19,16,256]{3,2,1,0:T(8,128)(2,1)S(1)}, u32[]{:S(2)}, u32[]{:S(2)}) %all-to-all-start.6) | async-done | bytes 2490400 | tf_op jit(solution)/shard_map/all_to_all | solution.py:40
  139.5 0.8 shard_map.51
  140.3 17.5 %all_to_all.51.parts_ref = s16[8,80,128]{2,1,0:T(8,128)(2,1)} all-to-all(s16[8,80,128]{2,1,0:T(8,128)(2,1)S(1)} %shard_map.51), channel_id=1, replica_groups=mesh['section'=2,'zh'=2,'y'=4,'x'=4,'dp'=4] {'zh','dp'}, dimensions={0} | all-to-all | bytes 327680 | tf_op jit(solution)/shard_map/all_to_all | solution.py:40
  157.8 1.8 shard_map.52
  159.6 3.4 %all-to-all-start.8 = ((s16[8,80,128]{2,1,0:T(8,128)(2,1)}), s16[8,80,128]{2,1,0:T(8,128)(2,1)S(1)}, u32[]{:S(2)}, u32[]{:S(2)}) async-start(s16[8,80,128]{2,1,0:T(8,128)(2,1)} %shard_map.52), calls=%async_computation.8 | async-start | bytes 327680 | tf_op jit(solution)/shard_map/all_to_all | solution.py:40
  163.0 1.4 slice_reduce_fusion
  165.0 7.3 %all-to-all-done.8 = s16[8,80,128]{2,1,0:T(8,128)(2,1)S(1)} async-done(((s16[8,80,128]{2,1,0:T(8,128)(2,1)}), s16[8,80,128]{2,1,0:T(8,128)(2,1)S(1)}, u32[]{:S(2)}, u32[]{:S(2)}) %all-to-all-start.8) | async-done | bytes 163872 | tf_op jit(solution)/shard_map/all_to_all | solution.py:40
  172.3 1.7 shard_map.53
  174.1 36.0 %all_to_all.52.plane_ref = s16[16,592,128]{2,1,0:T(8,128)(2,1)S(1)} all-to-all(s16[16,592,128]{2,1,0:T(8,128)(2,1)} %shard_map.53), channel_id=1, replica_groups=mesh['section'=2,'zh'=2,'y'=4,'x'=4,'dp'=4] {'y','x'}, dimensions={0} | all-to-all | bytes 4849664 | tf_op jit(solution)/shard_map/all_to_all | solution.py:40
  210.0 2.7 %shard_map.54 = f32[2,3,3,256,256]{4,3,2,1,0:T(8,128)} custom-call(s16[16,592,128]{2,1,0:T(8,128)(2,1)S(1)} %all_to_all.52.plane_ref), custom_call_target="tpu_custom_call" | custom-call | tf_op jit(solution)/shard_map/pallas_call | solution.py:408
  (32 shorter events, 0.4 us)
Async XLA Ops:
  6.5 18.7 %copy-start.5 = (s32[64,4,2,64]{3,2,1,0:T(2,128)S(1)}, s32[64,4,2,64]{3,2,1,0:T(2,128)}, u32[]{:S(2)}) copy-start(s32[64,4,2,64]{3,2,1,0:T(2,128)} %param.9) | copy-start | bytes 393220
  7.6 18.8 %collective-permute-start.6 = (bf16[512,256]{1,0:T(8,128)(2,1)S(1)}, bf16[512,256]{1,0:T(8,128)(2,1)S(1)}, u32[]{:S(2)}, u32[]{:S(2)}) collective-permute-start(bf16[512,256]{1,0:T(8,128)(2,1)S(1)} %constant_dynamic-slice_fusion), channel_id=1, source_target_pairs={{0,64},{64,0},{1,65},{65,1},{2,66},{66,2},{3,67},{67,3},{4,68},{68... | collective-permute-start | bytes 786440 | tf_op jit(solution)/shard_map/ppermute | solution.py:428
  14.8 13.1 %copy-start.2 = (bf16[1024,256]{1,0:T(8,128)(2,1)S(1)}, bf16[1024,256]{1,0:T(8,128)(2,1)}, u32[]{:S(2)}) copy-start(bf16[1024,256]{1,0:T(8,128)(2,1)} %param.8) | copy-start | bytes 1572868
  17.6 24.5 %all-to-all-start.4 = ((bf16[32,32,256]{2,1,0:T(8,128)(2,1)}), bf16[32,32,256]{2,1,0:T(8,128)(2,1)S(1)}, u32[]{:S(2)}, u32[]{:S(2)}) async-start(bf16[32,32,256]{2,1,0:T(8,128)(2,1)} %bitcast.25), calls=%async_computation.4 | async-start | bytes 1048576 | tf_op jit(solution)/shard_map/all_to_all | solution.py:40
  25.8 25.0 %copy-start.7 = (s32[33,1024]{1,0:T(8,128)}, s32[33,1024]{1,0:T(8,128)S(1)}, u32[]{:S(2)}) copy-start(s32[33,1024]{1,0:T(8,128)S(1)} %fusion.72) | copy-start | bytes 405508
  26.3 1.1 copy-start.10
  26.3 1.6 collective-permute-start.7
  42.1 3.7 %copy-start.8 = (bf16[32,32,256]{2,1,0:T(8,128)(2,1)}, bf16[32,32,256]{2,1,0:T(8,128)(2,1)S(1)}, u32[]{:S(2)}) copy-start(bf16[32,32,256]{2,1,0:T(8,128)(2,1)S(1)} %all-to-all-done.4) | copy-start | bytes 1572868
  42.1 8.6 %copy-start.4 = (bf16[1,2,4,2,64,256]{5,4,3,2,1,0:T(8,128)(2,1)S(1)}, bf16[1,2,4,2,64,256]{5,4,3,2,1,0:T(8,128)(2,1)}, u32[]{:S(2)}) copy-start(bf16[1,2,4,2,64,256]{5,4,3,2,1,0:T(8,128)(2,1)} %param.6) | copy-start | bytes 1572868
  45.8 18.2 %all-to-all-start.5 = ((bf16[16,112,256]{2,1,0:T(8,128)(2,1)}), bf16[16,112,256]{2,1,0:T(8,128)(2,1)S(1)}, u32[]{:S(2)}, u32[]{:S(2)}) async-start(bf16[16,112,256]{2,1,0:T(8,128)(2,1)} %bitcast.95), calls=%async_computation.5 | async-start | bytes 1835008 | tf_op jit(solution)/shard_map/all_to_all | solution.py:40
  64.1 3.0 %copy-start.9 = (bf16[32,32,256]{2,1,0:T(8,128)(2,1)S(1)}, bf16[32,32,256]{2,1,0:T(8,128)(2,1)}, u32[]{:S(2)}) copy-start(bf16[32,32,256]{2,1,0:T(8,128)(2,1)} %copy-done.8) | copy-start | bytes 1572868
  65.5 2.4 %collective-permute-start.8 = (bf16[1024,256]{1,0:T(8,128)(2,1)S(1)}, bf16[1024,256]{1,0:T(8,128)(2,1)S(1)}, u32[]{:S(2)}, u32[]{:S(2)}) collective-permute-start(bf16[1024,256]{1,0:T(8,128)(2,1)S(1)} %fusion.64), channel_id=1, source_target_pairs={{0,128},{128,0},{1,129},{129,1},{2,130},{130,2},{3,131},{131,3},{4... | collective-permute-start | bytes 1572872 | tf_op jit(solution)/shard_map/ppermute | solution.py:525
  65.6 9.3 %collective-permute-start.10 = (bf16[2,256,256]{2,1,0:T(8,128)(2,1)S(1)}, bf16[2,256,256]{2,1,0:T(8,128)(2,1)S(1)}, u32[]{:S(2)}, u32[]{:S(2)}) collective-permute-start(bf16[2,256,256]{2,1,0:T(8,128)(2,1)S(1)} %get-tuple-element.43), channel_id=1, source_target_pairs={{60,64},{61,65},{62,66},{63,67}} | collective-permute-start | bytes 786440 | tf_op jit(solution)/shard_map/ppermute | solution.py:33
  66.3 8.6 %collective-permute-start.12 = (bf16[2,256,256]{2,1,0:T(8,128)(2,1)S(1)}, bf16[2,256,256]{2,1,0:T(8,128)(2,1)S(1)}, u32[]{:S(2)}, u32[]{:S(2)}) collective-permute-start(bf16[2,256,256]{2,1,0:T(8,128)(2,1)S(1)} %get-tuple-element.42), channel_id=1, source_target_pairs={{64,60},{65,61},{66,62},{67,63}} | collective-permute-start | bytes 786440 | tf_op jit(solution)/shard_map/ppermute | solution.py:35
  67.0 1.7 copy-start
  69.0 9.6 %collective-permute-start.9 = (bf16[2,256,256]{2,1,0:T(8,128)(2,1)S(1)}, bf16[2,256,256]{2,1,0:T(8,128)(2,1)S(1)}, u32[]{:S(2)}, u32[]{:S(2)}) collective-permute-start(bf16[2,256,256]{2,1,0:T(8,128)(2,1)S(1)} %get-tuple-element.45), channel_id=1, source_target_pairs={{0,4},{4,8},{8,12},{12,16},{16,20},{20,24},{24,28},{28,32},{32,36}... | collective-permute-start | bytes 786440 | tf_op jit(solution)/shard_map/ppermute | solution.py:33
  70.9 9.6 %collective-permute-start.11 = (bf16[2,256,256]{2,1,0:T(8,128)(2,1)S(1)}, bf16[2,256,256]{2,1,0:T(8,128)(2,1)S(1)}, u32[]{:S(2)}, u32[]{:S(2)}) collective-permute-start(bf16[2,256,256]{2,1,0:T(8,128)(2,1)S(1)} %get-tuple-element.44), channel_id=1, source_target_pairs={{4,0},{8,4},{12,8},{16,12},{20,16},{24,20},{28,24},{32,28},{36,32}... | collective-permute-start | bytes 786440 | tf_op jit(solution)/shard_map/ppermute | solution.py:35
  83.0 4.0 %collective-permute-start.13 = (bf16[2,2,256,256]{3,2,1,0:T(8,128)(2,1)S(1)}, bf16[2,2,256,256]{3,2,1,0:T(8,128)(2,1)S(1)}, u32[]{:S(2)}, u32[]{:S(2)}) collective-permute-start(bf16[2,2,256,256]{3,2,1,0:T(8,128)(2,1)S(1)} %get-tuple-element.30), channel_id=1, source_target_pairs={{128,0},{129,1},{130,2},{131,3},{132,4},{133,5},{134,6},{135,7},{1... | collective-permute-start | bytes 1572872 | tf_op jit(solution)/shard_map/ppermute | solution.py:547
  91.6 47.9 %all-to-all-start.6 = ((s16[16,19,16,256]{3,2,1,0:T(8,128)(2,1)}), s16[16,19,16,256]{3,2,1,0:T(8,128)(2,1)S(1)}, u32[]{:S(2)}, u32[]{:S(2)}) async-start(s16[16,19,16,256]{3,2,1,0:T(8,128)(2,1)} %shard_map.50), calls=%async_computation.6 | async-start | bytes 4980736 | tf_op jit(solution)/shard_map/all_to_all | solution.py:40
  159.6 12.7 %all-to-all-start.8 = ((s16[8,80,128]{2,1,0:T(8,128)(2,1)}), s16[8,80,128]{2,1,0:T(8,128)(2,1)S(1)}, u32[]{:S(2)}, u32[]{:S(2)}) async-start(s16[8,80,128]{2,1,0:T(8,128)(2,1)} %shard_map.52), calls=%async_computation.8 | async-start | bytes 327680 | tf_op jit(solution)/shard_map/all_to_all | solution.py:40

commit v9 on v8

--- a/solution.py
+++ b/solution.py
@@ -24,15 +24,18 @@
     return sig * (1.0 + pre_act * (1.0 - sig))
 
 
-def neighbours(lower, upper, own_lower, own_upper):
+def halo_pairs():
     slabs = lax.axis_size(SLAB)
     cut = slabs // lax.axis_size("zh")
-    axes = ("section",) + SLAB
     early = [(i, i + 1) for i in range(cut - 1, slabs - 1, cut)]
     late = [(i, i + 1) for i in range(2 * slabs - 1) if i != slabs - 1 and (i, i + 1) not in early]
-    above = lax.ppermute(lower, axes, late), lax.ppermute(own_lower, axes, early)
-    late, early = [(j, i) for i, j in late], [(j, i) for i, j in early]
-    below = lax.ppermute(upper, axes, late), lax.ppermute(own_upper, axes, early)
+    return late, early
+
+
+def neighbours(cells, pairs):
+    axes = ("section",) + SLAB
+    above = lax.ppermute(cells[:, -1], axes, pairs)
+    below = lax.ppermute(cells[:, 0], axes, [(j, i) for i, j in pairs])
     return above, below
 
 
@@ -415,7 +418,7 @@
     )(plane)
 
 
-def routed(codebook, shifted, holder, slots, turned):
+def routed(codebook, shifted, holder, slots, turned, early):
     section_id = lax.axis_index("section")
     slab_id = lax.axis_index(SLAB)
     near = lax.axis_index("zh")
@@ -454,6 +457,7 @@
     words = jnp.dot(picks, table, preferred_element_type=F32).astype(BF16)
     looked = exchange(words.reshape(planes, slots, channels), PLANE)
     looked = looked.reshape(planes * slots, channels)
+    looked, early = lax.optimization_barrier((looked, early))
 
     own_wanted = lax.dynamic_index_in_dim(shifted, slab_id + section_id, 0, keepdims=False)
     own_holder = lax.dynamic_index_in_dim(holder, slab_id + section_id, 0, keepdims=False)
@@ -465,7 +469,7 @@
         order[:, None] == lax.broadcasted_iota(jnp.int32, (1, planes * slots), 1)
     ).astype(BF16)
     pair = jnp.dot(gather, looked, preferred_element_type=F32).astype(BF16)
-    return pair, turned
+    return pair, turned, early
 
 
 def front(own_field, codebook, codes, whole):
@@ -496,6 +500,7 @@
     turned = exchange(turned, SLAB).reshape(positions, channels)
 
     own = jnp.transpose(own_field, (2, 0, 1, 3, 4)).reshape(cells)
+    early = neighbours(own, halo_pairs()[1])
 
     edge = jnp.full((1,) + codes.shape[1:], -1, codes.dtype)
     shifted = jnp.concatenate([edge, codes, edge], axis=0)
@@ -509,7 +514,7 @@
         taken = jnp.take(every, jnp.maximum(wanted, 0), axis=0)
         pair = jnp.where(wanted[:, None] >= 0, taken, 0).astype(BF16)
     else:
-        pair, turned = routed(codebook, shifted, holder, slots, turned)
+        pair, turned, early = routed(codebook, shifted, holder, slots, turned, early)
 
     place = lax.broadcasted_iota(jnp.int32, (positions, 1), 0)
     group, column = place // across, place % across
@@ -528,6 +533,7 @@
         other.reshape(cells),
         cotangent.reshape(frame_count, -1, channels),
         own,
+        early,
         crowded,
     )
 
@@ -538,10 +544,10 @@
     own_field = fields[0]
     kernel = kernels[0]
     row_count, batch_count, frame_count, across, channels = own_field.shape
-    pair, other, cotangent, own, crowded = front(own_field, codebook, codes, whole)
+    pair, other, cotangent, own, early, crowded = front(own_field, codebook, codes, whole)
     source = shift_source(section, pair, other, across)
     cells = decoder_grad(section, source, kernel, cotangent, own)
-    above, below = neighbours(cells[:, -1], cells[:, 0], own[:, -1], own[:, 0])
+    above, below = zip(neighbours(cells, halo_pairs()[0]), early)
     back_dec, pre_act = back_and_forth(section, cells, above, below, kernel, across)
     source = turn_source(section, source, cells, above, below, across)
     returned = lax.ppermute(back_dec, "section", [(1, 0)])

time: 220 us -> 223 us (1.014)
  starting transfers between devices: 46.4 us -> 51.8 us
    all_to_all x4, starting transfers between devices: 30.4 us -> 35.8 us  [exchange(): return lax.all_to_all(cells, axes, split_axis=0, concat_axis=0, tiled=True)]
  transfers between devices with their start and end apart: 12 -> 12, of which waited for: 8 -> 9; matrix products, arithmetic and copies ran while one was open for 5% -> 6% of each run, Pallas kernels for 1% -> 0%
where the time goes in v9:
time: 223 us
  waiting for transfers between devices  69.5 us (31%)
  blocking collectives  52.4 us (23%)
  starting transfers between devices  51.8 us (23%)
  Pallas kernels  15.3 us (7%)
  between operations  15 us (7%)
  matrix products  9.37 us (4%)
  other arithmetic  7.01 us (3%)
  local copies, waits for them, and re-layouts  2.35 us (1%)
    all_to_all x4, waiting for transfers between devices, exchange(): return lax.all_to_all(cells, axes, split_axis=0, concat_axis=0, tiled=True)  60.7 us
    all_to_all x2, blocking collectives, exchange(): return lax.all_to_all(cells, axes, split_axis=0, concat_axis=0, tiled=True)  52.4 us
    all_to_all x4, starting transfers between devices, exchange(): return lax.all_to_all(cells, axes, split_axis=0, concat_axis=0, tiled=True)  35.8 us
    pallas_call x5, Pallas kernels, call(): pl.pallas_call(body, in_specs=[pl.BlockSpec(memory_space=pltpu.SMEM)] + [...  8.26 us
    ppermute x1, starting transfers between devices, routed(): lax.ppermute(lax.dynamic_slice_in_dim(codebook, section_id * half, half,...  7.28 us
    ppermute x2, starting transfers between devices, neighbours(): below = lax.ppermute(cells[:, 0], axes, [(j, i) for i, j in pairs])  4.61 us
  transfers between devices with their start and end apart: 12, of which 9 were waited for; matrix products, arithmetic and copies ran while one was open for 6% of the time, Pallas kernels for 0%

profile of v9, /device:TPU:2, one launch (start us, length us, event | category | flops | bytes accessed | tf_op | source)
XLA Modules:
  0.0 222.7 jit_solution(7777482954054305874)
XLA Ops:
  6.5 1.0 constant_dynamic-slice_fusion
  7.6 7.3 %collective-permute-start.6 = (bf16[512,256]{1,0:T(8,128)(2,1)S(1)}, bf16[512,256]{1,0:T(8,128)(2,1)S(1)}, u32[]{:S(2)}, u32[]{:S(2)}) collective-permute-start(bf16[512,256]{1,0:T(8,128)(2,1)S(1)} %constant_dynamic-slice_fusion), channel_id=1, source_target_pairs={{0,64},{64,0},{1,65},{65,1},{2,66},{66,2},{3,67},{67,3},{4,68},{68... | collective-permute-start | bytes 786440 | tf_op jit(solution)/shard_map/ppermute | solution.py:431
  14.9 2.7 %fusion.63 = bf16[1024,256]{1,0:T(8,128)(2,1)} fusion(bf16[1024,256]{1,0:T(8,128)(2,1)} %bitcast.86, s32[1024]{0:T(1024)S(1)} %fusion.103), kind=kOutput, calls=%fused_computation.127 | convolution fusion | flops 538181632 | bytes 1052672 | tf_op jit(solution)/shard_map/dot_general | solution.py:496
  17.6 7.6 %all-to-all-start.4 = ((bf16[32,32,256]{2,1,0:T(8,128)(2,1)}), bf16[32,32,256]{2,1,0:T(8,128)(2,1)S(1)}, u32[]{:S(2)}, u32[]{:S(2)}) async-start(bf16[32,32,256]{2,1,0:T(8,128)(2,1)} %bitcast.25), calls=%async_computation.4 | async-start | bytes 1048576 | tf_op jit(solution)/shard_map/all_to_all | solution.py:43
  25.2 0.1 pad_add_fusion.1
  25.4 0.2 reshape.869
  25.6 0.2 fusion.72
  25.8 0.1 fusion.77
  26.0 0.3 fusion.68
  26.3 0.1 collective-permute-start.7
  26.4 1.0 select_reduce_fusion
  27.5 0.5 collective-permute-done.7
  28.0 1.0 pad_maximum_fusion
  29.0 13.1 %all-to-all-done.4 = bf16[32,32,256]{2,1,0:T(8,128)(2,1)S(1)} async-done(((bf16[32,32,256]{2,1,0:T(8,128)(2,1)}), bf16[32,32,256]{2,1,0:T(8,128)(2,1)S(1)}, u32[]{:S(2)}, u32[]{:S(2)}) %all-to-all-start.4) | async-done | bytes 524320 | tf_op jit(solution)/shard_map/all_to_all | solution.py:43
  42.1 3.7 %fusion.59 = bf16[1792,256]{1,0:T(8,128)(2,1)} fusion(bf16[2048,256]{1,0:T(8,128)(2,1)S(1)} %pad_maximum_fusion, s32[1792]{0:T(1024)S(1)} %eq.187), kind=kOutput, calls=%fused_computation.121 | convolution fusion | flops 1883176960 | bytes 1973248 | tf_op jit(solution)/shard_map/dot_general | solution.py:457
  45.8 4.9 %all-to-all-start.5 = ((bf16[16,112,256]{2,1,0:T(8,128)(2,1)}), bf16[16,112,256]{2,1,0:T(8,128)(2,1)S(1)}, u32[]{:S(2)}, u32[]{:S(2)}) async-start(bf16[16,112,256]{2,1,0:T(8,128)(2,1)} %bitcast.95), calls=%async_computation.5 | async-start | bytes 1835008 | tf_op jit(solution)/shard_map/all_to_all | solution.py:43
  50.8 0.8 slice_bitcast_fusion.6
  51.6 0.7 collective-permute-start.8
  52.3 0.7 collective-permute-start.9
  53.0 0.3 fusion.69
  53.4 10.6 %all-to-all-done.5 = bf16[16,112,256]{2,1,0:T(8,128)(2,1)S(1)} async-done(((bf16[16,112,256]{2,1,0:T(8,128)(2,1)}), bf16[16,112,256]{2,1,0:T(8,128)(2,1)S(1)}, u32[]{:S(2)}, u32[]{:S(2)}) %all-to-all-start.5) | async-done | bytes 917536 | tf_op jit(solution)/shard_map/all_to_all | solution.py:43
  64.1 1.4 fusion.64
  65.5 0.1 collective-permute-start.10
  65.6 0.8 fusion.62
  66.5 1.0 collective-permute-done.10
  67.5 0.2 shard_map.47.cells_ref.dec_ref
  67.7 1.9 collective-permute-start.11
  69.7 3.9 %collective-permute-start.12 = (bf16[2,256,256]{2,1,0:T(8,128)(2,1)S(1)}, bf16[2,256,256]{2,1,0:T(8,128)(2,1)S(1)}, u32[]{:S(2)}, u32[]{:S(2)}) collective-permute-start(bf16[2,256,256]{2,1,0:T(8,128)(2,1)S(1)} %get-tuple-element.48), channel_id=1, source_target_pairs={{4,0},{8,4},{12,8},{16,12},{20,16},{24,20},{28,24},{32,28},{36,32}... | collective-permute-start | bytes 786440 | tf_op jit(solution)/shard_map/ppermute | solution.py:38
  73.6 3.4 %collective-permute-done.11.refs_0_ = bf16[2,256,256]{2,1,0:T(8,128)(2,1)S(1)} collective-permute-done((bf16[2,256,256]{2,1,0:T(8,128)(2,1)S(1)}, bf16[2,256,256]{2,1,0:T(8,128)(2,1)S(1)}, u32[]{:S(2)}, u32[]{:S(2)}) %collective-permute-start.11) | collective-permute-done | bytes 262176 | tf_op jit(solution)/shard_map/ppermute | solution.py:37
  77.0 1.9 collective-permute-done.12.refs_2_
  78.9 2.5 %shard_map.49 = (bf16[2,2,256,256]{3,2,1,0:T(8,128)(2,1)S(1)}, f32[2,512,256]{2,1,0:T(8,128)S(1)}) custom-call(s32[1]{0:T(128)} %bitcast.22.section_ref, bf16[2,2,256,256]{3,2,1,0:T(8,128)(2,1)S(1)} %shard_map.47.cells_ref.dec_ref, bf16[2,256,256]{2,1,0:T(8,128)(2,1)S(1)} %collective-permute-done.11.refs_0_, ...), custom_call_target="tpu_custom_call" | custom-call | flops 1811939328 | bytes 5505028 | tf_op jit(solution)/shard_map/pallas_call | solution.py:84
  81.4 1.3 collective-permute-start.13
  82.7 1.0 shard_map.48.turned_ref
  83.7 2.1 collective-permute-done.13.returned_ref
  85.8 4.6 %shard_map.50 = s16[16,19,16,256]{3,2,1,0:T(8,128)(2,1)} custom-call(s32[1]{0:T(128)} %bitcast.22.section_ref, bf16[3,256,2048]{2,1,0:T(8,128)(2,1)S(1)} %shard_map.48.turned_ref, f32[2,512,256]{2,1,0:T(8,128)S(1)} %get-tuple-element.35.pre_ref, bf16[2,2,256,256]{3,2,1,0:T(8,128)(2,1)S(1)} %shard_map.47.cells_ref.dec_ref, ...), custom_call_target="tpu_custom_call" | custom-call | flops 1811939328 | bytes 8781828 | tf_op jit(solution)/shard_map/pallas_call | solution.py:84
  90.3 20.0 %all-to-all-start.6 = ((s16[16,19,16,256]{3,2,1,0:T(8,128)(2,1)}), s16[16,19,16,256]{3,2,1,0:T(8,128)(2,1)S(1)}, u32[]{:S(2)}, u32[]{:S(2)}) async-start(s16[16,19,16,256]{3,2,1,0:T(8,128)(2,1)} %shard_map.50), calls=%async_computation.6 | async-start | bytes 4980736 | tf_op jit(solution)/shard_map/all_to_all | solution.py:43
  110.3 1.8 convert_reduce_fusion.1
  112.1 1.4 reduce_max.27
  114.1 29.6 %all-to-all-done.6.packed_ref = s16[16,19,16,256]{3,2,1,0:T(8,128)(2,1)S(1)} async-done(((s16[16,19,16,256]{3,2,1,0:T(8,128)(2,1)}), s16[16,19,16,256]{3,2,1,0:T(8,128)(2,1)S(1)}, u32[]{:S(2)}, u32[]{:S(2)}) %all-to-all-start.6) | async-done | bytes 2490400 | tf_op jit(solution)/shard_map/all_to_all | solution.py:43
  143.7 0.8 shard_map.51
  144.5 16.4 %all_to_all.51.parts_ref = s16[8,80,128]{2,1,0:T(8,128)(2,1)} all-to-all(s16[8,80,128]{2,1,0:T(8,128)(2,1)S(1)} %shard_map.51), channel_id=1, replica_groups=mesh['section'=2,'zh'=2,'y'=4,'x'=4,'dp'=4] {'zh','dp'}, dimensions={0} | all-to-all | bytes 327680 | tf_op jit(solution)/shard_map/all_to_all | solution.py:43
  160.9 1.8 shard_map.52
  162.7 3.4 %all-to-all-start.8 = ((s16[8,80,128]{2,1,0:T(8,128)(2,1)}), s16[8,80,128]{2,1,0:T(8,128)(2,1)S(1)}, u32[]{:S(2)}, u32[]{:S(2)}) async-start(s16[8,80,128]{2,1,0:T(8,128)(2,1)} %shard_map.52), calls=%async_computation.8 | async-start | bytes 327680 | tf_op jit(solution)/shard_map/all_to_all | solution.py:43
  166.1 1.4 slice_reduce_fusion
  168.1 7.3 %all-to-all-done.8 = s16[8,80,128]{2,1,0:T(8,128)(2,1)S(1)} async-done(((s16[8,80,128]{2,1,0:T(8,128)(2,1)}), s16[8,80,128]{2,1,0:T(8,128)(2,1)S(1)}, u32[]{:S(2)}, u32[]{:S(2)}) %all-to-all-start.8) | async-done | bytes 163872 | tf_op jit(solution)/shard_map/all_to_all | solution.py:43
  175.4 1.7 shard_map.53
  177.2 36.0 %all_to_all.52.plane_ref = s16[16,592,128]{2,1,0:T(8,128)(2,1)S(1)} all-to-all(s16[16,592,128]{2,1,0:T(8,128)(2,1)} %shard_map.53), channel_id=1, replica_groups=mesh['section'=2,'zh'=2,'y'=4,'x'=4,'dp'=4] {'y','x'}, dimensions={0} | all-to-all | bytes 4849664 | tf_op jit(solution)/shard_map/all_to_all | solution.py:43
  213.1 2.7 %shard_map.54 = f32[2,3,3,256,256]{4,3,2,1,0:T(8,128)} custom-call(s16[16,592,128]{2,1,0:T(8,128)(2,1)S(1)} %all_to_all.52.plane_ref), custom_call_target="tpu_custom_call" | custom-call | tf_op jit(solution)/shard_map/pallas_call | solution.py:411
  (32 shorter events, 0.4 us)
Async XLA Ops:
  6.5 18.7 %copy-start.5 = (s32[64,4,2,64]{3,2,1,0:T(2,128)S(1)}, s32[64,4,2,64]{3,2,1,0:T(2,128)}, u32[]{:S(2)}) copy-start(s32[64,4,2,64]{3,2,1,0:T(2,128)} %param.9) | copy-start | bytes 393220
  7.6 18.8 %collective-permute-start.6 = (bf16[512,256]{1,0:T(8,128)(2,1)S(1)}, bf16[512,256]{1,0:T(8,128)(2,1)S(1)}, u32[]{:S(2)}, u32[]{:S(2)}) collective-permute-start(bf16[512,256]{1,0:T(8,128)(2,1)S(1)} %constant_dynamic-slice_fusion), channel_id=1, source_target_pairs={{0,64},{64,0},{1,65},{65,1},{2,66},{66,2},{3,67},{67,3},{4,68},{68... | collective-permute-start | bytes 786440 | tf_op jit(solution)/shard_map/ppermute | solution.py:431
  14.8 13.1 %copy-start.2 = (bf16[1024,256]{1,0:T(8,128)(2,1)S(1)}, bf16[1024,256]{1,0:T(8,128)(2,1)}, u32[]{:S(2)}) copy-start(bf16[1024,256]{1,0:T(8,128)(2,1)} %param.8) | copy-start | bytes 1572868
  17.6 24.5 %all-to-all-start.4 = ((bf16[32,32,256]{2,1,0:T(8,128)(2,1)}), bf16[32,32,256]{2,1,0:T(8,128)(2,1)S(1)}, u32[]{:S(2)}, u32[]{:S(2)}) async-start(bf16[32,32,256]{2,1,0:T(8,128)(2,1)} %bitcast.25), calls=%async_computation.4 | async-start | bytes 1048576 | tf_op jit(solution)/shard_map/all_to_all | solution.py:43
  25.8 27.2 %copy-start.7 = (s32[33,1024]{1,0:T(8,128)}, s32[33,1024]{1,0:T(8,128)S(1)}, u32[]{:S(2)}) copy-start(s32[33,1024]{1,0:T(8,128)S(1)} %fusion.72) | copy-start | bytes 405508
  26.3 1.1 copy-start.10
  26.3 1.6 collective-permute-start.7
  42.1 3.7 %copy-start.8 = (bf16[32,32,256]{2,1,0:T(8,128)(2,1)}, bf16[32,32,256]{2,1,0:T(8,128)(2,1)S(1)}, u32[]{:S(2)}) copy-start(bf16[32,32,256]{2,1,0:T(8,128)(2,1)S(1)} %all-to-all-done.4) | copy-start | bytes 1572868
  42.1 8.6 %copy-start.4 = (bf16[1,2,4,2,64,256]{5,4,3,2,1,0:T(8,128)(2,1)S(1)}, bf16[1,2,4,2,64,256]{5,4,3,2,1,0:T(8,128)(2,1)}, u32[]{:S(2)}) copy-start(bf16[1,2,4,2,64,256]{5,4,3,2,1,0:T(8,128)(2,1)} %param.6) | copy-start | bytes 1572868
  45.8 18.2 %all-to-all-start.5 = ((bf16[16,112,256]{2,1,0:T(8,128)(2,1)}), bf16[16,112,256]{2,1,0:T(8,128)(2,1)S(1)}, u32[]{:S(2)}, u32[]{:S(2)}) async-start(bf16[16,112,256]{2,1,0:T(8,128)(2,1)} %bitcast.95), calls=%async_computation.5 | async-start | bytes 1835008 | tf_op jit(solution)/shard_map/all_to_all | solution.py:43
  51.6 1.8 collective-permute-start.8
  52.3 1.1 collective-permute-start.9
  64.1 1.6 copy-start.9
  65.5 2.0 collective-permute-start.10
  65.6 1.8 copy-start
  67.7 9.2 %collective-permute-start.11 = (bf16[2,256,256]{2,1,0:T(8,128)(2,1)S(1)}, bf16[2,256,256]{2,1,0:T(8,128)(2,1)S(1)}, u32[]{:S(2)}, u32[]{:S(2)}) collective-permute-start(bf16[2,256,256]{2,1,0:T(8,128)(2,1)S(1)} %get-tuple-element.49), channel_id=1, source_target_pairs={{0,4},{4,8},{8,12},{12,16},{16,20},{20,24},{24,28},{28,32},{32,36}... | collective-permute-start | bytes 786440 | tf_op jit(solution)/shard_map/ppermute | solution.py:37
  69.7 9.2 %collective-permute-start.12 = (bf16[2,256,256]{2,1,0:T(8,128)(2,1)S(1)}, bf16[2,256,256]{2,1,0:T(8,128)(2,1)S(1)}, u32[]{:S(2)}, u32[]{:S(2)}) collective-permute-start(bf16[2,256,256]{2,1,0:T(8,128)(2,1)S(1)} %get-tuple-element.48), channel_id=1, source_target_pairs={{4,0},{8,4},{12,8},{16,12},{20,16},{24,20},{28,24},{32,28},{36,32}... | collective-permute-start | bytes 786440 | tf_op jit(solution)/shard_map/ppermute | solution.py:38
  81.4 4.4 %collective-permute-start.13 = (bf16[2,2,256,256]{3,2,1,0:T(8,128)(2,1)S(1)}, bf16[2,2,256,256]{3,2,1,0:T(8,128)(2,1)S(1)}, u32[]{:S(2)}, u32[]{:S(2)}) collective-permute-start(bf16[2,2,256,256]{3,2,1,0:T(8,128)(2,1)S(1)} %get-tuple-element.36), channel_id=1, source_target_pairs={{128,0},{129,1},{130,2},{131,3},{132,4},{133,5},{134,6},{135,7},{1... | collective-permute-start | bytes 1572872 | tf_op jit(solution)/shard_map/ppermute | solution.py:553
  90.3 53.4 %all-to-all-start.6 = ((s16[16,19,16,256]{3,2,1,0:T(8,128)(2,1)}), s16[16,19,16,256]{3,2,1,0:T(8,128)(2,1)S(1)}, u32[]{:S(2)}, u32[]{:S(2)}) async-start(s16[16,19,16,256]{3,2,1,0:T(8,128)(2,1)} %shard_map.50), calls=%async_computation.6 | async-start | bytes 4980736 | tf_op jit(solution)/shard_map/all_to_all | solution.py:43
  162.7 12.7 %all-to-all-start.8 = ((s16[8,80,128]{2,1,0:T(8,128)(2,1)}), s16[8,80,128]{2,1,0:T(8,128)(2,1)S(1)}, u32[]{:S(2)}, u32[]{:S(2)}) async-start(s16[8,80,128]{2,1,0:T(8,128)(2,1)} %shard_map.52), calls=%async_computation.8 | async-start | bytes 327680 | tf_op jit(solution)/shard_map/all_to_all | solution.py:43

commit v10 on v8

--- a/solution.py
+++ b/solution.py
@@ -24,16 +24,12 @@
     return sig * (1.0 + pre_act * (1.0 - sig))
 
 
-def neighbours(lower, upper, own_lower, own_upper):
-    slabs = lax.axis_size(SLAB)
-    cut = slabs // lax.axis_size("zh")
-    axes = ("section",) + SLAB
-    early = [(i, i + 1) for i in range(cut - 1, slabs - 1, cut)]
-    late = [(i, i + 1) for i in range(2 * slabs - 1) if i != slabs - 1 and (i, i + 1) not in early]
-    above = lax.ppermute(lower, axes, late), lax.ppermute(own_lower, axes, early)
-    late, early = [(j, i) for i, j in late], [(j, i) for i, j in early]
-    below = lax.ppermute(upper, axes, late), lax.ppermute(own_upper, axes, early)
-    return above, below
+def neighbours(lower, upper):
+    count = lax.axis_size(SLAB)
+    above = lax.ppermute(lower, SLAB, [(i, i + 1) for i in range(count - 1)])
+    below = lax.ppermute(upper, SLAB, [(i + 1, i) for i in range(count - 1)])
+    none = jnp.zeros_like(lower)
+    return (above, none), (below, none)
 
 
 def exchange(cells, axes):
@@ -541,7 +537,7 @@
     pair, other, cotangent, own, crowded = front(own_field, codebook, codes, whole)
     source = shift_source(section, pair, other, across)
     cells = decoder_grad(section, source, kernel, cotangent, own)
-    above, below = neighbours(cells[:, -1], cells[:, 0], own[:, -1], own[:, 0])
+    above, below = neighbours(cells[:, -1], cells[:, 0])
     back_dec, pre_act = back_and_forth(section, cells, above, below, kernel, across)
     source = turn_source(section, source, cells, above, below, across)
     returned = lax.ppermute(back_dec, "section", [(1, 0)])

time: 220 us -> 223 us (1.014)
    ppermute x4 -> x2, starting transfers between devices: 7.21 us -> 6.03 us  [the longest x1 4.11 us: neighbours(): below = lax.ppermute(upper, SLAB, [(i + 1, i) for i in range(count - 1)])]
    ppermute x4 -> x2, waiting for transfers between devices: 5.66 us -> 5.12 us  [the longest x1 3.19 us: neighbours(): above = lax.ppermute(lower, SLAB, [(i, i + 1) for i in range(count - 1)])]
  transfers between devices with their start and end apart: 12 -> 10, of which waited for: 8 -> 9; matrix products, arithmetic and copies ran while one was open for 5% -> 5% of each run, Pallas kernels for 1% -> 0%
where the time goes in v10:
time: 223 us; the launch traced here: 222 us
  waiting for transfers between devices  72.6 us (33%)
  blocking collectives  55.6 us (25%)
  starting transfers between devices  46.9 us (21%)
  Pallas kernels  15.1 us (7%)
  between operations  14.9 us (7%)
  matrix products  9.36 us (4%)
  other arithmetic  6.05 us (3%)
    all_to_all x4, waiting for transfers between devices, exchange(): return lax.all_to_all(cells, axes, split_axis=0, concat_axis=0, tiled=True)  64 us
    all_to_all x2, blocking collectives, exchange(): return lax.all_to_all(cells, axes, split_axis=0, concat_axis=0, tiled=True)  55.6 us
    all_to_all x4, starting transfers between devices, exchange(): return lax.all_to_all(cells, axes, split_axis=0, concat_axis=0, tiled=True)  32.1 us
    pallas_call x5, Pallas kernels, call(): pl.pallas_call(body, in_specs=[pl.BlockSpec(memory_space=pltpu.SMEM)] + [...  8.1 us
    ppermute x1, starting transfers between devices, routed(): lax.ppermute(lax.dynamic_slice_in_dim(codebook, section_id * half, half,...  7.28 us
  transfers between devices with their start and end apart: 10, of which 9 were waited for; matrix products, arithmetic and copies ran while one was open for 5% of the time, Pallas kernels for 0%

profile of v10, /device:TPU:2, one launch (start us, length us, event | category | flops | bytes accessed | tf_op | source)
XLA Modules:
  0.0 222.1 jit_solution(15618392089859295301)
XLA Ops:
  6.5 1.0 constant_dynamic-slice_fusion
  7.6 7.3 %collective-permute-start.4 = (bf16[512,256]{1,0:T(8,128)(2,1)S(1)}, bf16[512,256]{1,0:T(8,128)(2,1)S(1)}, u32[]{:S(2)}, u32[]{:S(2)}) collective-permute-start(bf16[512,256]{1,0:T(8,128)(2,1)S(1)} %constant_dynamic-slice_fusion), channel_id=1, source_target_pairs={{0,64},{64,0},{1,65},{65,1},{2,66},{66,2},{3,67},{67,3},{4,68},{68... | collective-permute-start | bytes 786440 | tf_op jit(solution)/shard_map/ppermute | solution.py:424
  14.8 0.0 copy-start.2
  14.9 2.7 %fusion.63 = bf16[1024,256]{1,0:T(8,128)(2,1)} fusion(bf16[1024,256]{1,0:T(8,128)(2,1)} %bitcast.76, s32[1024]{0:T(1024)S(1)} %fusion.103), kind=kOutput, calls=%fused_computation.125 | convolution fusion | flops 538181632 | bytes 1052672 | tf_op jit(solution)/shard_map/dot_general | solution.py:488
  17.6 7.6 %all-to-all-start.4 = ((bf16[32,32,256]{2,1,0:T(8,128)(2,1)}), bf16[32,32,256]{2,1,0:T(8,128)(2,1)S(1)}, u32[]{:S(2)}, u32[]{:S(2)}) async-start(bf16[32,32,256]{2,1,0:T(8,128)(2,1)} %bitcast.23), calls=%async_computation.4 | async-start | bytes 1048576 | tf_op jit(solution)/shard_map/all_to_all | solution.py:36
  25.2 0.1 pad_add_fusion.1
  25.4 0.1 copy.39
  25.4 0.2 reshape.869
  25.6 0.2 fusion.72
  25.8 0.1 fusion.77
  26.0 0.3 fusion.68
  26.3 0.1 collective-permute-start.5
  26.4 1.0 select_reduce_fusion
  27.4 0.1 eq.187
  27.5 0.5 collective-permute-done.5
  28.0 0.1 pad_maximum_fusion
  28.0 14.1 %all-to-all-done.4 = bf16[32,32,256]{2,1,0:T(8,128)(2,1)S(1)} async-done(((bf16[32,32,256]{2,1,0:T(8,128)(2,1)}), bf16[32,32,256]{2,1,0:T(8,128)(2,1)S(1)}, u32[]{:S(2)}, u32[]{:S(2)}) %all-to-all-start.4) | async-done | bytes 524320 | tf_op jit(solution)/shard_map/all_to_all | solution.py:36
  42.1 3.7 %fusion.59 = bf16[1792,256]{1,0:T(8,128)(2,1)} fusion(bf16[2048,256]{1,0:T(8,128)(2,1)S(1)} %pad_maximum_fusion, s32[1792]{0:T(1024)S(1)} %eq.187), kind=kOutput, calls=%fused_computation.119 | convolution fusion | flops 1883176960 | bytes 1973248 | tf_op jit(solution)/shard_map/dot_general | solution.py:450
  45.8 4.9 %all-to-all-start.5 = ((bf16[16,112,256]{2,1,0:T(8,128)(2,1)}), bf16[16,112,256]{2,1,0:T(8,128)(2,1)S(1)}, u32[]{:S(2)}, u32[]{:S(2)}) async-start(bf16[16,112,256]{2,1,0:T(8,128)(2,1)} %bitcast.85), calls=%async_computation.5 | async-start | bytes 1835008 | tf_op jit(solution)/shard_map/all_to_all | solution.py:36
  50.8 0.3 fusion.69
  51.2 12.9 %all-to-all-done.5 = bf16[16,112,256]{2,1,0:T(8,128)(2,1)S(1)} async-done(((bf16[16,112,256]{2,1,0:T(8,128)(2,1)}), bf16[16,112,256]{2,1,0:T(8,128)(2,1)S(1)}, u32[]{:S(2)}, u32[]{:S(2)}) %all-to-all-start.5) | async-done | bytes 917536 | tf_op jit(solution)/shard_map/all_to_all | solution.py:36
  64.1 1.4 fusion.64
  65.4 0.1 collective-permute-start.6
  65.6 0.0 copy-start
  65.6 0.8 fusion.62
  66.5 1.0 collective-permute-done.6
  67.5 1.9 collective-permute-start.7
  69.5 4.1 %collective-permute-start.8 = (bf16[2,256,256]{2,1,0:T(8,128)(2,1)S(1)}, bf16[2,256,256]{2,1,0:T(8,128)(2,1)S(1)}, u32[]{:S(2)}, u32[]{:S(2)}) collective-permute-start(bf16[2,256,256]{2,1,0:T(8,128)(2,1)S(1)} %get-tuple-element.40), channel_id=1, source_target_pairs={{4,0},{8,4},{12,8},{16,12},{20,16},{24,20},{28,24},{32,28},{36,32}... | collective-permute-start | bytes 786440 | tf_op jit(solution)/shard_map/ppermute | solution.py:30
  73.6 3.2 %collective-permute-done.7.refs_0_ = bf16[2,256,256]{2,1,0:T(8,128)(2,1)S(1)} collective-permute-done((bf16[2,256,256]{2,1,0:T(8,128)(2,1)S(1)}, bf16[2,256,256]{2,1,0:T(8,128)(2,1)S(1)}, u32[]{:S(2)}, u32[]{:S(2)}) %collective-permute-start.7) | collective-permute-done | bytes 262176 | tf_op jit(solution)/shard_map/ppermute | solution.py:29
  76.8 1.9 collective-permute-done.8.refs_2_
  78.7 2.5 %shard_map.49 = (bf16[2,2,256,256]{3,2,1,0:T(8,128)(2,1)S(1)}, f32[2,512,256]{2,1,0:T(8,128)S(1)}) custom-call(s32[1]{0:T(128)} %bitcast.20.section_ref, bf16[2,2,256,256]{3,2,1,0:T(8,128)(2,1)S(1)} %shard_map.47.cells_ref.dec_ref, bf16[2,256,256]{2,1,0:T(8,128)(2,1)S(1)} %collective-permute-done.7.refs_0_, ...), custom_call_target="tpu_custom_call" | custom-call | flops 1811939328 | bytes 5505028 | tf_op jit(solution)/shard_map/pallas_call | solution.py:77
  81.2 1.3 collective-permute-start.9
  82.5 1.0 shard_map.48.turned_ref
  83.5 2.1 collective-permute-done.9.returned_ref
  85.6 4.6 %shard_map.50 = s16[16,19,16,256]{3,2,1,0:T(8,128)(2,1)} custom-call(s32[1]{0:T(128)} %bitcast.20.section_ref, bf16[3,256,2048]{2,1,0:T(8,128)(2,1)S(1)} %shard_map.48.turned_ref, f32[2,512,256]{2,1,0:T(8,128)S(1)} %get-tuple-element.29.pre_ref, bf16[2,2,256,256]{3,2,1,0:T(8,128)(2,1)S(1)} %shard_map.47.cells_ref.dec_ref, ...), custom_call_target="tpu_custom_call" | custom-call | flops 1811939328 | bytes 8781828 | tf_op jit(solution)/shard_map/pallas_call | solution.py:77
  90.2 16.2 %all-to-all-start.6 = ((s16[16,19,16,256]{3,2,1,0:T(8,128)(2,1)}), s16[16,19,16,256]{3,2,1,0:T(8,128)(2,1)S(1)}, u32[]{:S(2)}, u32[]{:S(2)}) async-start(s16[16,19,16,256]{3,2,1,0:T(8,128)(2,1)} %shard_map.50), calls=%async_computation.6 | async-start | bytes 4980736 | tf_op jit(solution)/shard_map/all_to_all | solution.py:36
  106.4 1.8 convert_reduce_fusion.1
  108.2 1.4 reduce_max.27
  110.2 29.6 %all-to-all-done.6.packed_ref = s16[16,19,16,256]{3,2,1,0:T(8,128)(2,1)S(1)} async-done(((s16[16,19,16,256]{3,2,1,0:T(8,128)(2,1)}), s16[16,19,16,256]{3,2,1,0:T(8,128)(2,1)S(1)}, u32[]{:S(2)}, u32[]{:S(2)}) %all-to-all-start.6) | async-done | bytes 2490400 | tf_op jit(solution)/shard_map/all_to_all | solution.py:36
  139.8 0.8 shard_map.51
  140.6 19.7 %all_to_all.51.parts_ref = s16[8,80,128]{2,1,0:T(8,128)(2,1)} all-to-all(s16[8,80,128]{2,1,0:T(8,128)(2,1)S(1)} %shard_map.51), channel_id=1, replica_groups=mesh['section'=2,'zh'=2,'y'=4,'x'=4,'dp'=4] {'zh','dp'}, dimensions={0} | all-to-all | bytes 327680 | tf_op jit(solution)/shard_map/all_to_all | solution.py:36
  160.3 1.8 shard_map.52
  162.1 3.4 %all-to-all-start.8 = ((s16[8,80,128]{2,1,0:T(8,128)(2,1)}), s16[8,80,128]{2,1,0:T(8,128)(2,1)S(1)}, u32[]{:S(2)}, u32[]{:S(2)}) async-start(s16[8,80,128]{2,1,0:T(8,128)(2,1)} %shard_map.52), calls=%async_computation.8 | async-start | bytes 327680 | tf_op jit(solution)/shard_map/all_to_all | solution.py:36
  165.5 1.4 slice_reduce_fusion
  167.4 7.4 %all-to-all-done.8 = s16[8,80,128]{2,1,0:T(8,128)(2,1)S(1)} async-done(((s16[8,80,128]{2,1,0:T(8,128)(2,1)}), s16[8,80,128]{2,1,0:T(8,128)(2,1)S(1)}, u32[]{:S(2)}, u32[]{:S(2)}) %all-to-all-start.8) | async-done | bytes 163872 | tf_op jit(solution)/shard_map/all_to_all | solution.py:36
  174.8 1.7 shard_map.53
  176.6 36.0 %all_to_all.52.plane_ref = s16[16,592,128]{2,1,0:T(8,128)(2,1)S(1)} all-to-all(s16[16,592,128]{2,1,0:T(8,128)(2,1)} %shard_map.53), channel_id=1, replica_groups=mesh['section'=2,'zh'=2,'y'=4,'x'=4,'dp'=4] {'y','x'}, dimensions={0} | all-to-all | bytes 4849664 | tf_op jit(solution)/shard_map/all_to_all | solution.py:36
  212.5 2.7 %shard_map.54 = f32[2,3,3,256,256]{4,3,2,1,0:T(8,128)} custom-call(s16[16,592,128]{2,1,0:T(8,128)(2,1)S(1)} %all_to_all.52.plane_ref), custom_call_target="tpu_custom_call" | custom-call | tf_op jit(solution)/shard_map/pallas_call | solution.py:404
  (21 shorter events, 0.2 us)
Async XLA Ops:
  6.5 18.7 %copy-start.5 = (s32[64,4,2,64]{3,2,1,0:T(2,128)S(1)}, s32[64,4,2,64]{3,2,1,0:T(2,128)}, u32[]{:S(2)}) copy-start(s32[64,4,2,64]{3,2,1,0:T(2,128)} %param.9) | copy-start | bytes 393220
  7.6 18.8 %collective-permute-start.4 = (bf16[512,256]{1,0:T(8,128)(2,1)S(1)}, bf16[512,256]{1,0:T(8,128)(2,1)S(1)}, u32[]{:S(2)}, u32[]{:S(2)}) collective-permute-start(bf16[512,256]{1,0:T(8,128)(2,1)S(1)} %constant_dynamic-slice_fusion), channel_id=1, source_target_pairs={{0,64},{64,0},{1,65},{65,1},{2,66},{66,2},{3,67},{67,3},{4,68},{68... | collective-permute-start | bytes 786440 | tf_op jit(solution)/shard_map/ppermute | solution.py:424
  14.8 13.1 %copy-start.2 = (bf16[1024,256]{1,0:T(8,128)(2,1)S(1)}, bf16[1024,256]{1,0:T(8,128)(2,1)}, u32[]{:S(2)}) copy-start(bf16[1024,256]{1,0:T(8,128)(2,1)} %param.8) | copy-start | bytes 1572868
  17.6 24.5 %all-to-all-start.4 = ((bf16[32,32,256]{2,1,0:T(8,128)(2,1)}), bf16[32,32,256]{2,1,0:T(8,128)(2,1)S(1)}, u32[]{:S(2)}, u32[]{:S(2)}) async-start(bf16[32,32,256]{2,1,0:T(8,128)(2,1)} %bitcast.23), calls=%async_computation.4 | async-start | bytes 1048576 | tf_op jit(solution)/shard_map/all_to_all | solution.py:36
  25.8 24.9 %copy-start.7 = (s32[33,1024]{1,0:T(8,128)}, s32[33,1024]{1,0:T(8,128)S(1)}, u32[]{:S(2)}) copy-start(s32[33,1024]{1,0:T(8,128)S(1)} %fusion.72) | copy-start | bytes 405508
  26.3 1.6 collective-permute-start.5
  45.8 18.2 %all-to-all-start.5 = ((bf16[16,112,256]{2,1,0:T(8,128)(2,1)}), bf16[16,112,256]{2,1,0:T(8,128)(2,1)S(1)}, u32[]{:S(2)}, u32[]{:S(2)}) async-start(bf16[16,112,256]{2,1,0:T(8,128)(2,1)} %bitcast.85), calls=%async_computation.5 | async-start | bytes 1835008 | tf_op jit(solution)/shard_map/all_to_all | solution.py:36
  64.1 1.5 copy-start.4
  65.4 2.0 collective-permute-start.6
  65.6 1.8 copy-start
  67.5 9.2 %collective-permute-start.7 = (bf16[2,256,256]{2,1,0:T(8,128)(2,1)S(1)}, bf16[2,256,256]{2,1,0:T(8,128)(2,1)S(1)}, u32[]{:S(2)}, u32[]{:S(2)}) collective-permute-start(bf16[2,256,256]{2,1,0:T(8,128)(2,1)S(1)} %get-tuple-element.41), channel_id=1, source_target_pairs={{0,4},{4,8},{8,12},{12,16},{16,20},{20,24},{24,28},{28,32},{32,36}... | collective-permute-start | bytes 786440 | tf_op jit(solution)/shard_map/ppermute | solution.py:29
  69.5 9.2 %collective-permute-start.8 = (bf16[2,256,256]{2,1,0:T(8,128)(2,1)S(1)}, bf16[2,256,256]{2,1,0:T(8,128)(2,1)S(1)}, u32[]{:S(2)}, u32[]{:S(2)}) collective-permute-start(bf16[2,256,256]{2,1,0:T(8,128)(2,1)S(1)} %get-tuple-element.40), channel_id=1, source_target_pairs={{4,0},{8,4},{12,8},{16,12},{20,16},{24,20},{28,24},{32,28},{36,32}... | collective-permute-start | bytes 786440 | tf_op jit(solution)/shard_map/ppermute | solution.py:30
  81.2 4.4 %collective-permute-start.9 = (bf16[2,2,256,256]{3,2,1,0:T(8,128)(2,1)S(1)}, bf16[2,2,256,256]{3,2,1,0:T(8,128)(2,1)S(1)}, u32[]{:S(2)}, u32[]{:S(2)}) collective-permute-start(bf16[2,2,256,256]{3,2,1,0:T(8,128)(2,1)S(1)} %get-tuple-element.30), channel_id=1, source_target_pairs={{128,0},{129,1},{130,2},{131,3},{132,4},{133,5},{134,6},{135,7},{1... | collective-permute-start | bytes 1572872 | tf_op jit(solution)/shard_map/ppermute | solution.py:543
  90.2 49.6 %all-to-all-start.6 = ((s16[16,19,16,256]{3,2,1,0:T(8,128)(2,1)}), s16[16,19,16,256]{3,2,1,0:T(8,128)(2,1)S(1)}, u32[]{:S(2)}, u32[]{:S(2)}) async-start(s16[16,19,16,256]{3,2,1,0:T(8,128)(2,1)} %shard_map.50), calls=%async_computation.6 | async-start | bytes 4980736 | tf_op jit(solution)/shard_map/all_to_all | solution.py:36
  162.1 12.7 %all-to-all-start.8 = ((s16[8,80,128]{2,1,0:T(8,128)(2,1)}), s16[8,80,128]{2,1,0:T(8,128)(2,1)S(1)}, u32[]{:S(2)}, u32[]{:S(2)}) async-start(s16[8,80,128]{2,1,0:T(8,128)(2,1)} %shard_map.52), calls=%async_computation.8 | async-start | bytes 327680 | tf_op jit(solution)/shard_map/all_to_all | solution.py:36
